TPU v7x, 256 devices: a whole 4x4x8 slice. The times are simulated.
256 devices in a mesh: seq: 32 (over y, z), head: 8 (over x, core).
Axes of the slice: x: 4, y: 4, z: 8, core: 2. Of those that a mesh axis runs over, the one named last changes fastest.
Arguments:
- queries: bfloat16 [4096, 4096], P('seq', 'head'), may hold values from -6 to 6
- keys: bfloat16 [4096, 4096], P('seq', 'head'), may hold values from -6 to 6
- values: bfloat16 [4096, 4096], P('seq', 'head'), may hold values from -6 to 6
- log_decay: float32 [32, 4096], P('head', 'seq'), may hold values from -1 to 0, as said below
- beta: float32 [32, 4096], P('head', 'seq'), may hold values from 0.001 to 0.6
- level_weights: float32 [10, 32, 4096], P(None, 'head', 'seq'), may hold values from 0.25 to 2
- document_ends: int32 [64], P('seq'), may hold values 0 or 1
- out_weight: bfloat16 [4096, 4096], P('head', 'seq'), may hold values from -0.09375 to 0.09375
- grad_y: bfloat16 [4096, 4096], P('seq', 'head'), may hold values from -6 to 6
- final_state_grad: float32 [32, 128, 128], P('head'), may hold values from -6 to 6
Outputs:
- layer_out: bfloat16 [4096, 4096], P('seq', 'head')
- grad_queries: bfloat16 [4096, 4096], P('seq', 'head')
- grad_values: bfloat16 [4096, 4096], P('seq', 'head')
Inputs may be any that keep to these rules, and one draw needn't show every extreme that they name: `log_decay`: strictly negative.
All inputs are finite; a program needn't handle non-finite values. No bound on the sum of `document_ends` on one device may be relied on, other than what follows from the above.
Results may differ from a plain program's by a relative error of at most 0.023.
Values may be sent and summed in bfloat16 or wider, within the bound.
No kernel may reach another device: no remote copies, remote signals or barrier semaphores. Data moves between devices by JAX's collectives and lax.ppermute only.
A program may use at most 64 MiB of HBM per device.

v0:
```python
import jax
import jax.numpy as jnp
from jax import lax
from jax.experimental import pallas as pl
from jax.experimental.pallas import tpu as pltpu
from jax.sharding import PartitionSpec as P

F32 = jnp.float32
BF = jnp.bfloat16
NN = (((1,), (0,)), ((), ()))
NT = (((1,), (1,)), ((), ()))
TIERS = 7
SCAL = 32
SOME_VMEM = 16 * 1024 * 1024
MOST_VMEM = 63_000_000


SIZES = (("a", 1024), ("a2", 512), ("a4", 256), ("s", 1536), ("m", 1024), ("w", 512), ("u", 512), ("inv", 512),
         ("p", 512), ("e", 512), ("qe", 512), ("kt", 512), ("qn", 512), ("ks", 512))
STARTS = {}
KEPT = 0
for name, rows in SIZES:
    STARTS[name] = KEPT
    KEPT += rows
READS = [(c, n) for c in range(8) for n in (1, 2, 3) if c >> (n - 1) & 1]


def at(name, index, rows=128):
    start = STARTS[name] + index * rows
    return slice(start, start + rows)


def mm(a, b, dims=NN):
    return lax.dot_general(a, b, dims, preferred_element_type=F32)


def split(x):
    hi = x.astype(BF)
    return hi, (x - hi.astype(F32)).astype(BF)


def dot1(a, b, dims=NN):
    return mm(a.astype(BF), b.astype(BF), dims)


def dot3(a, b, dims=NN):
    ah, al = split(a)
    bh, bl = split(b)
    return mm(ah, bh, dims) + (mm(ah, bl, dims) + mm(al, bh, dims))


def dot2(a, b, dims=NN):
    ah, al = split(a)
    return mm(ah, b, dims) + mm(al, b, dims)


def tn(a, b, dot):
    return dot(a.T, b)


def iotas(rows, cols):
    return (
        lax.broadcasted_iota(jnp.int32, (rows, cols), 0),
        lax.broadcasted_iota(jnp.int32, (rows, cols), 1),
    )


def call(us, body, out_shapes, ins, scratch=(), fetch=False):
    count, outs = len(ins), len(out_shapes)
    big = [n for n, a in enumerate(ins) if a.dtype != jnp.int32]

    def fetching(*refs):
        held = refs[count + outs : count + outs + len(big)]
        sems = refs[count + outs + len(big)]
        own = list(refs[:count])
        copies = []
        for n, index in enumerate(big):
            copies.append(pltpu.make_async_copy(refs[index], held[n], sems.at[n]))
            own[index] = held[n]
        for copy in copies:
            copy.start()
        for copy in copies:
            copy.wait()
        body(*own, *refs[count : count + outs], *refs[count + outs + len(big) + 1 :])

    space = pltpu.HBM if fetch else pltpu.VMEM
    extra = [pltpu.VMEM(ins[n].shape, ins[n].dtype) for n in big] + [pltpu.SemaphoreType.DMA((len(big),))]
    return pl.pallas_call(
        fetching if fetch else body,
        out_shape=[jax.ShapeDtypeStruct(s, d) for s, d in out_shapes],
        in_specs=[pl.BlockSpec(memory_space=pltpu.SMEM if a.dtype == jnp.int32 else space) for a in ins],
        out_specs=[pl.BlockSpec(memory_space=pltpu.VMEM)] * outs,
        scratch_shapes=(extra if fetch else []) + list(scratch),
        cost_estimate=pl.CostEstimate(flops=int(us * 1.15e9), bytes_accessed=0, transcendentals=0),
        compiler_params=pltpu.CompilerParams(vmem_limit_bytes=MOST_VMEM if fetch else SOME_VMEM),
    )(*ins)


def pack_body(wh, ends, q, k, v, gy, gate, rate, tiers, *rest):
    outs, scal = rest[:-1], rest[-1]
    own, core = wh[4], wh[5]
    lane = lax.broadcasted_iota(jnp.int32, (1, 128), 1)
    keep = jnp.where(
        lane < 64, 1.0 - ends[0].astype(F32), 1.0 - ends[1].astype(F32)
    )

    def put(row, value, parts):
        for part in range(parts):
            piece = value.astype(BF).astype(F32)
            scal[row + part : row + part + 1, :] = piece
            value = value - piece

    for m in range(4):
        j = own ^ m
        cols = pl.ds(pl.multiple_of(j * 128, 128), 128)
        gcols = pl.ds(pl.multiple_of((j ^ (2 * core)) * 128, 128), 128)
        scal[...] = jnp.zeros((SCAL, 128), F32)
        put(0, gate[pl.ds(j, 1), :], 3)
        put(3, rate[pl.ds(j, 1), :], 2)
        for tier in range(TIERS):
            put(5 + 2 * tier, tiers[tier, pl.ds(j, 1), :], 2)
        scal[19:20, :] = keep
        outs[m][0:128, :] = k[:, cols]
        outs[m][128:256, :] = v[:, cols]
        outs[m][256:288, :] = scal[...].astype(BF)
        outs[m][288:416, :] = q[:, cols]
        outs[m][416:544, :] = gy[:, gcols]


def collect_body(p0, p1, p2, p3, out):
    for m, p in enumerate((p0, p1, p2, p3)):
        out[128 * m : 128 * m + 128, :] = p[416:544, :]


def join_body(p0, p1, p2, p3, out):
    for m, p in enumerate((p0, p1, p2, p3)):
        out[512 * m : 512 * m + 512, :] = p[...]


def block_body(wh, a0, a1, a2, a3, w0, ab_out, abf_out, far_out, kept, pack):
    del w0
    zlo = wh[0]
    for m, a in enumerate((a0, a1, a2, a3)):
        pack[pl.ds(zlo ^ m, 1)] = a[0:416, :][None]
    row, col = iotas(128, 128)
    same = (row >> 6) == (col >> 6)
    causal = same & (row >= col)
    strict = same & (row > col)
    eye = row == col
    eyef = eye.astype(F32)
    lblk = causal.astype(BF)
    top = row < 64
    trans, writes, local, qeff = [], [], [], []
    for i in range(4):
        k = pack[i, 0:128, :]
        v = pack[i, 128:256, :]
        scal = pack[i, 256:288, :]
        q = pack[i, 288:416, :]
        scalf = scal.astype(F32)
        cum3 = mm(lblk, scal, NT)
        cols = mm(eyef.astype(BF), scal, NT)
        cum_col = cum3[:, 0:1] + cum3[:, 1:2] + cum3[:, 2:3]
        cumr = mm(scal, lblk, NT)
        cum_row = cumr[0:1] + cumr[1:2] + cumr[2:3]
        beta_col = cols[:, 3:4] + cols[:, 4:5]
        beta_row = scalf[3:4] + scalf[4:5]
        kf, qf = k.astype(F32), q.astype(F32)
        rk_col = lax.rsqrt(jnp.sum(kf * kf, 1, keepdims=True) + 1e-6)
        rq_col = lax.rsqrt(jnp.sum(qf * qf, 1, keepdims=True) + 1e-6)
        rk_row = jnp.sum(jnp.where(eye, rk_col, 0.0), 0, keepdims=True)
        decay = jnp.where(causal, jnp.exp(jnp.where(causal, cum_col - cum_row, 0.0)), 0.0)
        kept[at("e", i), :] = decay
        gram = mm(k, k, NT)
        lower = jnp.where(strict, (beta_col * rk_col) * decay * (gram * rk_row), 0.0)
        inv = eyef - jnp.where((row >> 1) == (col >> 1), lower, 0.0)
        for bit in range(1, 6):
            near = ((row >> (bit + 1)) == (col >> (bit + 1))) & ((row >> bit) != (col >> bit))
            inv = inv - dot3(dot3(inv, jnp.where(near, lower, 0.0)), inv)
        kept[at("inv", i), :] = inv
        exp_col = jnp.exp(cum_col)
        w = dot2(inv * (beta_row * jnp.exp(cum_row) * rk_row), k)
        u = dot2(inv * beta_row, v)
        wu = jnp.concatenate([w, u], 1)
        kept[at("w", i), :] = w
        kept[at("u", i), :] = u
        last0, last1 = cum_row[:, 63:64], cum_row[:, 127:128]
        tail = jnp.exp(jnp.where(top[:, 0:1], last0, last1) - cum_col) * rk_col
        kept[at("kt", i), :] = tail * kf
        rhs = wu * tail
        top2 = lax.broadcasted_iota(jnp.int32, (128, 256), 0) < 64
        rhs = jnp.concatenate([jnp.where(top2, rhs, 0.0), jnp.where(top2, 0.0, rhs)], 1)
        rh, rl = split(rhs)
        kt = kf.T.astype(BF)
        ab = mm(kt, rh) + mm(kt, rl)
        for b, last in ((0, last0), (1, last1)):
            keep = scalf[19:20, 64 * b : 64 * b + 1]
            trans.append(keep * (jnp.exp(last) * eyef - ab[:, 256 * b : 256 * b + 128]))
            writes.append(keep * ab[:, 256 * b + 128 : 256 * b + 256])
        scores = decay * (mm(q, k, NT) * (rq_col * rk_row))
        kept[at("p", i), :] = scores
        pw = dot3(scores, wu)
        qn = rq_col * qf
        qe = exp_col * qn - pw[:, 0:128]
        kept[at("qe", i), :] = qe
        kept[at("qn", i), :] = qn
        kept[at("ks", i), :] = rk_col * kf
        weights = [cols[:, 5 + 2 * n : 6 + 2 * n] + cols[:, 6 + 2 * n : 7 + 2 * n] for n in range(TIERS)]
        far_out[i * 128 : (i + 1) * 128, :] = jnp.concatenate(
            weights + [cols[:, 19:20], rq_col, exp_col, beta_col, jnp.zeros((128, 128 - TIERS - 4), F32)], 1
        )
        local.append(pw[:, 128:256])
        qeff.append(qe)

    def both(a, x, y):
        r = dot3(a, jnp.concatenate([x, y], 1))
        return r[:, 0:128], r[:, 128:256]

    for c in range(8):
        kept[at("a", c), :] = trans[c]
    t2, w2 = [], []
    for p in range(4):
        t, s = both(trans[2 * p + 1], trans[2 * p], writes[2 * p])
        t2.append(t)
        w2.append(s + writes[2 * p + 1])
        kept[at("a2", p), :] = t
    t4, w4, map3, read3 = [], [], [], []
    for h in range(2):
        t, s = both(t2[2 * h + 1], t2[2 * h], w2[2 * h])
        t4.append(t)
        w4.append(s + w2[2 * h + 1])
        kept[at("a4", h), :] = t
        t, s = both(trans[4 * h + 2], t2[2 * h], w2[2 * h])
        map3.append(t)
        read3.append(s)
    tg, sg = both(t4[1], t4[0], w4[0])
    sg = sg + w4[1]
    ab_out[0:128, :] = tg.astype(BF)
    ab_out[128:256, :] = sg.astype(BF)
    abf_out[0:128, :] = tg
    abf_out[128:256, :] = sg
    maps = [eyef, trans[0], t2[0], map3[0], t4[0]]
    upper = [w4[0]]
    for inner in (trans[4], t2[2], map3[1]):
        t, s = both(inner, t4[0], w4[0])
        maps.append(t)
        upper.append(s)
    for c in range(8):
        kept[at("m", c), :] = maps[c]
        parts = []
        if c & 1:
            parts.append((1, writes[c - 1]))
        if c & 2:
            parts.append((2, w2[2 * (c >> 2)] if not c & 1 else read3[c >> 2]))
        if c & 4:
            parts.append((3, upper[c - 4]))
        rows = slice(64 * (c & 1), 64 * (c & 1) + 64)
        for level, state in parts:
            kept[at("s", READS.index((c, level))), :] = state
        rhs = jnp.concatenate([state for _, state in parts] + [maps[c]], 1)
        read = dot3(qeff[c >> 1][rows], rhs)
        weights = far_out[64 * c : 64 * c + 64, :]
        out = weights[:, 0:1] * local[c >> 1][rows]
        for n, (level, _) in enumerate(parts):
            out = out + weights[:, level : level + 1] * read[:, 128 * n : 128 * n + 128]
        far_out[1024 + 64 * c : 1024 + 64 * c + 64, :] = out
        far_out[512 + 64 * c : 512 + 64 * c + 64, :] = read[:, 128 * len(parts) :]


def pair_body(wh, own, other, bf_out, f_out, omap_out):
    up = wh[1] == 1
    o = other[...].astype(F32)
    mine = own[...]
    low = jnp.where(up, o, mine)
    high = jnp.where(up, mine, o)
    both = dot3(high[0:128], jnp.concatenate([low[0:128], low[128:256]], 1))
    t = both[:, 0:128]
    s = both[:, 128:256] + high[128:256]
    f_out[0:128, :] = t
    f_out[128:256, :] = s
    bf_out[0:128, :] = t.astype(BF)
    bf_out[128:256, :] = s.astype(BF)
    row, col = iotas(128, 128)
    omap_out[0:128, :] = jnp.where(up, low[0:128], (row == col).astype(F32))
    omap_out[128:256, :] = jnp.where(up, low[128:256], 0.0)


def far_body(wh, own, r1, r2, r3, omap, held, final, attn_out, s_out, up_out, fin_out, order):
    y = wh[2]
    for n, r in enumerate((own, r1, r2, r3)):
        order[pl.ds(y ^ n, 1)] = r[...].astype(F32)[None]
    up_out[...] = order[:, 0:128, :]
    o = omap[0:128, :]
    b5 = order[pl.ds(y ^ 1, 1)][0][128:256]
    b01 = dot3(order[1, 0:128, :], order[0, 128:256, :]) + order[1, 128:256, :]
    b6 = jnp.where(y == 3, dot3(order[2, 0:128, :], b01), b01)
    both = dot3(o, jnp.concatenate([jnp.where((y & 1) == 1, b5, 0.0), jnp.where(y >= 2, b6, 0.0)], 1))
    states = jnp.concatenate([omap[128:256, :], both], 1)
    s_out[...] = states
    read = dot3(held[512:1024, :], states)
    out = held[1024:1536, :]
    for n in range(3):
        out = out + held[0:512, 4 + n : 5 + n] * read[:, 128 * n : 128 * n + 128]
    attn_out[...] = out.astype(BF)
    f = final[pl.ds(wh[4], 1)][0]
    for j in (3, 2, 1):
        f = jnp.where(y < j, tn(order[j, 0:128, :], f, dot3), f)
    fin_out[...] = f


def pair_join_body(p0, p1, out):
    out[0:512, :] = p0[...]
    out[512:1024, :] = p1[...]


def order_weight(wh, parts, held):
    for n, part in enumerate(parts):
        for t in range(2):
            hb = 2 * (wh[2] ^ n) + (wh[1] ^ t)
            held[pl.ds(hb, 1)] = part[512 * t : 512 * t + 512, :][None]


def back_product_body(wh, ga, gb, w0, w1, w2, w3, own_out, o1, o2, o3, held):
    order_weight(wh, (w0, w1, w2, w3), held)
    total = None
    for n in range(4):
        for core, g in enumerate((ga, gb)):
            hb = wh[3] ^ (2 * n + core)
            w = held[pl.ds(hb, 1)][0]
            part = mm(g[512 * n : 512 * n + 512, :], w, NT)
            total = part if total is None else total + part
    acc = total
    for j in range(4):
        piece = acc[:, 128 * j : 128 * j + 128]

        for m, out in enumerate((own_out, o1, o2, o3)):

            @pl.when((wh[4] ^ m) == j)
            def _(piece=piece, out=out):
                out[...] = piece.astype(out.dtype)


def reach_body(wh, own, r1, r2, r3, held, omap, do_out, z5_out, z6_out, x4_out):
    for m in range(4):
        total = own[128 * m : 128 * m + 128, :]
        for k, r in ((1, r1), (2, r2), (3, r3)):
            total = total + r[128 * (m ^ k) : 128 * (m ^ k) + 128, :].astype(F32)
        do_out[pl.ds(wh[0] ^ m, 1)] = total.astype(BF)[None]
    do = do_out[...].reshape(512, 128).astype(F32)
    weighted = []
    for n in range(3):
        weighted.append(held[0:512, 4 + n : 5 + n] * do)
    x = tn(held[512:1024, :], jnp.concatenate(weighted, 1), dot3)
    x4_out[...] = jnp.where(wh[1] == 1, x[:, 0:128], 0.0)
    z = tn(omap[0:128, :], x[:, 128:384], dot3)
    z5_out[...] = z[:, 0:128].astype(BF)
    z6_out[...] = z[:, 128:256].astype(BF)


def grad_body(wh, do, held, far, kept, dq_out, dv_out, gmap_out):
    def weight(c, level):
        return held[64 * c : 64 * c + 64, level : level + 1]

    dof = do[...].reshape(512, 128).astype(F32)
    wd = [held[0:512, 4 + n : 5 + n] * dof for n in range(3)]
    carried = dot3(jnp.concatenate(wd, 1), far[...], NT)
    reach = {}
    dqe = []
    for c in range(8):
        rows = slice(64 * (c & 1), 64 * (c & 1) + 64)
        doc = do[c >> 1, rows, :].astype(F32)
        levels = [n for n in (1, 2, 3) if c >> (n - 1) & 1]
        left = jnp.concatenate([weight(c, n) * doc for n in levels] + [carried[64 * c : 64 * c + 64]], 1)
        right = jnp.concatenate(
            [kept[at("s", READS.index((c, n))), :] for n in levels] + [kept[at("m", c), :]], 1
        )
        dqe.append(dot3(left, right, NT))
        if levels:
            r = tn(kept[at("qe", c, 64), :], left[:, 0 : 128 * len(levels)], dot3)
            for n, level in enumerate(levels):
                reach[c, level] = r[:, 128 * n : 128 * n + 128]
    for i in range(4):
        doc = do[i].astype(F32)
        rows = slice(128 * i, 128 * i + 128)
        dqei = jnp.concatenate([dqe[2 * i], dqe[2 * i + 1]], 0)
        wu = jnp.concatenate([kept[at("w", i), :], kept[at("u", i), :]], 1)
        dp = dot3(jnp.concatenate([-dqei, held[rows, 0:1] * doc], 1), wu, NT) * kept[at("e", i), :]
        dqn = held[rows, 9:10] * dqei + dot3(dp, kept[at("ks", i), :])
        q = kept[at("qn", i), :]
        dq_out[i] = (held[rows, 8:9] * (dqn - q * jnp.sum(q * dqn, 1, keepdims=True))).astype(BF)
    row, col = iotas(128, 128)
    eyef = (row == col).astype(F32)

    def tnn(name, index, y):
        return tn(kept[at(name, index), :], y, dot3)

    d4 = reach[4, 3] + tnn("a", 4, reach[5, 3]) + tnn("a2", 2, reach[6, 3] + tnn("a", 6, reach[7, 3]))
    pair = {
        3: None,
        2: reach[6, 2] + tnn("a", 6, reach[7, 2]),
        1: d4,
        0: reach[2, 2] + tnn("a", 2, reach[3, 2]) + tnn("a2", 1, d4),
    }
    a4 = kept[at("a4", 1), :]
    suf = {3: eyef, 2: kept[at("a2", 3), :], 1: a4, 0: dot3(a4, kept[at("a2", 1), :])}
    for i in range(4):
        odd = pair[i]
        even = reach[2 * i + 1, 1] if odd is None else reach[2 * i + 1, 1] + tnn("a", 2 * i + 1, odd)
        odd = jnp.zeros((128, 128), F32) if odd is None else odd
        s_odd = suf[i]
        s_even = dot3(s_odd, kept[at("a", 2 * i + 1), :])
        rows = slice(128 * i, 128 * i + 128)
        doc = do[i].astype(F32)
        pd = tn(kept[at("p", i), :], held[rows, 0:1] * doc, dot3)
        kk = held[rows, 7:8] * kept[at("kt", i), :]
        left = dot3(kk[0:64], jnp.concatenate([even, s_even.T], 1))
        right = dot3(kk[64:128], jnp.concatenate([odd, s_odd.T], 1))
        hn = jnp.concatenate([left, right], 0)
        both = jnp.concatenate([pd + hn[:, 0:128], hn[:, 128:256]], 1)
        both = held[rows, 10:11] * tn(kept[at("inv", i), :], both, dot3)
        dv_out[rows, :] = both[:, 0:128]
        gmap_out[rows, :] = both[:, 128:256]


def near_body(wh, r1, r2, r3, ups, own, fin, x4, send_out, keep_out):
    y = wh[2]
    up = wh[1] == 1
    a = r2[...].astype(F32)
    b = r3[...].astype(F32)
    second = jnp.where(y == 0, a, b)
    third = jnp.where(y == 0, b, a)
    d01 = second + tn(ups[2], third, dot3)
    d01 = jnp.where(y == 0, tn(ups[1], d01, dot3), jnp.where(y == 1, d01, 0.0))
    part = d01 + jnp.where((y & 1) == 0, r1[...].astype(F32), 0.0)
    trans = own[0:128, :]
    full = part + fin[...]
    pulled = tn(trans, part, dot3) + x4[...]
    send_out[...] = jnp.where(up, pulled, part).astype(BF)
    keep_out[...] = full


def value_body(wh, r, kept, other, dv, gmap, dq, o0, o1, o2, o3, dvs):
    up = wh[1] == 1
    got = r[...].astype(F32)
    pulled = tn(other[0:128, :].astype(F32), kept[...], dot3)
    g = got + jnp.where(up, kept[...], pulled)
    res = dv[...] + dot3(gmap[...], g)
    dvs[...] = res.astype(BF).reshape(4, 128, 128)
    for m, out in enumerate((o0, o1, o2, o3)):
        out[0:128, :] = dq[pl.ds(wh[0] ^ m, 1)][0]
        out[128:256, :] = dvs[pl.ds(wh[0] ^ m, 1)][0]


def project_body(wh, a0, a1, a2, a3, w0, w1, w2, w3, even, odd, held):
    order_weight(wh, (w0, w1, w2, w3), held)
    for n in range(8):
        total = None
        for m, a in enumerate((a0, a1, a2, a3)):
            rows = pl.ds(pl.multiple_of((wh[4] ^ m) * 128, 128), 128)
            w = held[pl.ds(wh[3] ^ n, 1), rows, :][0]
            part = mm(a[...], w)
            total = part if total is None else total + part
        out = odd if n & 1 else even
        out[512 * (n >> 1) : 512 * (n >> 1) + 512, :] = total.astype(BF)


def sum_pair_body(own, r, f_out, o2, o4, o6):
    f_out[...] = own[0:512, :].astype(F32) + r[0:512, :].astype(F32)
    for n, out in ((1, o2), (2, o4), (3, o6)):
        rows = slice(512 * n, 512 * n + 512)
        out[...] = (own[rows, :].astype(F32) + r[rows, :].astype(F32)).astype(BF)


def sum_last_body(wh, f, r2, r4, r6, o0, o1, o2, o3, done):
    total = f[...] + r2[...].astype(F32) + r4[...].astype(F32) + r6[...].astype(F32)
    done[...] = total.astype(BF).reshape(4, 128, 128)
    for m, out in enumerate((o0, o1, o2, o3)):
        out[...] = done[pl.ds(wh[0] ^ m, 1)][0]


def place_heads_body(wh, r0, r1, r2, r3, dq, dv):
    for m, r in enumerate((r0, r1, r2, r3)):
        cols = pl.ds(pl.multiple_of((wh[4] ^ m) * 128, 128), 128)
        dq[:, cols] = r[0:128, :]
        dv[:, cols] = r[128:256, :]


def place_columns_body(wh, r0, r1, r2, r3, out):
    for m, r in enumerate((r0, r1, r2, r3)):
        j = wh[4] ^ m ^ (2 * wh[5])
        out[:, pl.ds(pl.multiple_of(j * 128, 128), 128)] = r[...]


def xor(value, axis, mask):
    return lax.ppermute(value, axis, [(s, s ^ mask) for s in range(lax.axis_size(axis))])


def own_head(z):
    return (z & 3) ^ (2 * (z >> 2))


def shards(queries, keys, values, log_decay, beta, level_weights, document_ends, out_weight, grad_y, final_state_grad):
    s = lax.axis_index("seq")
    h = lax.axis_index("head")
    z = s & 7
    where = jnp.stack([z & 3, z >> 2, s >> 3, h, own_head(z), h & 1, 0 * h, 0 * h]).astype(jnp.int32)
    wz = xor(out_weight, "seq", 6)
    w0 = call(1, pair_join_body, [((1024, 128), BF)], [out_weight, wz])[0]
    weight = [w0] + [xor(w0, "seq", 8 * n) for n in (1, 2, 3)]

    packs = call(
        3, pack_body,
        [((544, 128), BF)] * 4,
        [where, document_ends, queries, keys, values, grad_y, log_decay, beta, level_weights],
        [pltpu.VMEM((SCAL, 128), F32)],
        fetch=True,
    )
    mine = [packs[0]] + [xor(packs[m], "seq", m) for m in (1, 2, 3)]
    gm = call(1, collect_body, [((512, 128), BF)], mine)[0]
    ga = [gm] + [xor(gm, "head", 2 * n) for n in (1, 2, 3)]

    T = (512, 128)
    S = (128, 128)
    ab, abf, held, kept = call(
        11, block_body,
        [((256, 128), BF), ((256, 128), F32), ((1536, 128), F32), ((KEPT, 128), F32)],
        [where] + mine + [w0],
        [pltpu.VMEM((4, 416, 128), BF)],
    )
    other = xor(ab, "seq", 6)
    gj = call(1, join_body, [((2048, 128), BF)], ga)[0]
    gb = xor(gj, "head", 1)
    pair_bf, pair_f, omap = call(
        1, pair_body, [((256, 128), BF), ((256, 128), F32), ((256, 128), F32)], [where, abf, other]
    )
    far = [xor(pair_bf, "seq", 8 * n) for n in (1, 2, 3)]
    attn, far_states, ups, fin = call(
        2, far_body,
        [(T, BF), ((128, 384), F32), ((4,) + S, F32), (S, F32)],
        [where, pair_f] + far + [omap, held, final_state_grad],
        [pltpu.VMEM((4, 256, 128), F32)],
    )

    back = call(3, back_product_body, [(T, F32), (T, BF), (T, BF), (T, BF)], [where, gj, gb] + weight, [pltpu.VMEM((8, 512, 128), BF)])
    rb = [xor(back[m], "seq", m) for m in (1, 2, 3)]
    do, z5, z6, x4 = call(
        2, reach_body, [((4,) + S, BF), (S, BF), (S, BF), (S, F32)], [where, back[0]] + rb + [held, omap]
    )
    near = [xor(z5, "seq", 8), xor(z6, "seq", 16), xor(z6, "seq", 24)]
    dq, dv_part, gmap = call(
        7, grad_body, [((4,) + S, BF), (T, F32), (T, F32)], [where, do, held, far_states, kept]
    )
    send, local = call(1, near_body, [(S, BF), (S, F32)], [where] + near + [ups, abf, fin, x4])
    got = xor(send, "seq", 6)
    dqv = call(
        1, value_body, [((256, 128), BF)] * 4, [where, got, local, other, dv_part, gmap, dq], [pltpu.VMEM((4,) + S, BF)]
    )

    at = [attn] + [xor(attn, "seq", m) for m in (1, 2, 3)]
    even, odd = call(3, project_body, [((2048, 128), BF)] * 2, [where] + at + weight, [pltpu.VMEM((8, 512, 128), BF)])
    swapped = xor(odd, "head", 1)
    sums = call(1, sum_pair_body, [(T, F32), (T, BF), (T, BF), (T, BF)], [even, swapped])
    rx = [xor(sums[n], "head", 2 * n) for n in (1, 2, 3)]
    lo = call(1, sum_last_body, [(S, BF)] * 4, [where, sums[0]] + rx, [pltpu.VMEM((4,) + S, BF)])

    def home(parts):
        return [parts[0]] + [xor(parts[m], "seq", m) for m in (1, 2, 3)]

    whole = (128, 512)
    layer = call(1, place_columns_body, [(whole, BF)], [where] + home(lo))[0]
    grad_q, grad_v = call(1, place_heads_body, [(whole, BF)] * 2, [where] + home(dqv))
    return (layer, grad_q, grad_v)


def solution(mesh):
    in_specs = (
        P("seq", "head"),
        P("seq", "head"),
        P("seq", "head"),
        P("head", "seq"),
        P("head", "seq"),
        P(None, "head", "seq"),
        P("seq"),
        P("head", "seq"),
        P("seq", "head"),
        P("head", None, None),
    )
    out_specs = (P("seq", "head"), P("seq", "head"), P("seq", "head"))
    return jax.shard_map(shards, mesh=mesh, in_specs=in_specs, out_specs=out_specs, check_vma=False)
```

profile of v0, /device:TPU:32, one launch (start us, length us, event | category | flops | bytes accessed | tf_op | source)
XLA Modules:
  0.0 128.1 jit_solution(5508246263360043509)
XLA Ops:
  0.6 5.5 %collective-permute-start.3 = (bf16[512,128]{1,0:T(8,128)(2,1)}, bf16[512,128]{1,0:T(8,128)(2,1)S(1)}, u32[]{:S(2)}, u32[]{:S(2)}) collective-permute-start(bf16[512,128]{1,0:T(8,128)(2,1)} %p0.1), channel_id=1, source_target_pairs={{0,48},{8,56},{16,32},{24,40},{32,16},{40,24},{48,0},{56,8},{64,11... | collective-permute-start | bytes 393224 | tf_op jit(solution)/shard_map/ppermute | solution.py:494
  6.7 2.9 %shard_map.121 = (bf16[544,128]{1,0:T(8,128)(2,1)}, bf16[544,128]{1,0:T(8,128)(2,1)}, bf16[544,128]{1,0:T(8,128)(2,1)}, bf16[544,128]{1,0:T(8,128)(2,1)}) custom-call(s32[8]{0:T(128)} %stack.27.refs_0_.wh, s32[2]{0:T(128)} %refs_1_.1, bf16[128,512]{1,0:T(8,128)(2,1)} %refs_2_.1, bf16[128,512]{1,0:T(8,128)(2,1)} %refs_3_.1, bf16[128,512]{1,0:T(8,128)(2,1)} %refs_4_.1, ...), custom_call_target="tpu_custom_call" | custom-call | flops 3449999872 | tf_op jit(solution)/shard_map/pallas_call | solution.py:88
  9.6 1.1 collective-permute-start
  10.7 1.5 %collective-permute-start.1 = (bf16[544,128]{1,0:T(8,128)(2,1)}, bf16[544,128]{1,0:T(8,128)(2,1)S(1)}, u32[]{:S(2)}, u32[]{:S(2)}) collective-permute-start(bf16[544,128]{1,0:T(8,128)(2,1)} %get-tuple-element.49), channel_id=1, source_target_pairs={{0,16},{8,24},{16,0},{24,8},{32,48},{40,56},{48,32},{56,40},{64,80... | collective-permute-start | bytes 417800 | tf_op jit(solution)/shard_map/ppermute | solution.py:494
  12.2 1.0 collective-permute-start.2
  13.2 3.3 %collective-permute-done.a1.p1 = bf16[544,128]{1,0:T(8,128)(2,1)S(1)} collective-permute-done((bf16[544,128]{1,0:T(8,128)(2,1)}, bf16[544,128]{1,0:T(8,128)(2,1)S(1)}, u32[]{:S(2)}, u32[]{:S(2)}) %collective-permute-start) | collective-permute-done | bytes 139296 | tf_op jit(solution)/shard_map/ppermute | solution.py:494
  16.5 5.8 %collective-permute-done.1.a2.p2 = bf16[544,128]{1,0:T(8,128)(2,1)S(1)} collective-permute-done((bf16[544,128]{1,0:T(8,128)(2,1)}, bf16[544,128]{1,0:T(8,128)(2,1)S(1)}, u32[]{:S(2)}, u32[]{:S(2)}) %collective-permute-start.1) | collective-permute-done | bytes 139296 | tf_op jit(solution)/shard_map/ppermute | solution.py:494
  22.4 2.9 %collective-permute-done.2.a3.p3 = bf16[544,128]{1,0:T(8,128)(2,1)S(1)} collective-permute-done((bf16[544,128]{1,0:T(8,128)(2,1)}, bf16[544,128]{1,0:T(8,128)(2,1)S(1)}, u32[]{:S(2)}, u32[]{:S(2)}) %collective-permute-start.2) | collective-permute-done | bytes 139296 | tf_op jit(solution)/shard_map/ppermute | solution.py:494
  25.2 0.9 copy-done.3
  26.1 10.9 %shard_map.123 = (bf16[256,128]{1,0:T(8,128)(2,1)S(1)}, f32[256,128]{1,0:T(8,128)S(1)}, f32[1536,128]{1,0:T(8,128)S(1)}, f32[8960,128]{1,0:T(8,128)S(1)}) custom-call(s32[8]{0:T(128)S(1)} %copy-done, bf16[544,128]{1,0:T(8,128)(2,1)S(1)} %copy-done.3, bf16[544,128]{1,0:T(8,128)(2,1)S(1)} %collective-permute-done.a1.p1, ...), custom_call_target="tpu_custom_call" | custom-call | flops 12650000384 | tf_op jit(solution)/shard_map/pallas_call | solution.py:88
  37.2 1.6 %collective-permute-start.21 = (bf16[512,128]{1,0:T(8,128)(2,1)S(1)}, bf16[512,128]{1,0:T(8,128)(2,1)S(1)}, u32[]{:S(2)}, u32[]{:S(2)}) collective-permute-start(bf16[512,128]{1,0:T(8,128)(2,1)S(1)} %shard_map.130.p0), channel_id=1, source_target_pairs={{0,2},{1,3},{2,0},{3,1},{4,6},{5,7},{6,4},{7,5},{8,10},{9,11},{10,... | collective-permute-start | bytes 393224 | tf_op jit(solution)/shard_map/ppermute | solution.py:494
  38.7 2.7 %collective-permute-start.22 = (bf16[512,128]{1,0:T(8,128)(2,1)S(1)}, bf16[512,128]{1,0:T(8,128)(2,1)S(1)}, u32[]{:S(2)}, u32[]{:S(2)}) collective-permute-start(bf16[512,128]{1,0:T(8,128)(2,1)S(1)} %shard_map.130.p0), channel_id=1, source_target_pairs={{0,4},{1,5},{2,6},{3,7},{4,0},{5,1},{6,2},{7,3},{8,12},{9,13},{10,... | collective-permute-start | bytes 393224 | tf_op jit(solution)/shard_map/ppermute | solution.py:494
  41.9 1.6 %collective-permute-start.11 = (bf16[1024,128]{1,0:T(8,128)(2,1)S(1)}, bf16[1024,128]{1,0:T(8,128)(2,1)S(1)}, u32[]{:S(2)}, u32[]{:S(2)}) collective-permute-start(bf16[1024,128]{1,0:T(8,128)(2,1)S(1)} %shard_map.122.w0), channel_id=1, source_target_pairs={{0,64},{8,72},{16,80},{24,88},{32,96},{40,104},{48,112},{56,120},{... | collective-permute-start | bytes 786440 | tf_op jit(solution)/shard_map/ppermute | solution.py:494
  43.6 3.2 %collective-permute-start.12 = (bf16[1024,128]{1,0:T(8,128)(2,1)S(1)}, bf16[1024,128]{1,0:T(8,128)(2,1)S(1)}, u32[]{:S(2)}, u32[]{:S(2)}) collective-permute-start(bf16[1024,128]{1,0:T(8,128)(2,1)S(1)} %shard_map.122.w0), channel_id=1, source_target_pairs={{0,128},{8,136},{16,144},{24,152},{32,160},{40,168},{48,176},{56,1... | collective-permute-start | bytes 786440 | tf_op jit(solution)/shard_map/ppermute | solution.py:494
  47.6 0.8 collective-permute-start.5
  48.3 1.8 %collective-permute-start.6 = (bf16[256,128]{1,0:T(8,128)(2,1)S(1)}, bf16[256,128]{1,0:T(8,128)(2,1)S(1)}, u32[]{:S(2)}, u32[]{:S(2)}) collective-permute-start(bf16[256,128]{1,0:T(8,128)(2,1)S(1)} %get-tuple-element.54), channel_id=1, source_target_pairs={{0,128},{8,136},{16,144},{24,152},{32,160},{40,168},{48,176},{56,1... | collective-permute-start | bytes 196616 | tf_op jit(solution)/shard_map/ppermute | solution.py:494
  50.2 2.2 %collective-permute-start.7 = (bf16[256,128]{1,0:T(8,128)(2,1)S(1)}, bf16[256,128]{1,0:T(8,128)(2,1)S(1)}, u32[]{:S(2)}, u32[]{:S(2)}) collective-permute-start(bf16[256,128]{1,0:T(8,128)(2,1)S(1)} %get-tuple-element.54), channel_id=1, source_target_pairs={{0,192},{8,200},{16,208},{24,216},{32,224},{40,232},{48,240},{56,2... | collective-permute-start | bytes 196616 | tf_op jit(solution)/shard_map/ppermute | solution.py:494
  52.4 3.0 %collective-permute-done.5.r1 = bf16[256,128]{1,0:T(8,128)(2,1)S(1)} collective-permute-done((bf16[256,128]{1,0:T(8,128)(2,1)S(1)}, bf16[256,128]{1,0:T(8,128)(2,1)S(1)}, u32[]{:S(2)}, u32[]{:S(2)}) %collective-permute-start.5) | collective-permute-done | bytes 65568 | tf_op jit(solution)/shard_map/ppermute | solution.py:494
  55.4 2.8 %collective-permute-start.13 = (bf16[1024,128]{1,0:T(8,128)(2,1)S(1)}, bf16[1024,128]{1,0:T(8,128)(2,1)S(1)}, u32[]{:S(2)}, u32[]{:S(2)}) collective-permute-start(bf16[1024,128]{1,0:T(8,128)(2,1)S(1)} %shard_map.122.w0), channel_id=1, source_target_pairs={{0,192},{8,200},{16,208},{24,216},{32,224},{40,232},{48,240},{56,2... | collective-permute-start | bytes 786440 | tf_op jit(solution)/shard_map/ppermute | solution.py:494
  59.0 1.9 %shard_map.125 = (bf16[512,128]{1,0:T(8,128)(2,1)S(1)}, f32[128,384]{1,0:T(8,128)S(1)}, f32[4,128,128]{2,1,0:T(8,128)S(1)}, f32[128,128]{1,0:T(8,128)S(1)}) custom-call(s32[8]{0:T(128)S(1)} %copy-done, f32[256,128]{1,0:T(8,128)S(1)} %get-tuple-element.53.own, bf16[256,128]{1,0:T(8,128)(2,1)S(1)} %collective-permute-done.5.r1, ...), custom_call_target="tpu_custom_call" | custom-call | flops 2300000000 | tf_op jit(solution)/shard_map/pallas_call | solution.py:88
  60.9 1.1 collective-permute-start.10
  62.5 2.0 %collective-permute-start.9 = (bf16[512,128]{1,0:T(8,128)(2,1)S(1)}, bf16[512,128]{1,0:T(8,128)(2,1)S(1)}, u32[]{:S(2)}, u32[]{:S(2)}) collective-permute-start(bf16[512,128]{1,0:T(8,128)(2,1)S(1)} %get-tuple-element.57.a0), channel_id=1, source_target_pairs={{0,16},{8,24},{16,0},{24,8},{32,48},{40,56},{48,32},{56,40},{64,80... | collective-permute-start | bytes 393224 | tf_op jit(solution)/shard_map/ppermute | solution.py:494
  64.5 7.3 %collective-permute-done.10.a3 = bf16[512,128]{1,0:T(8,128)(2,1)S(1)} collective-permute-done((bf16[512,128]{1,0:T(8,128)(2,1)S(1)}, bf16[512,128]{1,0:T(8,128)(2,1)S(1)}, u32[]{:S(2)}, u32[]{:S(2)}) %collective-permute-start.10) | collective-permute-done | bytes 131104 | tf_op jit(solution)/shard_map/ppermute | solution.py:494
  71.8 1.2 collective-permute-done.9.a2
  73.0 1.9 %shard_map.126 = (bf16[2048,128]{1,0:T(8,128)(2,1)S(1)}, bf16[2048,128]{1,0:T(8,128)(2,1)S(1)}) custom-call(s32[8]{0:T(128)S(1)} %copy-done, bf16[512,128]{1,0:T(8,128)(2,1)S(1)} %get-tuple-element.57.a0, bf16[512,128]{1,0:T(8,128)(2,1)S(1)} %collective-permute-done.8.a1, bf16[512,128]{1,0:T(8,128)(2,1)S(1)} %collective-permute-done.9.a2, ...), custom_call_target="tpu_custom_call" | custom-call | flops 3449999872 | tf_op jit(solution)/shard_map/pallas_call | solution.py:88
  75.0 2.0 %shard_map.132 = (f32[512,128]{1,0:T(8,128)S(1)}, bf16[512,128]{1,0:T(8,128)(2,1)S(1)}, bf16[512,128]{1,0:T(8,128)(2,1)S(1)}, bf16[512,128]{1,0:T(8,128)(2,1)S(1)}) custom-call(s32[8]{0:T(128)S(1)} %copy-done, bf16[2048,128]{1,0:T(8,128)(2,1)S(1)} %shard_map.131.ga, bf16[2048,128]{1,0:T(8,128)(2,1)S(1)} %collective-permute-done.24.gb, ...), custom_call_target="tpu_custom_call" | custom-call | flops 3449999872 | tf_op jit(solution)/shard_map/pallas_call | solution.py:88
  77.0 3.0 %collective-permute-start.25 = (bf16[512,128]{1,0:T(8,128)(2,1)S(1)}, bf16[512,128]{1,0:T(8,128)(2,1)S(1)}, u32[]{:S(2)}, u32[]{:S(2)}) collective-permute-start(bf16[512,128]{1,0:T(8,128)(2,1)S(1)} %get-tuple-element.69), channel_id=1, source_target_pairs={{0,8},{8,0},{16,24},{24,16},{32,40},{40,32},{48,56},{56,48},{64,72... | collective-permute-start | bytes 393224 | tf_op jit(solution)/shard_map/ppermute | solution.py:494
  80.6 1.0 collective-permute-start.27
  81.6 3.9 %collective-permute-done.25.r1 = bf16[512,128]{1,0:T(8,128)(2,1)S(1)} collective-permute-done((bf16[512,128]{1,0:T(8,128)(2,1)S(1)}, bf16[512,128]{1,0:T(8,128)(2,1)S(1)}, u32[]{:S(2)}, u32[]{:S(2)}) %collective-permute-start.25) | collective-permute-done | bytes 131104 | tf_op jit(solution)/shard_map/ppermute | solution.py:494
  85.5 4.6 %collective-permute-done.26.r2 = bf16[512,128]{1,0:T(8,128)(2,1)S(1)} collective-permute-done((bf16[512,128]{1,0:T(8,128)(2,1)S(1)}, bf16[512,128]{1,0:T(8,128)(2,1)S(1)}, u32[]{:S(2)}, u32[]{:S(2)}) %collective-permute-start.26) | collective-permute-done | bytes 131104 | tf_op jit(solution)/shard_map/ppermute | solution.py:494
  90.1 3.9 %collective-permute-done.27.r3 = bf16[512,128]{1,0:T(8,128)(2,1)S(1)} collective-permute-done((bf16[512,128]{1,0:T(8,128)(2,1)S(1)}, bf16[512,128]{1,0:T(8,128)(2,1)S(1)}, u32[]{:S(2)}, u32[]{:S(2)}) %collective-permute-start.27) | collective-permute-done | bytes 131104 | tf_op jit(solution)/shard_map/ppermute | solution.py:494
  93.9 1.5 %shard_map.133 = (bf16[4,128,128]{2,1,0:T(8,128)(2,1)S(1)}, bf16[128,128]{1,0:T(8,128)(2,1)S(1)}, bf16[128,128]{1,0:T(8,128)(2,1)S(1)}, f32[128,128]{1,0:T(8,128)S(1)}) custom-call(s32[8]{0:T(128)S(1)} %copy-done, f32[512,128]{1,0:T(8,128)S(1)} %get-tuple-element.68.own, bf16[512,128]{1,0:T(8,128)(2,1)S(1)} %collective-permute-done.25.r1, ...), custom_call_target="tpu_custom_call" | custom-call | flops 2300000000 | tf_op jit(solution)/shard_map/pallas_call | solution.py:88
  95.4 0.8 collective-permute-start.29
  96.2 2.1 %collective-permute-start.30 = (bf16[128,128]{1,0:T(8,128)(2,1)S(1)}, bf16[128,128]{1,0:T(8,128)(2,1)S(1)}, u32[]{:S(2)}, u32[]{:S(2)}) collective-permute-start(bf16[128,128]{1,0:T(8,128)(2,1)S(1)} %get-tuple-element.73), channel_id=1, source_target_pairs={{0,192},{8,200},{16,208},{24,216},{32,224},{40,232},{48,240},{56,2... | collective-permute-start | bytes 98312 | tf_op jit(solution)/shard_map/ppermute | solution.py:494
  99.4 4.0 %collective-permute-start.16 = (bf16[512,128]{1,0:T(8,128)(2,1)S(1)}, bf16[512,128]{1,0:T(8,128)(2,1)S(1)}, u32[]{:S(2)}, u32[]{:S(2)}) collective-permute-start(bf16[512,128]{1,0:T(8,128)(2,1)S(1)} %get-tuple-element.62), channel_id=1, source_target_pairs={{0,4},{1,5},{2,6},{3,7},{4,0},{5,1},{6,2},{7,3},{8,12},{9,13},{10,... | collective-permute-start | bytes 393224 | tf_op jit(solution)/shard_map/ppermute | solution.py:494
  103.4 1.6 %collective-permute-start.17 = (bf16[512,128]{1,0:T(8,128)(2,1)S(1)}, bf16[512,128]{1,0:T(8,128)(2,1)S(1)}, u32[]{:S(2)}, u32[]{:S(2)}) collective-permute-start(bf16[512,128]{1,0:T(8,128)(2,1)S(1)} %get-tuple-element.63), channel_id=1, source_target_pairs={{0,6},{1,7},{2,4},{3,5},{4,2},{5,3},{6,0},{7,1},{8,14},{9,15},{10,... | collective-permute-start | bytes 393224 | tf_op jit(solution)/shard_map/ppermute | solution.py:494
  105.0 1.1 shard_map.134
  106.2 1.3 %collective-permute-start.31 = (bf16[128,128]{1,0:T(8,128)(2,1)S(1)}, bf16[128,128]{1,0:T(8,128)(2,1)S(1)}, u32[]{:S(2)}, u32[]{:S(2)}) collective-permute-start(bf16[128,128]{1,0:T(8,128)(2,1)S(1)} %get-tuple-element.77), channel_id=1, source_target_pairs={{0,48},{8,56},{16,32},{24,40},{32,16},{40,24},{48,0},{56,8},{64,11... | collective-permute-start | bytes 98312 | tf_op jit(solution)/shard_map/ppermute | solution.py:494
  107.5 5.6 %shard_map.135 = (bf16[4,128,128]{2,1,0:T(8,128)(2,1)S(1)}, f32[512,128]{1,0:T(8,128)S(1)}, f32[512,128]{1,0:T(8,128)S(1)}) custom-call(s32[8]{0:T(128)S(1)} %copy-done, bf16[4,128,128]{2,1,0:T(8,128)(2,1)S(1)} %get-tuple-element.79.do, f32[1536,128]{1,0:T(8,128)S(1)} %get-tuple-element.56.held, f32[128,384]{1,0:T(8,128)S(1)} %get-tuple-element.80.far, ...), custom_call_target="tpu_custom_call" | custom-call | flops 8049999872 | tf_op jit(solution)/shard_map/pallas_call | solution.py:88
  113.1 1.1 shard_map.136
  114.2 2.7 %collective-permute-start.32 = (bf16[256,128]{1,0:T(8,128)(2,1)S(1)}, bf16[256,128]{1,0:T(8,128)(2,1)S(1)}, u32[]{:S(2)}, u32[]{:S(2)}) collective-permute-start(bf16[256,128]{1,0:T(8,128)(2,1)S(1)} %get-tuple-element.86), channel_id=1, source_target_pairs={{0,8},{8,0},{16,24},{24,16},{32,40},{40,32},{48,56},{56,48},{64,72... | collective-permute-start | bytes 196616 | tf_op jit(solution)/shard_map/ppermute | solution.py:494
  117.5 1.0 collective-permute-start.34
  119.1 2.9 %collective-permute-start.18 = (bf16[128,128]{1,0:T(8,128)(2,1)S(1)}, bf16[128,128]{1,0:T(8,128)(2,1)S(1)}, u32[]{:S(2)}, u32[]{:S(2)}) collective-permute-start(bf16[128,128]{1,0:T(8,128)(2,1)S(1)} %get-tuple-element.65), channel_id=1, source_target_pairs={{0,8},{8,0},{16,24},{24,16},{32,40},{40,32},{48,56},{56,48},{64,72... | collective-permute-start | bytes 98312 | tf_op jit(solution)/shard_map/ppermute | solution.py:494
  122.6 1.0 collective-permute-start.20
  123.6 1.0 collective-permute-done.34.r3
  124.5 1.3 %shard_map.137 = (bf16[128,512]{1,0:T(8,128)(2,1)}, bf16[128,512]{1,0:T(8,128)(2,1)}) custom-call(s32[8]{0:T(128)S(1)} %copy-done, bf16[256,128]{1,0:T(8,128)(2,1)S(1)} %get-tuple-element.85.r0, bf16[256,128]{1,0:T(8,128)(2,1)S(1)} %collective-permute-done.32.r1, bf16[256,128]{1,0:T(8,128)(2,1)S(1)} %collective-permute-done.33.r2, ...), custom_call_target="tpu_custom_call" | custom-call | flops 1150000000 | tf_op jit(solution)/shard_map/pallas_call | solution.py:88
  125.8 1.0 collective-permute-done.19.r2
  126.8 1.2 shard_map.129
  (49 shorter events, 6.9 us)
Async XLA Ops:
  0.6 12.6 %collective-permute-start.3 = (bf16[512,128]{1,0:T(8,128)(2,1)}, bf16[512,128]{1,0:T(8,128)(2,1)S(1)}, u32[]{:S(2)}, u32[]{:S(2)}) collective-permute-start(bf16[512,128]{1,0:T(8,128)(2,1)} %p0.1), channel_id=1, source_target_pairs={{0,48},{8,56},{16,32},{24,40},{32,16},{40,24},{48,0},{56,8},{64,11... | collective-permute-start | bytes 393224 | tf_op jit(solution)/shard_map/ppermute | solution.py:494
  6.7 6.5 %copy-start.2 = (bf16[512,128]{1,0:T(8,128)(2,1)S(1)}, bf16[512,128]{1,0:T(8,128)(2,1)}, u32[]{:S(2)}) copy-start(bf16[512,128]{1,0:T(8,128)(2,1)} %p0.1) | copy-start | bytes 393220
  6.7 18.5 %copy-start = (s32[8]{0:T(128)S(1)}, s32[8]{0:T(128)}, u32[]{:S(2)}) copy-start(s32[8]{0:T(128)} %stack.27.refs_0_.wh) | copy-start | bytes 100
  9.6 6.9 %collective-permute-start = (bf16[544,128]{1,0:T(8,128)(2,1)}, bf16[544,128]{1,0:T(8,128)(2,1)S(1)}, u32[]{:S(2)}, u32[]{:S(2)}) collective-permute-start(bf16[544,128]{1,0:T(8,128)(2,1)} %get-tuple-element.48), channel_id=1, source_target_pairs={{0,8},{8,0},{16,24},{24,16},{32,40},{40,32},{48,56},{56,48},{64,72... | collective-permute-start | bytes 417800 | tf_op jit(solution)/shard_map/ppermute | solution.py:494
  10.7 11.6 %collective-permute-start.1 = (bf16[544,128]{1,0:T(8,128)(2,1)}, bf16[544,128]{1,0:T(8,128)(2,1)S(1)}, u32[]{:S(2)}, u32[]{:S(2)}) collective-permute-start(bf16[544,128]{1,0:T(8,128)(2,1)} %get-tuple-element.49), channel_id=1, source_target_pairs={{0,16},{8,24},{16,0},{24,8},{32,48},{40,56},{48,32},{56,40},{64,80... | collective-permute-start | bytes 417800 | tf_op jit(solution)/shard_map/ppermute | solution.py:494
  12.2 13.1 %collective-permute-start.2 = (bf16[544,128]{1,0:T(8,128)(2,1)}, bf16[544,128]{1,0:T(8,128)(2,1)S(1)}, u32[]{:S(2)}, u32[]{:S(2)}) collective-permute-start(bf16[544,128]{1,0:T(8,128)(2,1)} %get-tuple-element.50), channel_id=1, source_target_pairs={{0,24},{8,16},{16,8},{24,0},{32,56},{40,48},{48,40},{56,32},{64,88... | collective-permute-start | bytes 417800 | tf_op jit(solution)/shard_map/ppermute | solution.py:494
  25.2 0.9 copy-start.3
  37.0 6.6 %collective-permute-start.4 = (bf16[256,128]{1,0:T(8,128)(2,1)S(1)}, bf16[256,128]{1,0:T(8,128)(2,1)S(1)}, u32[]{:S(2)}, u32[]{:S(2)}) collective-permute-start(bf16[256,128]{1,0:T(8,128)(2,1)S(1)} %get-tuple-element.52), channel_id=1, source_target_pairs={{0,48},{8,56},{16,32},{24,40},{32,16},{40,24},{48,0},{56,8},{64,11... | collective-permute-start | bytes 196616 | tf_op jit(solution)/shard_map/ppermute | solution.py:494
  37.1 21.9 %copy-start.1 = (f32[4,128,128]{2,1,0:T(8,128)S(1)}, f32[4,128,128]{2,1,0:T(8,128)}, u32[]{:S(2)}) copy-start(f32[4,128,128]{2,1,0:T(8,128)} %final.1) | copy-start | bytes 786436
  37.2 10.4 %collective-permute-start.21 = (bf16[512,128]{1,0:T(8,128)(2,1)S(1)}, bf16[512,128]{1,0:T(8,128)(2,1)S(1)}, u32[]{:S(2)}, u32[]{:S(2)}) collective-permute-start(bf16[512,128]{1,0:T(8,128)(2,1)S(1)} %shard_map.130.p0), channel_id=1, source_target_pairs={{0,2},{1,3},{2,0},{3,1},{4,6},{5,7},{6,4},{7,5},{8,10},{9,11},{10,... | collective-permute-start | bytes 393224 | tf_op jit(solution)/shard_map/ppermute | solution.py:494
  38.7 9.6 %collective-permute-start.22 = (bf16[512,128]{1,0:T(8,128)(2,1)S(1)}, bf16[512,128]{1,0:T(8,128)(2,1)S(1)}, u32[]{:S(2)}, u32[]{:S(2)}) collective-permute-start(bf16[512,128]{1,0:T(8,128)(2,1)S(1)} %shard_map.130.p0), channel_id=1, source_target_pairs={{0,4},{1,5},{2,6},{3,7},{4,0},{5,1},{6,2},{7,3},{8,12},{9,13},{10,... | collective-permute-start | bytes 393224 | tf_op jit(solution)/shard_map/ppermute | solution.py:494
  41.5 8.7 %collective-permute-start.23 = (bf16[512,128]{1,0:T(8,128)(2,1)S(1)}, bf16[512,128]{1,0:T(8,128)(2,1)S(1)}, u32[]{:S(2)}, u32[]{:S(2)}) collective-permute-start(bf16[512,128]{1,0:T(8,128)(2,1)S(1)} %shard_map.130.p0), channel_id=1, source_target_pairs={{0,6},{1,7},{2,4},{3,5},{4,2},{5,3},{6,0},{7,1},{8,14},{9,15},{10,... | collective-permute-start | bytes 393224 | tf_op jit(solution)/shard_map/ppermute | solution.py:494
  41.9 20.0 %collective-permute-start.11 = (bf16[1024,128]{1,0:T(8,128)(2,1)S(1)}, bf16[1024,128]{1,0:T(8,128)(2,1)S(1)}, u32[]{:S(2)}, u32[]{:S(2)}) collective-permute-start(bf16[1024,128]{1,0:T(8,128)(2,1)S(1)} %shard_map.122.w0), channel_id=1, source_target_pairs={{0,64},{8,72},{16,80},{24,88},{32,96},{40,104},{48,112},{56,120},{... | collective-permute-start | bytes 786440 | tf_op jit(solution)/shard_map/ppermute | solution.py:494
  43.6 18.9 %collective-permute-start.12 = (bf16[1024,128]{1,0:T(8,128)(2,1)S(1)}, bf16[1024,128]{1,0:T(8,128)(2,1)S(1)}, u32[]{:S(2)}, u32[]{:S(2)}) collective-permute-start(bf16[1024,128]{1,0:T(8,128)(2,1)S(1)} %shard_map.122.w0), channel_id=1, source_target_pairs={{0,128},{8,136},{16,144},{24,152},{32,160},{40,168},{48,176},{56,1... | collective-permute-start | bytes 786440 | tf_op jit(solution)/shard_map/ppermute | solution.py:494
  47.6 7.8 %collective-permute-start.5 = (bf16[256,128]{1,0:T(8,128)(2,1)S(1)}, bf16[256,128]{1,0:T(8,128)(2,1)S(1)}, u32[]{:S(2)}, u32[]{:S(2)}) collective-permute-start(bf16[256,128]{1,0:T(8,128)(2,1)S(1)} %get-tuple-element.54), channel_id=1, source_target_pairs={{0,64},{8,72},{16,80},{24,88},{32,96},{40,104},{48,112},{56,120},{... | collective-permute-start | bytes 196616 | tf_op jit(solution)/shard_map/ppermute | solution.py:494
  48.3 10.1 %collective-permute-start.6 = (bf16[256,128]{1,0:T(8,128)(2,1)S(1)}, bf16[256,128]{1,0:T(8,128)(2,1)S(1)}, u32[]{:S(2)}, u32[]{:S(2)}) collective-permute-start(bf16[256,128]{1,0:T(8,128)(2,1)S(1)} %get-tuple-element.54), channel_id=1, source_target_pairs={{0,128},{8,136},{16,144},{24,152},{32,160},{40,168},{48,176},{56,1... | collective-permute-start | bytes 196616 | tf_op jit(solution)/shard_map/ppermute | solution.py:494
  50.2 8.8 %collective-permute-start.7 = (bf16[256,128]{1,0:T(8,128)(2,1)S(1)}, bf16[256,128]{1,0:T(8,128)(2,1)S(1)}, u32[]{:S(2)}, u32[]{:S(2)}) collective-permute-start(bf16[256,128]{1,0:T(8,128)(2,1)S(1)} %get-tuple-element.54), channel_id=1, source_target_pairs={{0,192},{8,200},{16,208},{24,216},{32,224},{40,232},{48,240},{56,2... | collective-permute-start | bytes 196616 | tf_op jit(solution)/shard_map/ppermute | solution.py:494
  55.4 9.1 %collective-permute-start.13 = (bf16[1024,128]{1,0:T(8,128)(2,1)S(1)}, bf16[1024,128]{1,0:T(8,128)(2,1)S(1)}, u32[]{:S(2)}, u32[]{:S(2)}) collective-permute-start(bf16[1024,128]{1,0:T(8,128)(2,1)S(1)} %shard_map.122.w0), channel_id=1, source_target_pairs={{0,192},{8,200},{16,208},{24,216},{32,224},{40,232},{48,240},{56,2... | collective-permute-start | bytes 786440 | tf_op jit(solution)/shard_map/ppermute | solution.py:494
  58.4 16.6 %collective-permute-start.24 = (bf16[2048,128]{1,0:T(8,128)(2,1)S(1)}, bf16[2048,128]{1,0:T(8,128)(2,1)S(1)}, u32[]{:S(2)}, u32[]{:S(2)}) collective-permute-start(bf16[2048,128]{1,0:T(8,128)(2,1)S(1)} %shard_map.131.ga), channel_id=1, source_target_pairs={{0,1},{1,0},{2,3},{3,2},{4,5},{5,4},{6,7},{7,6},{8,9},{9,8},{10,11... | collective-permute-start | bytes 1572872 | tf_op jit(solution)/shard_map/ppermute | solution.py:494
  60.9 10.9 %collective-permute-start.10 = (bf16[512,128]{1,0:T(8,128)(2,1)S(1)}, bf16[512,128]{1,0:T(8,128)(2,1)S(1)}, u32[]{:S(2)}, u32[]{:S(2)}) collective-permute-start(bf16[512,128]{1,0:T(8,128)(2,1)S(1)} %get-tuple-element.57.a0), channel_id=1, source_target_pairs={{0,24},{8,16},{16,8},{24,0},{32,56},{40,48},{48,40},{56,32},{64,88... | collective-permute-start | bytes 393224 | tf_op jit(solution)/shard_map/ppermute | solution.py:494
  62.0 9.8 %collective-permute-start.8 = (bf16[512,128]{1,0:T(8,128)(2,1)S(1)}, bf16[512,128]{1,0:T(8,128)(2,1)S(1)}, u32[]{:S(2)}, u32[]{:S(2)}) collective-permute-start(bf16[512,128]{1,0:T(8,128)(2,1)S(1)} %get-tuple-element.57.a0), channel_id=1, source_target_pairs={{0,8},{8,0},{16,24},{24,16},{32,40},{40,32},{48,56},{56,48},{64,72... | collective-permute-start | bytes 393224 | tf_op jit(solution)/shard_map/ppermute | solution.py:494
  62.5 10.5 %collective-permute-start.9 = (bf16[512,128]{1,0:T(8,128)(2,1)S(1)}, bf16[512,128]{1,0:T(8,128)(2,1)S(1)}, u32[]{:S(2)}, u32[]{:S(2)}) collective-permute-start(bf16[512,128]{1,0:T(8,128)(2,1)S(1)} %get-tuple-element.57.a0), channel_id=1, source_target_pairs={{0,16},{8,24},{16,0},{24,8},{32,48},{40,56},{48,32},{56,40},{64,80... | collective-permute-start | bytes 393224 | tf_op jit(solution)/shard_map/ppermute | solution.py:494
  74.9 24.1 %collective-permute-start.14 = (bf16[2048,128]{1,0:T(8,128)(2,1)S(1)}, bf16[2048,128]{1,0:T(8,128)(2,1)S(1)}, u32[]{:S(2)}, u32[]{:S(2)}) collective-permute-start(bf16[2048,128]{1,0:T(8,128)(2,1)S(1)} %get-tuple-element.59), channel_id=1, source_target_pairs={{0,1},{1,0},{2,3},{3,2},{4,5},{5,4},{6,7},{7,6},{8,9},{9,8},{10,11... | collective-permute-start | bytes 1572872 | tf_op jit(solution)/shard_map/ppermute | solution.py:494
  77.0 8.5 %collective-permute-start.25 = (bf16[512,128]{1,0:T(8,128)(2,1)S(1)}, bf16[512,128]{1,0:T(8,128)(2,1)S(1)}, u32[]{:S(2)}, u32[]{:S(2)}) collective-permute-start(bf16[512,128]{1,0:T(8,128)(2,1)S(1)} %get-tuple-element.69), channel_id=1, source_target_pairs={{0,8},{8,0},{16,24},{24,16},{32,40},{40,32},{48,56},{56,48},{64,72... | collective-permute-start | bytes 393224 | tf_op jit(solution)/shard_map/ppermute | solution.py:494
  80.0 10.0 %collective-permute-start.26 = (bf16[512,128]{1,0:T(8,128)(2,1)S(1)}, bf16[512,128]{1,0:T(8,128)(2,1)S(1)}, u32[]{:S(2)}, u32[]{:S(2)}) collective-permute-start(bf16[512,128]{1,0:T(8,128)(2,1)S(1)} %get-tuple-element.70), channel_id=1, source_target_pairs={{0,16},{8,24},{16,0},{24,8},{32,48},{40,56},{48,32},{56,40},{64,80... | collective-permute-start | bytes 393224 | tf_op jit(solution)/shard_map/ppermute | solution.py:494
  80.6 13.3 %collective-permute-start.27 = (bf16[512,128]{1,0:T(8,128)(2,1)S(1)}, bf16[512,128]{1,0:T(8,128)(2,1)S(1)}, u32[]{:S(2)}, u32[]{:S(2)}) collective-permute-start(bf16[512,128]{1,0:T(8,128)(2,1)S(1)} %get-tuple-element.71), channel_id=1, source_target_pairs={{0,24},{8,16},{16,8},{24,0},{32,56},{40,48},{48,40},{56,32},{64,88... | collective-permute-start | bytes 393224 | tf_op jit(solution)/shard_map/ppermute | solution.py:494
  95.4 9.6 %collective-permute-start.29 = (bf16[128,128]{1,0:T(8,128)(2,1)S(1)}, bf16[128,128]{1,0:T(8,128)(2,1)S(1)}, u32[]{:S(2)}, u32[]{:S(2)}) collective-permute-start(bf16[128,128]{1,0:T(8,128)(2,1)S(1)} %get-tuple-element.73), channel_id=1, source_target_pairs={{0,128},{8,136},{16,144},{24,152},{32,160},{40,168},{48,176},{56,1... | collective-permute-start | bytes 98312 | tf_op jit(solution)/shard_map/ppermute | solution.py:494
  96.2 8.8 %collective-permute-start.30 = (bf16[128,128]{1,0:T(8,128)(2,1)S(1)}, bf16[128,128]{1,0:T(8,128)(2,1)S(1)}, u32[]{:S(2)}, u32[]{:S(2)}) collective-permute-start(bf16[128,128]{1,0:T(8,128)(2,1)S(1)} %get-tuple-element.73), channel_id=1, source_target_pairs={{0,192},{8,200},{16,208},{24,216},{32,224},{40,232},{48,240},{56,2... | collective-permute-start | bytes 98312 | tf_op jit(solution)/shard_map/ppermute | solution.py:494
  98.3 5.1 %collective-permute-start.28 = (bf16[128,128]{1,0:T(8,128)(2,1)S(1)}, bf16[128,128]{1,0:T(8,128)(2,1)S(1)}, u32[]{:S(2)}, u32[]{:S(2)}) collective-permute-start(bf16[128,128]{1,0:T(8,128)(2,1)S(1)} %get-tuple-element.72), channel_id=1, source_target_pairs={{0,64},{8,72},{16,80},{24,88},{32,96},{40,104},{48,112},{56,120},{... | collective-permute-start | bytes 98312 | tf_op jit(solution)/shard_map/ppermute | solution.py:494
  99.1 18.4 %collective-permute-start.15 = (bf16[512,128]{1,0:T(8,128)(2,1)S(1)}, bf16[512,128]{1,0:T(8,128)(2,1)S(1)}, u32[]{:S(2)}, u32[]{:S(2)}) collective-permute-start(bf16[512,128]{1,0:T(8,128)(2,1)S(1)} %get-tuple-element.61), channel_id=1, source_target_pairs={{0,2},{1,3},{2,0},{3,1},{4,6},{5,7},{6,4},{7,5},{8,10},{9,11},{10,... | collective-permute-start | bytes 393224 | tf_op jit(solution)/shard_map/ppermute | solution.py:494
  99.4 19.1 %collective-permute-start.16 = (bf16[512,128]{1,0:T(8,128)(2,1)S(1)}, bf16[512,128]{1,0:T(8,128)(2,1)S(1)}, u32[]{:S(2)}, u32[]{:S(2)}) collective-permute-start(bf16[512,128]{1,0:T(8,128)(2,1)S(1)} %get-tuple-element.62), channel_id=1, source_target_pairs={{0,4},{1,5},{2,6},{3,7},{4,0},{5,1},{6,2},{7,3},{8,12},{9,13},{10,... | collective-permute-start | bytes 393224 | tf_op jit(solution)/shard_map/ppermute | solution.py:494
  103.4 15.1 %collective-permute-start.17 = (bf16[512,128]{1,0:T(8,128)(2,1)S(1)}, bf16[512,128]{1,0:T(8,128)(2,1)S(1)}, u32[]{:S(2)}, u32[]{:S(2)}) collective-permute-start(bf16[512,128]{1,0:T(8,128)(2,1)S(1)} %get-tuple-element.63), channel_id=1, source_target_pairs={{0,6},{1,7},{2,4},{3,5},{4,2},{5,3},{6,0},{7,1},{8,14},{9,15},{10,... | collective-permute-start | bytes 393224 | tf_op jit(solution)/shard_map/ppermute | solution.py:494
  106.2 6.9 %collective-permute-start.31 = (bf16[128,128]{1,0:T(8,128)(2,1)S(1)}, bf16[128,128]{1,0:T(8,128)(2,1)S(1)}, u32[]{:S(2)}, u32[]{:S(2)}) collective-permute-start(bf16[128,128]{1,0:T(8,128)(2,1)S(1)} %get-tuple-element.77), channel_id=1, source_target_pairs={{0,48},{8,56},{16,32},{24,40},{32,16},{40,24},{48,0},{56,8},{64,11... | collective-permute-start | bytes 98312 | tf_op jit(solution)/shard_map/ppermute | solution.py:494
  114.2 8.4 %collective-permute-start.32 = (bf16[256,128]{1,0:T(8,128)(2,1)S(1)}, bf16[256,128]{1,0:T(8,128)(2,1)S(1)}, u32[]{:S(2)}, u32[]{:S(2)}) collective-permute-start(bf16[256,128]{1,0:T(8,128)(2,1)S(1)} %get-tuple-element.86), channel_id=1, source_target_pairs={{0,8},{8,0},{16,24},{24,16},{32,40},{40,32},{48,56},{56,48},{64,72... | collective-permute-start | bytes 196616 | tf_op jit(solution)/shard_map/ppermute | solution.py:494
  116.9 6.7 %collective-permute-start.33 = (bf16[256,128]{1,0:T(8,128)(2,1)S(1)}, bf16[256,128]{1,0:T(8,128)(2,1)S(1)}, u32[]{:S(2)}, u32[]{:S(2)}) collective-permute-start(bf16[256,128]{1,0:T(8,128)(2,1)S(1)} %get-tuple-element.87), channel_id=1, source_target_pairs={{0,16},{8,24},{16,0},{24,8},{32,48},{40,56},{48,32},{56,40},{64,80... | collective-permute-start | bytes 196616 | tf_op jit(solution)/shard_map/ppermute | solution.py:494
  117.5 7.1 %collective-permute-start.34 = (bf16[256,128]{1,0:T(8,128)(2,1)S(1)}, bf16[256,128]{1,0:T(8,128)(2,1)S(1)}, u32[]{:S(2)}, u32[]{:S(2)}) collective-permute-start(bf16[256,128]{1,0:T(8,128)(2,1)S(1)} %get-tuple-element.88), channel_id=1, source_target_pairs={{0,24},{8,16},{16,8},{24,0},{32,56},{40,48},{48,40},{56,32},{64,88... | collective-permute-start | bytes 196616 | tf_op jit(solution)/shard_map/ppermute | solution.py:494
  119.1 6.7 %collective-permute-start.18 = (bf16[128,128]{1,0:T(8,128)(2,1)S(1)}, bf16[128,128]{1,0:T(8,128)(2,1)S(1)}, u32[]{:S(2)}, u32[]{:S(2)}) collective-permute-start(bf16[128,128]{1,0:T(8,128)(2,1)S(1)} %get-tuple-element.65), channel_id=1, source_target_pairs={{0,8},{8,0},{16,24},{24,16},{32,40},{40,32},{48,56},{56,48},{64,72... | collective-permute-start | bytes 98312 | tf_op jit(solution)/shard_map/ppermute | solution.py:494
  122.0 4.8 %collective-permute-start.19 = (bf16[128,128]{1,0:T(8,128)(2,1)S(1)}, bf16[128,128]{1,0:T(8,128)(2,1)S(1)}, u32[]{:S(2)}, u32[]{:S(2)}) collective-permute-start(bf16[128,128]{1,0:T(8,128)(2,1)S(1)} %get-tuple-element.66), channel_id=1, source_target_pairs={{0,16},{8,24},{16,0},{24,8},{32,48},{40,56},{48,32},{56,40},{64,80... | collective-permute-start | bytes 98312 | tf_op jit(solution)/shard_map/ppermute | solution.py:494
  122.6 4.3 %collective-permute-start.20 = (bf16[128,128]{1,0:T(8,128)(2,1)S(1)}, bf16[128,128]{1,0:T(8,128)(2,1)S(1)}, u32[]{:S(2)}, u32[]{:S(2)}) collective-permute-start(bf16[128,128]{1,0:T(8,128)(2,1)S(1)} %get-tuple-element.67), channel_id=1, source_target_pairs={{0,24},{8,16},{16,8},{24,0},{32,56},{40,48},{48,40},{56,32},{64,88... | collective-permute-start | bytes 98312 | tf_op jit(solution)/shard_map/ppermute | solution.py:494
where the time goes:
time: 131 us; the launch traced here: 128 us
  starting transfers between devices  54.1 us (41%)
  waiting for transfers between devices  38.8 us (30%)
  Pallas kernels  32.8 us (25%)
  local copies, waits for them, and re-layouts  1.55 us (1%)
    ppermute x35, starting transfers between devices, xor(): lax.ppermute(value, axis, [(s, s ^ mask) for s in range(lax.axis_size(axi...  54.1 us
    ppermute x35, waiting for transfers between devices, xor(): lax.ppermute(value, axis, [(s, s ^ mask) for s in range(lax.axis_size(axi...  38.8 us
    pallas_call x17, Pallas kernels, call(): pl.pallas_call(fetching if fetch else body, out_shape=[jax.ShapeDtypeStru...  32.8 us
  transfers between devices with their start and end apart: 35, of which 14 were waited for; matrix products, arithmetic and copies ran while one was open for 0% of the time, Pallas kernels for 16%

commit v1 on v0

v1 whole, which is shorter than its diff:
```python
import jax
import jax.numpy as jnp
from jax import lax
from jax.experimental import pallas as pl
from jax.experimental.pallas import tpu as pltpu
from jax.sharding import PartitionSpec as P

F32 = jnp.float32
BF = jnp.bfloat16
NN = (((1,), (0,)), ((), ()))
NT = (((1,), (1,)), ((), ()))
TIERS = 7
SCALE = 1e8
SCAL = 32
SOME_VMEM = 16 * 1024 * 1024
MOST_VMEM = 63_000_000


SIZES = (("a", 1024), ("a2", 512), ("a4", 256), ("s", 1536), ("m", 1024), ("w", 512), ("u", 512), ("inv", 512),
         ("er", 512), ("kt", 512), ("k", 512))
LATER = (("p", 512), ("qe", 512), ("qn", 512))
STARTS = {}


def lay(sizes):
    total = 0
    for name, rows in sizes:
        STARTS[name] = total
        total += rows
    return total


KEPT = lay(SIZES)
KEPT_LATER = lay(LATER)
READS = [(c, n) for c in range(8) for n in (1, 2, 3) if c >> (n - 1) & 1]


def at(name, index, rows=128):
    start = STARTS[name] + index * rows
    return slice(start, start + rows)


def mm(a, b, dims=NN):
    return lax.dot_general(a, b, dims, preferred_element_type=F32)


def split(x):
    hi = x.astype(BF)
    return hi, (x - hi.astype(F32)).astype(BF)


def stack(dims, a, b):
    return mm(jnp.concatenate(a, 1), jnp.concatenate(b, dims[0][1][0]), dims)


def dot3(a, b, dims=NN):
    ah, al = split(a)
    bh, bl = split(b)
    return stack(dims, [ah, al, ah], [bh, bh, bl])


def dot2(a, b, dims=NN):
    b = b.astype(BF)
    return stack(dims, split(a), [b, b])


TREE = dot3


def tn(a, b, dot):
    return dot(a.T, b)


def iotas(rows, cols):
    return (
        lax.broadcasted_iota(jnp.int32, (rows, cols), 0),
        lax.broadcasted_iota(jnp.int32, (rows, cols), 1),
    )


def call(us, body, out_shapes, ins, scratch=(), fetch=False, after=()):
    count, outs, waits = len(ins), len(out_shapes), len(after)
    big = [n for n, a in enumerate(ins) if a.dtype != jnp.int32]

    def fetching(*refs):
        held = refs[count + outs : count + outs + len(big)]
        sems = refs[count + outs + len(big)]
        own = list(refs[:count])
        copies = []
        for n, index in enumerate(big):
            copies.append(pltpu.make_async_copy(refs[index], held[n], sems.at[n]))
            own[index] = held[n]
        for copy in copies:
            copy.start()
        for copy in copies:
            copy.wait()
        body(*own, *refs[count : count + outs], *refs[count + outs + len(big) + 1 :])

    def waiting(*refs):
        (fetching if fetch else body)(*refs[:count], *refs[count + waits :])

    space = pltpu.HBM if fetch else pltpu.VMEM
    extra = [pltpu.VMEM(ins[n].shape, ins[n].dtype) for n in big] + [pltpu.SemaphoreType.DMA((len(big),))]
    with jax.named_scope(body.__name__.removesuffix("_body")):
        return pl.pallas_call(
            waiting,
            out_shape=[jax.ShapeDtypeStruct(s, d) for s, d in out_shapes],
            in_specs=[pl.BlockSpec(memory_space=pltpu.SMEM if a.dtype == jnp.int32 else space) for a in ins]
            + [pl.BlockSpec(memory_space=pl.ANY)] * waits,
            out_specs=[pl.BlockSpec(memory_space=pltpu.VMEM)] * outs,
            scratch_shapes=(extra if fetch else []) + list(scratch),
            cost_estimate=pl.CostEstimate(flops=int(us * SCALE), bytes_accessed=0, transcendentals=0),
            compiler_params=pltpu.CompilerParams(vmem_limit_bytes=MOST_VMEM if fetch else SOME_VMEM),
        )(*ins, *after)


def pack_body(wh, ends, q, k, v, gy, gate, rate, tiers, *rest):
    outs, scal = rest[:-1], rest[-1]
    own, core = wh[4], wh[5]
    lane = lax.broadcasted_iota(jnp.int32, (1, 128), 1)
    keep = jnp.where(
        lane < 64, 1.0 - ends[0].astype(F32), 1.0 - ends[1].astype(F32)
    )

    def put(row, value, parts):
        for part in range(parts):
            piece = value.astype(BF).astype(F32)
            scal[row + part : row + part + 1, :] = piece
            value = value - piece

    for m in range(4):
        j = own ^ m
        cols = pl.ds(pl.multiple_of(j * 128, 128), 128)
        gcols = pl.ds(pl.multiple_of((j ^ (2 * core)) * 128, 128), 128)
        scal[...] = jnp.zeros((SCAL, 128), F32)
        put(0, gate[pl.ds(j, 1), :], 3)
        put(3, rate[pl.ds(j, 1), :], 2)
        for tier in range(TIERS):
            put(5 + 2 * tier, tiers[tier, pl.ds(j, 1), :], 2)
        scal[19:20, :] = keep
        outs[m][0:128, :] = k[:, cols]
        outs[m][128:256, :] = v[:, cols]
        outs[m][256:288, :] = scal[...].astype(BF)
        outs[m][288:416, :] = q[:, cols]
        outs[m][416:544, :] = gy[:, gcols]


def collect_body(p0, p1, p2, p3, out):
    for m, p in enumerate((p0, p1, p2, p3)):
        out[128 * m : 128 * m + 128, :] = p[416:544, :]


def join_body(p0, p1, p2, p3, out):
    for m, p in enumerate((p0, p1, p2, p3)):
        out[512 * m : 512 * m + 512, :] = p[...]


def block_masks():
    row, col = iotas(128, 128)
    same = (row >> 6) == (col >> 6)
    return row, col, same & (row >= col), same & (row > col)


def gates(scal, lblk):
    cum3 = mm(lblk, scal, NT)
    eye = jnp.where(jnp.equal(*iotas(128, 128)), 1.0, 0.0).astype(BF)
    return cum3[:, 0:1] + cum3[:, 1:2] + cum3[:, 2:3], mm(eye, scal, NT)


def block_body(wh, a0, a1, a2, a3, ab_out, abf_out, kept, pack):
    zlo = wh[0]
    for m, a in enumerate((a0, a1, a2, a3)):
        pack[pl.ds(zlo ^ m, 1)] = a[0:288, :][None]
    row, col, causal, strict = block_masks()
    eye = row == col
    eyef = eye.astype(F32)
    lblk = causal.astype(BF)
    trans, writes = [], []
    for i in range(4):
        k = pack[i, 0:128, :]
        v = pack[i, 128:256, :]
        scal = pack[i, 256:288, :]
        scalf = scal.astype(F32)
        cum_col, cols = gates(scal, lblk)
        cumr = mm(scal, lblk, NT)
        cum_row = cumr[0:1] + cumr[1:2] + cumr[2:3]
        beta_col = cols[:, 3:4] + cols[:, 4:5]
        beta_row = scalf[3:4] + scalf[4:5]
        kf = k.astype(F32)
        rk_col = lax.rsqrt(jnp.sum(kf * kf, 1, keepdims=True) + 1e-6)
        rk_row = jnp.sum(jnp.where(eye, rk_col, 0.0), 0, keepdims=True)
        decay = rk_row * jnp.where(causal, jnp.exp(jnp.where(causal, cum_col - cum_row, 0.0)), 0.0)
        kept[at("er", i), :] = decay
        kept[at("k", i), :] = kf
        lower = jnp.where(strict, (beta_col * rk_col) * (decay * mm(k, k, NT)), 0.0)
        inv = eyef - jnp.where((row >> 1) == (col >> 1), lower, 0.0)
        for bit in range(1, 6):
            near = ((row >> (bit + 1)) == (col >> (bit + 1))) & ((row >> bit) != (col >> bit))
            inv = inv - dot3(dot3(inv, jnp.where(near, lower, 0.0)), inv)
        kept[at("inv", i), :] = inv
        w = dot2(inv * (beta_row * jnp.exp(cum_row) * rk_row), k)
        u = dot2(inv * beta_row, v)
        wu = jnp.concatenate([w, u], 1)
        kept[at("w", i), :] = w
        kept[at("u", i), :] = u
        last0, last1 = cum_row[:, 63:64], cum_row[:, 127:128]
        tail = jnp.exp(jnp.where(row[:, 0:1] < 64, last0, last1) - cum_col) * rk_col
        kept[at("kt", i), :] = tail * kf
        rhs = wu * tail
        top = lax.broadcasted_iota(jnp.int32, (128, 256), 0) < 64
        rhs = jnp.concatenate([jnp.where(top, rhs, 0.0), jnp.where(top, 0.0, rhs)], 1)
        kt = kf.T.astype(BF)
        ab = stack(NN, [kt, kt], split(rhs))
        for b, last in ((0, last0), (1, last1)):
            keep = scalf[19:20, 64 * b : 64 * b + 1]
            trans.append(keep * (jnp.exp(last) * eyef - ab[:, 256 * b : 256 * b + 128]))
            writes.append(keep * ab[:, 256 * b + 128 : 256 * b + 256])

    def both(a, x, y):
        r = TREE(a, jnp.concatenate([x, y], 1))
        return r[:, 0:128], r[:, 128:256]

    for c in range(8):
        kept[at("a", c), :] = trans[c]
    t2, w2 = [], []
    for p in range(4):
        t, s = both(trans[2 * p + 1], trans[2 * p], writes[2 * p])
        t2.append(t)
        w2.append(s + writes[2 * p + 1])
        kept[at("a2", p), :] = t
    t4, w4 = [], []
    for h in range(2):
        t, s = both(t2[2 * h + 1], t2[2 * h], w2[2 * h])
        t4.append(t)
        w4.append(s + w2[2 * h + 1])
        kept[at("a4", h), :] = t
    tg, sg = both(t4[1], t4[0], w4[0])
    sg = sg + w4[1]
    ab_out[0:128, :] = tg.astype(BF)
    ab_out[128:256, :] = sg.astype(BF)
    abf_out[0:128, :] = tg
    abf_out[128:256, :] = sg
    map3, read3 = [], []
    for h in range(2):
        t, s = both(trans[4 * h + 2], t2[2 * h], w2[2 * h])
        map3.append(t)
        read3.append(s)
    maps = [eyef, trans[0], t2[0], map3[0], t4[0]]
    upper = [w4[0]]
    for inner in (trans[4], t2[2], map3[1]):
        t, s = both(inner, t4[0], w4[0])
        maps.append(t)
        upper.append(s)
    for c in range(8):
        kept[at("m", c), :] = maps[c]
    for n, (c, level) in enumerate(READS):
        if level == 1:
            state = writes[c - 1]
        elif level == 2:
            state = read3[c >> 2] if c & 1 else w2[2 * (c >> 2)]
        else:
            state = upper[c - 4]
        kept[at("s", n), :] = state


def query_body(wh, a0, a1, a2, a3, kept, held, later, scals, qs):
    for m, a in enumerate((a0, a1, a2, a3)):
        scals[pl.ds(wh[0] ^ m, 1)] = a[256:288, :][None]
        qs[pl.ds(wh[0] ^ m, 1)] = a[288:416, :][None]
    lblk = block_masks()[2].astype(BF)
    for i in range(4):
        q = qs[i]
        qf = q.astype(F32)
        cum_col, cols = gates(scals[i], lblk)
        exp_col = jnp.exp(cum_col)
        rq_col = lax.rsqrt(jnp.sum(qf * qf, 1, keepdims=True) + 1e-6)
        scores = kept[at("er", i), :] * (rq_col * mm(q, kept[at("k", i), :].astype(BF), NT))
        later[at("p", i), :] = scores
        pw = dot2(scores, jnp.concatenate([kept[at("w", i), :], kept[at("u", i), :]], 1))
        qn = rq_col * qf
        qe = exp_col * qn - pw[:, 0:128]
        later[at("qe", i), :] = qe
        later[at("qn", i), :] = qn
        weights = [cols[:, 5 + 2 * n : 6 + 2 * n] + cols[:, 6 + 2 * n : 7 + 2 * n] for n in range(TIERS)]
        beta_col = cols[:, 3:4] + cols[:, 4:5]
        held[i * 128 : (i + 1) * 128, :] = jnp.concatenate(
            weights + [cols[:, 19:20], rq_col, exp_col, beta_col, jnp.zeros((128, 128 - TIERS - 4), F32)], 1
        )
        for c in (2 * i, 2 * i + 1):
            rows = slice(64 * (c & 1), 64 * (c & 1) + 64)
            levels = [n for n in (1, 2, 3) if c >> (n - 1) & 1]
            rhs = jnp.concatenate(
                [kept[at("s", READS.index((c, n))), :] for n in levels] + [kept[at("m", c), :]], 1
            )
            read = dot2(qe[rows], rhs)
            out = weights[0][rows] * pw[rows, 128:256]
            for n, level in enumerate(levels):
                out = out + weights[level][rows] * read[:, 128 * n : 128 * n + 128]
            held[1024 + 64 * c : 1024 + 64 * c + 64, :] = out
            held[512 + 64 * c : 512 + 64 * c + 64, :] = read[:, 128 * len(levels) :]


def pair_body(wh, own, other, bf_out, f_out, omap_out):
    up = wh[1] == 1
    o = other[...].astype(F32)
    mine = own[...]
    low = jnp.where(up, o, mine)
    high = jnp.where(up, mine, o)
    both = dot3(high[0:128], jnp.concatenate([low[0:128], low[128:256]], 1))
    t = both[:, 0:128]
    s = both[:, 128:256] + high[128:256]
    f_out[0:128, :] = t
    f_out[128:256, :] = s
    bf_out[0:128, :] = t.astype(BF)
    bf_out[128:256, :] = s.astype(BF)
    row, col = iotas(128, 128)
    omap_out[0:128, :] = jnp.where(up, low[0:128], (row == col).astype(F32))
    omap_out[128:256, :] = jnp.where(up, low[128:256], 0.0)


def far_body(wh, own, r1, r2, r3, omap, held, final, attn_out, s_out, up_out, fin_out, order):
    y = wh[2]
    for n, r in enumerate((own, r1, r2, r3)):
        order[pl.ds(y ^ n, 1)] = r[...].astype(F32)[None]
    up_out[...] = order[:, 0:128, :]
    o = omap[0:128, :]
    b5 = order[pl.ds(y ^ 1, 1)][0][128:256]
    b01 = dot3(order[1, 0:128, :], order[0, 128:256, :]) + order[1, 128:256, :]
    b6 = jnp.where(y == 3, dot3(order[2, 0:128, :], b01), b01)
    both = dot3(o, jnp.concatenate([jnp.where((y & 1) == 1, b5, 0.0), jnp.where(y >= 2, b6, 0.0)], 1))
    states = jnp.concatenate([omap[128:256, :], both], 1)
    s_out[...] = states
    read = dot3(held[512:1024, :], states)
    out = held[1024:1536, :]
    for n in range(3):
        out = out + held[0:512, 4 + n : 5 + n] * read[:, 128 * n : 128 * n + 128]
    attn_out[...] = out.astype(BF)
    f = final[pl.ds(wh[4], 1)][0]
    for j in (3, 2, 1):
        f = jnp.where(y < j, tn(order[j, 0:128, :], f, dot3), f)
    fin_out[...] = f


def join_weight_body(p0, p1, pack, out, own):
    out[0:512, :] = p0[...]
    out[512:1024, :] = p1[...]
    own[...] = pack[...]


def order_weight(wh, parts, held):
    for n, part in enumerate(parts):
        for t in range(2):
            hb = 2 * (wh[2] ^ n) + (wh[1] ^ t)
            held[pl.ds(hb, 1)] = part[512 * t : 512 * t + 512, :][None]


def back_product_body(wh, ga, gb, w0, w1, w2, w3, own_out, o1, o2, o3, held):
    order_weight(wh, (w0, w1, w2, w3), held)
    total = None
    for n in range(4):
        for core, g in enumerate((ga, gb)):
            hb = wh[3] ^ (2 * n + core)
            w = held[pl.ds(hb, 1)][0]
            part = mm(g[512 * n : 512 * n + 512, :], w, NT)
            total = part if total is None else total + part
    acc = total
    for j in range(4):
        piece = acc[:, 128 * j : 128 * j + 128]

        for m, out in enumerate((own_out, o1, o2, o3)):

            @pl.when((wh[4] ^ m) == j)
            def _(piece=piece, out=out):
                out[...] = piece.astype(out.dtype)


def reach_body(wh, own, r1, r2, r3, held, omap, do_out, z5_out, z6_out, x4_out):
    for m in range(4):
        total = own[128 * m : 128 * m + 128, :]
        for k, r in ((1, r1), (2, r2), (3, r3)):
            total = total + r[128 * (m ^ k) : 128 * (m ^ k) + 128, :].astype(F32)
        do_out[pl.ds(wh[0] ^ m, 1)] = total.astype(BF)[None]
    do = do_out[...].reshape(512, 128).astype(F32)
    weighted = []
    for n in range(3):
        weighted.append(held[0:512, 4 + n : 5 + n] * do)
    x = tn(held[512:1024, :], jnp.concatenate(weighted, 1), dot2)
    x4_out[...] = jnp.where(wh[1] == 1, x[:, 0:128], 0.0)
    z = tn(omap[0:128, :], x[:, 128:384], dot2)
    z5_out[...] = z[:, 0:128].astype(BF)
    z6_out[...] = z[:, 128:256].astype(BF)


def grad_body(wh, do, held, far, kept, later, dq_out, dv_out, gmap_out):
    def weight(c, level):
        return held[64 * c : 64 * c + 64, level : level + 1]

    dof = do[...].reshape(512, 128).astype(F32)
    wd = [held[0:512, 4 + n : 5 + n] * dof for n in range(3)]
    carried = dot2(jnp.concatenate(wd, 1), far[...], NT)
    reach = {}
    dqe = []
    for c in range(8):
        rows = slice(64 * (c & 1), 64 * (c & 1) + 64)
        doc = do[c >> 1, rows, :].astype(F32)
        levels = [n for n in (1, 2, 3) if c >> (n - 1) & 1]
        left = jnp.concatenate([weight(c, n) * doc for n in levels] + [carried[64 * c : 64 * c + 64]], 1)
        right = jnp.concatenate(
            [kept[at("s", READS.index((c, n))), :] for n in levels] + [kept[at("m", c), :]], 1
        )
        dqe.append(dot2(left, right, NT))
        if levels:
            r = tn(later[at("qe", c, 64), :], left[:, 0 : 128 * len(levels)], dot2)
            for n, level in enumerate(levels):
                reach[c, level] = r[:, 128 * n : 128 * n + 128]
    for i in range(4):
        doc = do[i].astype(F32)
        rows = slice(128 * i, 128 * i + 128)
        dqei = jnp.concatenate([dqe[2 * i], dqe[2 * i + 1]], 0)
        wu = jnp.concatenate([kept[at("w", i), :], kept[at("u", i), :]], 1)
        dp = dot2(jnp.concatenate([-dqei, held[rows, 0:1] * doc], 1), wu, NT) * kept[at("er", i), :]
        dqn = held[rows, 9:10] * dqei + dot2(dp, kept[at("k", i), :])
        q = later[at("qn", i), :]
        dq_out[i] = (held[rows, 8:9] * (dqn - q * jnp.sum(q * dqn, 1, keepdims=True))).astype(BF)
    row, col = iotas(128, 128)
    eyef = (row == col).astype(F32)

    def tnn(name, index, y):
        return tn(kept[at(name, index), :], y, dot3)

    d4 = reach[4, 3] + tnn("a", 4, reach[5, 3]) + tnn("a2", 2, reach[6, 3] + tnn("a", 6, reach[7, 3]))
    pair = {
        3: None,
        2: reach[6, 2] + tnn("a", 6, reach[7, 2]),
        1: d4,
        0: reach[2, 2] + tnn("a", 2, reach[3, 2]) + tnn("a2", 1, d4),
    }
    a4 = kept[at("a4", 1), :]
    suf = {3: eyef, 2: kept[at("a2", 3), :], 1: a4, 0: dot3(a4, kept[at("a2", 1), :])}
    for i in range(4):
        odd = pair[i]
        even = reach[2 * i + 1, 1] if odd is None else reach[2 * i + 1, 1] + tnn("a", 2 * i + 1, odd)
        odd = jnp.zeros((128, 128), F32) if odd is None else odd
        s_odd = suf[i]
        s_even = dot3(s_odd, kept[at("a", 2 * i + 1), :])
        rows = slice(128 * i, 128 * i + 128)
        doc = do[i].astype(F32)
        pd = tn(later[at("p", i), :], held[rows, 0:1] * doc, dot3)
        kk = held[rows, 7:8] * kept[at("kt", i), :]
        left = dot3(kk[0:64], jnp.concatenate([even, s_even.T], 1))
        right = dot3(kk[64:128], jnp.concatenate([odd, s_odd.T], 1))
        hn = jnp.concatenate([left, right], 0)
        both = jnp.concatenate([pd + hn[:, 0:128], hn[:, 128:256]], 1)
        both = held[rows, 10:11] * tn(kept[at("inv", i), :], both, dot3)
        dv_out[rows, :] = both[:, 0:128]
        gmap_out[rows, :] = both[:, 128:256]


def near_body(wh, r1, r2, r3, ups, own, fin, x4, send_out, keep_out):
    y = wh[2]
    up = wh[1] == 1
    a = r2[...].astype(F32)
    b = r3[...].astype(F32)
    second = jnp.where(y == 0, a, b)
    third = jnp.where(y == 0, b, a)
    d01 = second + tn(ups[2], third, dot3)
    d01 = jnp.where(y == 0, tn(ups[1], d01, dot3), jnp.where(y == 1, d01, 0.0))
    part = d01 + jnp.where((y & 1) == 0, r1[...].astype(F32), 0.0)
    trans = own[0:128, :]
    full = part + fin[...]
    pulled = tn(trans, part, dot3) + x4[...]
    send_out[...] = jnp.where(up, pulled, part).astype(BF)
    keep_out[...] = full


def value_body(wh, r, kept, other, dv, gmap, out):
    up = wh[1] == 1
    got = r[...].astype(F32)
    pulled = tn(other[0:128, :].astype(F32), kept[...], dot3)
    g = got + jnp.where(up, kept[...], pulled)
    res = dv[...] + dot3(gmap[...], g)
    out[...] = res.astype(BF).reshape(4, 128, 128)


def project_body(wh, a0, a1, a2, a3, w0, w1, w2, w3, even, odd, held):
    order_weight(wh, (w0, w1, w2, w3), held)
    for n in range(8):
        total = None
        for m, a in enumerate((a0, a1, a2, a3)):
            rows = pl.ds(pl.multiple_of((wh[4] ^ m) * 128, 128), 128)
            w = held[pl.ds(wh[3] ^ n, 1), rows, :][0]
            part = mm(a[...], w)
            total = part if total is None else total + part
        out = odd if n & 1 else even
        out[512 * (n >> 1) : 512 * (n >> 1) + 512, :] = total.astype(BF)


def sum_pair_body(own, r, f_out, o2, o4, o6):
    f_out[...] = own[0:512, :].astype(F32) + r[0:512, :].astype(F32)
    for n, out in ((1, o2), (2, o4), (3, o6)):
        rows = slice(512 * n, 512 * n + 512)
        out[...] = (own[rows, :].astype(F32) + r[rows, :].astype(F32)).astype(BF)


def sum_last_body(wh, f, r2, r4, r6, dq, dv, o0, o1, o2, o3, done):
    total = f[...] + r2[...].astype(F32) + r4[...].astype(F32) + r6[...].astype(F32)
    done[...] = total.astype(BF).reshape(4, 128, 128)
    for m, out in enumerate((o0, o1, o2, o3)):
        for n, part in enumerate((done, dq, dv)):
            out[128 * n : 128 * n + 128, :] = part[pl.ds(wh[0] ^ m, 1)][0]


def place_body(wh, r0, r1, r2, r3, layer, dq, dv):
    for m, r in enumerate((r0, r1, r2, r3)):
        j = wh[4] ^ m
        cols = pl.ds(pl.multiple_of(j * 128, 128), 128)
        layer[:, pl.ds(pl.multiple_of((j ^ (2 * wh[5])) * 128, 128), 128)] = r[0:128, :]
        dq[:, cols] = r[128:256, :]
        dv[:, cols] = r[256:384, :]


def xor(value, axis, mask, name="exchange"):
    with jax.named_scope(name):
        return lax.ppermute(value, axis, [(s, s ^ mask) for s in range(lax.axis_size(axis))])


def own_head(z):
    return (z & 3) ^ (2 * (z >> 2))


def shards(queries, keys, values, log_decay, beta, level_weights, document_ends, out_weight, grad_y, final_state_grad):
    s = lax.axis_index("seq")
    h = lax.axis_index("head")
    z = s & 7
    where = jnp.stack([z & 3, z >> 2, s >> 3, h, own_head(z), h & 1, 0 * h, 0 * h]).astype(jnp.int32)
    packs = call(
        3, pack_body,
        [((544, 128), BF)] * 4,
        [where, document_ends, queries, keys, values, grad_y, log_decay, beta, level_weights],
        [pltpu.VMEM((SCAL, 128), F32)],
        fetch=True,
    )
    mine = [xor(packs[m], "seq", m, "reshard") for m in (1, 2, 3)]
    half = xor(out_weight, "seq", 6, "weight_half")
    w0, own = call(1, join_weight_body, [((1024, 128), BF), ((544, 128), BF)], [out_weight, half, packs[0]])
    weight = [w0] + [xor(w0, "seq", 8 * n, "weight_y") for n in (1, 2, 3)]
    mine = [own] + mine
    gm = call(1, collect_body, [((512, 128), BF)], mine, after=[w0])[0]
    T = (512, 128)
    S = (128, 128)
    ab, abf, kept = call(
        60, block_body,
        [((256, 128), BF), ((256, 128), F32), ((KEPT, 128), F32)],
        [where] + mine,
        [pltpu.VMEM((4, 288, 128), BF)],
        after=[gm],
    )
    other = xor(ab, "seq", 6, "scan_half")
    ga = [gm] + [xor(gm, "head", 2 * n, "grad_y_x") for n in (1, 2, 3)]
    gj = call(1, join_body, [((2048, 128), BF)], ga, after=[ab] + weight[1:])[0]
    gb = xor(gj, "head", 1, "grad_y_core")
    back = call(3, back_product_body, [(T, F32), (T, BF), (T, BF), (T, BF)], [where, gj, gb] + weight, [pltpu.VMEM((8, 512, 128), BF)])
    pair_bf, pair_f, omap = call(
        1, pair_body, [((256, 128), BF), ((256, 128), F32), ((256, 128), F32)], [where, abf, other], after=[back[1]]
    )
    far = [xor(pair_bf, "seq", 8 * n, "scan_y") for n in (1, 2, 3)]
    held, later = call(
        4, query_body,
        [((1536, 128), F32), ((KEPT_LATER, 128), F32)],
        [where] + mine + [kept],
        [pltpu.VMEM((4, SCAL, 128), BF), pltpu.VMEM((4,) + S, BF)],
        after=[pair_bf],
    )
    attn, far_states, ups, fin = call(
        2, far_body,
        [(T, BF), ((128, 384), F32), ((4,) + S, F32), (S, F32)],
        [where, pair_f] + far + [omap, held, final_state_grad],
        [pltpu.VMEM((4, 256, 128), F32)],
    )
    rb = [xor(back[m], "seq", m, "grad_attn") for m in (1, 2, 3)]
    do, z5, z6, x4 = call(
        2, reach_body, [((4,) + S, BF), (S, BF), (S, BF), (S, F32)], [where, back[0]] + rb + [held, omap], after=[attn]
    )
    near = [xor(z5, "seq", 8, "back_y"), xor(z6, "seq", 16, "back_y"), xor(z6, "seq", 24, "back_y")]
    send, local = call(1, near_body, [(S, BF), (S, F32)], [where] + near + [ups, abf, fin, x4])
    got = xor(send, "seq", 6, "back_half")

    at = [attn] + [xor(attn, "seq", m, "attn") for m in (1, 2, 3)]
    even, odd = call(3, project_body, [((2048, 128), BF)] * 2, [where] + at + weight, [pltpu.VMEM((8, 512, 128), BF)], after=[send])
    swapped = xor(odd, "head", 1, "out_core")
    sums = call(1, sum_pair_body, [(T, F32), (T, BF), (T, BF), (T, BF)], [even, swapped], after=[got])
    rx = [xor(sums[n], "head", 2 * n, "out_x") for n in (1, 2, 3)]
    dq, dv_part, gmap = call(
        4, grad_body,
        [((4,) + S, BF), (T, F32), (T, F32)],
        [where, do, held, far_states, kept, later],
        after=[sums[1]],
    )
    dv = call(1, value_body, [((4,) + S, BF)], [where, got, local, other, dv_part, gmap])[0]
    parts = call(
        1, sum_last_body, [((384, 128), BF)] * 4, [where, sums[0]] + rx + [dq, dv], [pltpu.VMEM((4,) + S, BF)]
    )
    home = [parts[0]] + [xor(parts[m], "seq", m, "home") for m in (1, 2, 3)]
    return tuple(call(1, place_body, [((128, 512), BF)] * 3, [where] + home))


def solution(mesh):
    in_specs = (
        P("seq", "head"),
        P("seq", "head"),
        P("seq", "head"),
        P("head", "seq"),
        P("head", "seq"),
        P(None, "head", "seq"),
        P("seq"),
        P("head", "seq"),
        P("seq", "head"),
        P("head", None, None),
    )
    out_specs = (P("seq", "head"), P("seq", "head"), P("seq", "head"))
    return jax.shard_map(shards, mesh=mesh, in_specs=in_specs, out_specs=out_specs, check_vma=False)
```

time: 131 us -> 120 us (0.916); the launches traced: 128 us -> 120 us
  starting transfers between devices: 54.1 us -> 49.2 us
  waiting for transfers between devices: 38.8 us -> 35.7 us
  Pallas kernels: 32.8 us -> 31.2 us
  local copies, waits for them, and re-layouts: 1.55 us -> 2.97 us
    ppermute x35 -> x32, starting transfers between devices: 54.1 us -> 49.2 us  [xor(): lax.ppermute(value, axis, [(s, s ^ mask) for s in range(lax.axis_size(axi...]
    ppermute x35 -> x32, waiting for transfers between devices: 38.8 us -> 35.7 us  [xor(): lax.ppermute(value, axis, [(s, s ^ mask) for s in range(lax.axis_size(axi...]
    pallas_call x17, Pallas kernels: 32.8 us -> 31.2 us  [call(): pl.pallas_call(waiting, out_shape=[jax.ShapeDtypeStruct(s, d) for s, d in...]
    unnamed x8 -> x10, local copies, waits for them, and re-layouts: 0.92 us -> 2.39 us
  transfers between devices with their start and end apart: 35 -> 32, of which waited for: 14 -> 12; matrix products, arithmetic and copies ran while one was open for 0% -> 0% of each run, Pallas kernels for 16% -> 22%
where the time goes in v1:
time: 120 us
  starting transfers between devices  49.2 us (41%)
  waiting for transfers between devices  35.7 us (30%)
  Pallas kernels  31.2 us (26%)
  local copies, waits for them, and re-layouts  2.97 us (2%)
    ppermute x32, starting transfers between devices, xor(): lax.ppermute(value, axis, [(s, s ^ mask) for s in range(lax.axis_size(axi...  49.2 us
    ppermute x32, waiting for transfers between devices, xor(): lax.ppermute(value, axis, [(s, s ^ mask) for s in range(lax.axis_size(axi...  35.7 us
    pallas_call x17, Pallas kernels, call(): pl.pallas_call(waiting, out_shape=[jax.ShapeDtypeStruct(s, d) for s, d in...  31.2 us
  transfers between devices with their start and end apart: 32, of which 12 were waited for; matrix products, arithmetic and copies ran while one was open for 0% of the time, Pallas kernels for 22%

profile of v1, /device:TPU:32, one launch (start us, length us, event | category | flops | bytes accessed | tf_op | source)
XLA Modules:
  0.0 120.0 jit_solution(17108130756690723314)
XLA Ops:
  0.6 5.5 %collective-permute-start = (bf16[512,128]{1,0:T(8,128)(2,1)}, bf16[512,128]{1,0:T(8,128)(2,1)S(1)}, u32[]{:S(2)}, u32[]{:S(2)}) collective-permute-start(bf16[512,128]{1,0:T(8,128)(2,1)} %refs_0_.1), channel_id=1, source_target_pairs={{0,48},{8,56},{16,32},{24,40},{32,16},{40,24},{48,0},{56,8},{64,11... | collective-permute-start | bytes 393224 | tf_op jit(solution)/shard_map/weight_half/ppermute | solution.py:524
  6.7 2.7 %pack.1 = (bf16[544,128]{1,0:T(8,128)(2,1)}, bf16[544,128]{1,0:T(8,128)(2,1)}, bf16[544,128]{1,0:T(8,128)(2,1)}, bf16[544,128]{1,0:T(8,128)(2,1)}) custom-call(s32[8]{0:T(128)} %stack.27.refs_0_, s32[2]{0:T(128)} %refs_1_.1, bf16[128,512]{1,0:T(8,128)(2,1)} %refs_2_.1, bf16[128,512]{1,0:T(8,128)(2,1)} %refs_3_.1, bf16[128,512]{1,0:T(8,128)(2,1)} %refs_4_.1, ...), custom_call_target="tpu_custom_call" | custom-call | flops 300000000 | tf_op jit(solution)/shard_map/pack/pallas_call | solution.py:105
  9.4 1.1 collective-permute-start.1
  10.5 1.5 %collective-permute-start.2 = (bf16[544,128]{1,0:T(8,128)(2,1)}, bf16[544,128]{1,0:T(8,128)(2,1)S(1)}, u32[]{:S(2)}, u32[]{:S(2)}) collective-permute-start(bf16[544,128]{1,0:T(8,128)(2,1)} %get-tuple-element.47), channel_id=1, source_target_pairs={{0,16},{8,24},{16,0},{24,8},{32,48},{40,56},{48,32},{56,40},{64,80... | collective-permute-start | bytes 417800 | tf_op jit(solution)/shard_map/reshard/ppermute | solution.py:524
  12.0 1.0 collective-permute-start.3
  13.0 0.9 copy-done.1
  13.9 0.9 copy-done.2
  14.8 1.5 %collective-permute-done.1.refs_1_.refs_2_ = bf16[544,128]{1,0:T(8,128)(2,1)S(1)} collective-permute-done((bf16[544,128]{1,0:T(8,128)(2,1)}, bf16[544,128]{1,0:T(8,128)(2,1)S(1)}, u32[]{:S(2)}, u32[]{:S(2)}) %collective-permute-start.1) | collective-permute-done | bytes 139296 | tf_op jit(solution)/shard_map/reshard/ppermute | solution.py:524
  16.3 5.8 %collective-permute-done.2.refs_2_.refs_3_ = bf16[544,128]{1,0:T(8,128)(2,1)S(1)} collective-permute-done((bf16[544,128]{1,0:T(8,128)(2,1)}, bf16[544,128]{1,0:T(8,128)(2,1)S(1)}, u32[]{:S(2)}, u32[]{:S(2)}) %collective-permute-start.2) | collective-permute-done | bytes 139296 | tf_op jit(solution)/shard_map/reshard/ppermute | solution.py:524
  22.2 2.9 %collective-permute-done.3.refs_3_.refs_4_ = bf16[544,128]{1,0:T(8,128)(2,1)S(1)} collective-permute-done((bf16[544,128]{1,0:T(8,128)(2,1)}, bf16[544,128]{1,0:T(8,128)(2,1)S(1)}, u32[]{:S(2)}, u32[]{:S(2)}) %collective-permute-start.3) | collective-permute-done | bytes 139296 | tf_op jit(solution)/shard_map/reshard/ppermute | solution.py:524
  25.0 1.6 %collective-permute-start.5 = (bf16[512,128]{1,0:T(8,128)(2,1)S(1)}, bf16[512,128]{1,0:T(8,128)(2,1)S(1)}, u32[]{:S(2)}, u32[]{:S(2)}) collective-permute-start(bf16[512,128]{1,0:T(8,128)(2,1)S(1)} %collect.1.refs_5_.refs_0_), channel_id=1, source_target_pairs={{0,2},{1,3},{2,0},{3,1},{4,6},{5,7},{6,4},{7,5},{8,10},{9,11},{10,... | collective-permute-start | bytes 393224 | tf_op jit(solution)/shard_map/grad_y_x/ppermute | solution.py:524
  26.6 3.0 %collective-permute-start.10 = (bf16[1024,128]{1,0:T(8,128)(2,1)S(1)}, bf16[1024,128]{1,0:T(8,128)(2,1)S(1)}, u32[]{:S(2)}, u32[]{:S(2)}) collective-permute-start(bf16[1024,128]{1,0:T(8,128)(2,1)S(1)} %get-tuple-element.49.refs_4_.refs_3_.refs_5_), channel_id=1, source_target_pairs={{0,192},{8,200},{16,208},{24,216},{32,224},{40,232},{48,240},{56,2... | collective-permute-start | bytes 786440 | tf_op jit(solution)/shard_map/weight_y/ppermute | solution.py:524
  29.8 1.5 %collective-permute-start.9 = (bf16[1024,128]{1,0:T(8,128)(2,1)S(1)}, bf16[1024,128]{1,0:T(8,128)(2,1)S(1)}, u32[]{:S(2)}, u32[]{:S(2)}) collective-permute-start(bf16[1024,128]{1,0:T(8,128)(2,1)S(1)} %get-tuple-element.49.refs_4_.refs_3_.refs_5_), channel_id=1, source_target_pairs={{0,128},{8,136},{16,144},{24,152},{32,160},{40,168},{48,176},{56,1... | collective-permute-start | bytes 786440 | tf_op jit(solution)/shard_map/weight_y/ppermute | solution.py:524
  31.3 2.7 %collective-permute-start.6 = (bf16[512,128]{1,0:T(8,128)(2,1)S(1)}, bf16[512,128]{1,0:T(8,128)(2,1)S(1)}, u32[]{:S(2)}, u32[]{:S(2)}) collective-permute-start(bf16[512,128]{1,0:T(8,128)(2,1)S(1)} %collect.1.refs_5_.refs_0_), channel_id=1, source_target_pairs={{0,4},{1,5},{2,6},{3,7},{4,0},{5,1},{6,2},{7,3},{8,12},{9,13},{10,... | collective-permute-start | bytes 393224 | tf_op jit(solution)/shard_map/grad_y_x/ppermute | solution.py:524
  35.1 8.9 %block.1 = (bf16[256,128]{1,0:T(8,128)(2,1)S(1)}, f32[256,128]{1,0:T(8,128)S(1)}, f32[7424,128]{1,0:T(8,128)S(1)}) custom-call(s32[8]{0:T(128)S(1)} %copy-done.3, bf16[544,128]{1,0:T(8,128)(2,1)S(1)} %get-tuple-element.45.refs_0_.refs_1_, bf16[544,128]{1,0:T(8,128)(2,1)S(1)} %collective-permute-done.1.refs_1_.refs_2_, ...), custom_call_target="tpu_custom_call" | custom-call | flops 6000000000 | tf_op jit(solution)/shard_map/block/pallas_call | solution.py:105
  44.3 1.8 %collective-permute-done.11.refs_2_ = bf16[2048,128]{1,0:T(8,128)(2,1)S(1)} collective-permute-done((bf16[2048,128]{1,0:T(8,128)(2,1)S(1)}, bf16[2048,128]{1,0:T(8,128)(2,1)S(1)}, u32[]{:S(2)}, u32[]{:S(2)}) %collective-permute-start.11) | collective-permute-done | bytes 524320 | tf_op jit(solution)/shard_map/grad_y_core/ppermute | solution.py:524
  46.1 2.0 %back_product.1 = (f32[512,128]{1,0:T(8,128)S(1)}, bf16[512,128]{1,0:T(8,128)(2,1)S(1)}, bf16[512,128]{1,0:T(8,128)(2,1)S(1)}, bf16[512,128]{1,0:T(8,128)(2,1)S(1)}) custom-call(s32[8]{0:T(128)S(1)} %copy-done.3, bf16[2048,128]{1,0:T(8,128)(2,1)S(1)} %join.1.refs_1_, bf16[2048,128]{1,0:T(8,128)(2,1)S(1)} %collective-permute-done.11.refs_2_, ...), custom_call_target="tpu_custom_call" | custom-call | flops 300000000 | tf_op jit(solution)/shard_map/back_product/pallas_call | solution.py:105
  48.1 3.5 %collective-permute-done.4.refs_2_.refs_3_ = bf16[256,128]{1,0:T(8,128)(2,1)S(1)} collective-permute-done((bf16[256,128]{1,0:T(8,128)(2,1)S(1)}, bf16[256,128]{1,0:T(8,128)(2,1)S(1)}, u32[]{:S(2)}, u32[]{:S(2)}) %collective-permute-start.4) | collective-permute-done | bytes 65568 | tf_op jit(solution)/shard_map/scan_half/ppermute | solution.py:524
  51.7 0.7 pair.1
  52.4 1.2 %collective-permute-start.12 = (bf16[256,128]{1,0:T(8,128)(2,1)S(1)}, bf16[256,128]{1,0:T(8,128)(2,1)S(1)}, u32[]{:S(2)}, u32[]{:S(2)}) collective-permute-start(bf16[256,128]{1,0:T(8,128)(2,1)S(1)} %get-tuple-element.54.refs_6_), channel_id=1, source_target_pairs={{0,64},{8,72},{16,80},{24,88},{32,96},{40,104},{48,112},{56,120},{... | collective-permute-start | bytes 196616 | tf_op jit(solution)/shard_map/scan_y/ppermute | solution.py:524
  53.6 2.4 %collective-permute-start.19 = (bf16[512,128]{1,0:T(8,128)(2,1)S(1)}, bf16[512,128]{1,0:T(8,128)(2,1)S(1)}, u32[]{:S(2)}, u32[]{:S(2)}) collective-permute-start(bf16[512,128]{1,0:T(8,128)(2,1)S(1)} %get-tuple-element.60), channel_id=1, source_target_pairs={{0,16},{8,24},{16,0},{24,8},{32,48},{40,56},{48,32},{56,40},{64,80... | collective-permute-start | bytes 393224 | tf_op jit(solution)/shard_map/grad_attn/ppermute | solution.py:524
  56.1 1.1 collective-permute-start.20
  57.1 3.5 %collective-permute-start.13 = (bf16[256,128]{1,0:T(8,128)(2,1)S(1)}, bf16[256,128]{1,0:T(8,128)(2,1)S(1)}, u32[]{:S(2)}, u32[]{:S(2)}) collective-permute-start(bf16[256,128]{1,0:T(8,128)(2,1)S(1)} %get-tuple-element.54.refs_6_), channel_id=1, source_target_pairs={{0,128},{8,136},{16,144},{24,152},{32,160},{40,168},{48,176},{56,1... | collective-permute-start | bytes 196616 | tf_op jit(solution)/shard_map/scan_y/ppermute | solution.py:524
  60.9 2.4 %query.1 = (f32[1536,128]{1,0:T(8,128)S(1)}, f32[1536,128]{1,0:T(8,128)S(1)}) custom-call(s32[8]{0:T(128)S(1)} %copy-done.4, bf16[544,128]{1,0:T(8,128)(2,1)S(1)} %get-tuple-element.45.refs_0_.refs_1_, bf16[544,128]{1,0:T(8,128)(2,1)S(1)} %collective-permute-done.1.refs_1_.refs_2_, bf16[544,128]{1,0:T(8,128)(2,1)S(1)} %collective-permute-done.2.refs_2_.refs_3_, ...), custom_call_target="tpu_custom_call" | custom-call | flops 400000000 | tf_op jit(solution)/shard_map/query/pallas_call | solution.py:105
  63.2 2.9 %collective-permute-done.14.refs_4_ = bf16[256,128]{1,0:T(8,128)(2,1)S(1)} collective-permute-done((bf16[256,128]{1,0:T(8,128)(2,1)S(1)}, bf16[256,128]{1,0:T(8,128)(2,1)S(1)}, u32[]{:S(2)}, u32[]{:S(2)}) %collective-permute-start.14) | collective-permute-done | bytes 65568 | tf_op jit(solution)/shard_map/scan_y/ppermute | solution.py:524
  66.1 1.9 %far.1 = (bf16[512,128]{1,0:T(8,128)(2,1)S(1)}, f32[128,384]{1,0:T(8,128)S(1)}, f32[4,128,128]{2,1,0:T(8,128)S(1)}, f32[128,128]{1,0:T(8,128)S(1)}) custom-call(s32[8]{0:T(128)S(1)} %copy-done.4, f32[256,128]{1,0:T(8,128)S(1)} %get-tuple-element.53.refs_1_, bf16[256,128]{1,0:T(8,128)(2,1)S(1)} %collective-permute-done.12.refs_2_, ...), custom_call_target="tpu_custom_call" | custom-call | flops 200000000 | tf_op jit(solution)/shard_map/far/pallas_call | solution.py:105
  68.0 1.0 collective-permute-start.15
  69.0 1.6 %collective-permute-start.16 = (bf16[512,128]{1,0:T(8,128)(2,1)S(1)}, bf16[512,128]{1,0:T(8,128)(2,1)S(1)}, u32[]{:S(2)}, u32[]{:S(2)}) collective-permute-start(bf16[512,128]{1,0:T(8,128)(2,1)S(1)} %get-tuple-element.58.refs_7_.refs_1_), channel_id=1, source_target_pairs={{0,16},{8,24},{16,0},{24,8},{32,48},{40,56},{48,32},{56,40},{64,80... | collective-permute-start | bytes 393224 | tf_op jit(solution)/shard_map/attn/ppermute | solution.py:524
  70.6 1.0 collective-permute-start.17
  71.6 1.4 %reach.1 = (bf16[4,128,128]{2,1,0:T(8,128)(2,1)S(1)}, bf16[128,128]{1,0:T(8,128)(2,1)S(1)}, bf16[128,128]{1,0:T(8,128)(2,1)S(1)}, f32[128,128]{1,0:T(8,128)S(1)}) custom-call(s32[8]{0:T(128)S(1)} %copy-done.4, f32[512,128]{1,0:T(8,128)S(1)} %get-tuple-element.59.refs_1_, bf16[512,128]{1,0:T(8,128)(2,1)S(1)} %collective-permute-done.18.refs_2_, ...), custom_call_target="tpu_custom_call" | custom-call | flops 200000000 | tf_op jit(solution)/shard_map/reach/pallas_call | solution.py:105
  73.0 1.3 %collective-permute-start.21 = (bf16[128,128]{1,0:T(8,128)(2,1)S(1)}, bf16[128,128]{1,0:T(8,128)(2,1)S(1)}, u32[]{:S(2)}, u32[]{:S(2)}) collective-permute-start(bf16[128,128]{1,0:T(8,128)(2,1)S(1)} %get-tuple-element.62), channel_id=1, source_target_pairs={{0,64},{8,72},{16,80},{24,88},{32,96},{40,104},{48,112},{56,120},{... | collective-permute-start | bytes 98312 | tf_op jit(solution)/shard_map/back_y/ppermute | solution.py:524
  74.3 6.0 %collective-permute-start.22 = (bf16[128,128]{1,0:T(8,128)(2,1)S(1)}, bf16[128,128]{1,0:T(8,128)(2,1)S(1)}, u32[]{:S(2)}, u32[]{:S(2)}) collective-permute-start(bf16[128,128]{1,0:T(8,128)(2,1)S(1)} %get-tuple-element.63), channel_id=1, source_target_pairs={{0,128},{8,136},{16,144},{24,152},{32,160},{40,168},{48,176},{56,1... | collective-permute-start | bytes 98312 | tf_op jit(solution)/shard_map/back_y/ppermute | solution.py:524
  80.4 2.4 %collective-permute-start.23 = (bf16[128,128]{1,0:T(8,128)(2,1)S(1)}, bf16[128,128]{1,0:T(8,128)(2,1)S(1)}, u32[]{:S(2)}, u32[]{:S(2)}) collective-permute-start(bf16[128,128]{1,0:T(8,128)(2,1)S(1)} %get-tuple-element.63), channel_id=1, source_target_pairs={{0,192},{8,200},{16,208},{24,216},{32,224},{40,232},{48,240},{56,2... | collective-permute-start | bytes 98312 | tf_op jit(solution)/shard_map/back_y/ppermute | solution.py:524
  82.7 2.8 %collective-permute-done.23.refs_3_ = bf16[128,128]{1,0:T(8,128)(2,1)S(1)} collective-permute-done((bf16[128,128]{1,0:T(8,128)(2,1)S(1)}, bf16[128,128]{1,0:T(8,128)(2,1)S(1)}, u32[]{:S(2)}, u32[]{:S(2)}) %collective-permute-start.23) | collective-permute-done | bytes 32800 | tf_op jit(solution)/shard_map/back_y/ppermute | solution.py:524
  85.5 1.1 near.1
  86.6 1.9 %project.1 = (bf16[2048,128]{1,0:T(8,128)(2,1)S(1)}, bf16[2048,128]{1,0:T(8,128)(2,1)S(1)}) custom-call(s32[8]{0:T(128)S(1)} %copy-done.4, bf16[512,128]{1,0:T(8,128)(2,1)S(1)} %get-tuple-element.58.refs_7_.refs_1_, bf16[512,128]{1,0:T(8,128)(2,1)S(1)} %collective-permute-done.15.refs_2_, bf16[512,128]{1,0:T(8,128)(2,1)S(1)} %collective-permute-done.16.refs_3_, ...), custom_call_target="tpu_custom_call" | custom-call | flops 300000000 | tf_op jit(solution)/shard_map/project/pallas_call | solution.py:105
  88.7 6.0 %collective-permute-done.25.refs_2_.refs_1_ = bf16[128,128]{1,0:T(8,128)(2,1)S(1)} collective-permute-done((bf16[128,128]{1,0:T(8,128)(2,1)S(1)}, bf16[128,128]{1,0:T(8,128)(2,1)S(1)}, u32[]{:S(2)}, u32[]{:S(2)}) %collective-permute-start.25) | collective-permute-done | bytes 32800 | tf_op jit(solution)/shard_map/back_half/ppermute | solution.py:524
  95.4 3.9 %collective-permute-start.27 = (bf16[512,128]{1,0:T(8,128)(2,1)S(1)}, bf16[512,128]{1,0:T(8,128)(2,1)S(1)}, u32[]{:S(2)}, u32[]{:S(2)}) collective-permute-start(bf16[512,128]{1,0:T(8,128)(2,1)S(1)} %get-tuple-element.72), channel_id=1, source_target_pairs={{0,4},{1,5},{2,6},{3,7},{4,0},{5,1},{6,2},{7,3},{8,12},{9,13},{10,... | collective-permute-start | bytes 393224 | tf_op jit(solution)/shard_map/out_x/ppermute | solution.py:524
  99.8 5.0 %grad.1 = (bf16[4,128,128]{2,1,0:T(8,128)(2,1)S(1)}, f32[512,128]{1,0:T(8,128)S(1)}, f32[512,128]{1,0:T(8,128)S(1)}) custom-call(s32[8]{0:T(128)S(1)} %copy-done.4, bf16[4,128,128]{2,1,0:T(8,128)(2,1)S(1)} %get-tuple-element.74.refs_1_, f32[1536,128]{1,0:T(8,128)S(1)} %get-tuple-element.57.refs_6_.refs_5_.refs_2_, f32[128,384]{1,0:T(8,128)S(1)} %get-tuple-element.75.refs_3_, ...), custom_call_target="tpu_custom_call" | custom-call | flops 400000000 | tf_op jit(solution)/shard_map/grad/pallas_call | solution.py:105
  104.8 1.0 value.1.refs_6_
  105.9 0.8 collective-permute-done.28.refs_4_
  106.7 0.6 sum_last.1
  107.4 2.5 %collective-permute-start.30 = (bf16[384,128]{1,0:T(8,128)(2,1)S(1)}, bf16[384,128]{1,0:T(8,128)(2,1)S(1)}, u32[]{:S(2)}, u32[]{:S(2)}) collective-permute-start(bf16[384,128]{1,0:T(8,128)(2,1)S(1)} %get-tuple-element.83), channel_id=1, source_target_pairs={{0,16},{8,24},{16,0},{24,8},{32,48},{40,56},{48,32},{56,40},{64,80... | collective-permute-start | bytes 294920 | tf_op jit(solution)/shard_map/home/ppermute | solution.py:524
  109.9 1.0 collective-permute-start.31
  110.9 2.3 %collective-permute-done.29.refs_2_ = bf16[384,128]{1,0:T(8,128)(2,1)S(1)} collective-permute-done((bf16[384,128]{1,0:T(8,128)(2,1)S(1)}, bf16[384,128]{1,0:T(8,128)(2,1)S(1)}, u32[]{:S(2)}, u32[]{:S(2)}) %collective-permute-start.29) | collective-permute-done | bytes 98336 | tf_op jit(solution)/shard_map/home/ppermute | solution.py:524
  113.2 2.7 %collective-permute-done.30.refs_3_ = bf16[384,128]{1,0:T(8,128)(2,1)S(1)} collective-permute-done((bf16[384,128]{1,0:T(8,128)(2,1)S(1)}, bf16[384,128]{1,0:T(8,128)(2,1)S(1)}, u32[]{:S(2)}, u32[]{:S(2)}) %collective-permute-start.30) | collective-permute-done | bytes 98336 | tf_op jit(solution)/shard_map/home/ppermute | solution.py:524
  115.9 2.7 %collective-permute-done.31.refs_4_ = bf16[384,128]{1,0:T(8,128)(2,1)S(1)} collective-permute-done((bf16[384,128]{1,0:T(8,128)(2,1)S(1)}, bf16[384,128]{1,0:T(8,128)(2,1)S(1)}, u32[]{:S(2)}, u32[]{:S(2)}) %collective-permute-start.31) | collective-permute-done | bytes 98336 | tf_op jit(solution)/shard_map/home/ppermute | solution.py:524
  118.6 1.4 %place.1 = (bf16[128,512]{1,0:T(8,128)(2,1)}, bf16[128,512]{1,0:T(8,128)(2,1)}, bf16[128,512]{1,0:T(8,128)(2,1)}) custom-call(s32[8]{0:T(128)S(1)} %copy-done.4, bf16[384,128]{1,0:T(8,128)(2,1)S(1)} %get-tuple-element.81.refs_1_, bf16[384,128]{1,0:T(8,128)(2,1)S(1)} %collective-permute-done.29.refs_2_, bf16[384,128]{1,0:T(8,128)(2,1)S(1)} %collective-permute-done.30.refs_3_, ...), custom_call_target="tpu_custom_call" | custom-call | flops 100000000 | tf_op jit(solution)/shard_map/place/pallas_call | solution.py:105
  (45 shorter events, 3.8 us)
Async XLA Ops:
  0.6 12.4 %collective-permute-start = (bf16[512,128]{1,0:T(8,128)(2,1)}, bf16[512,128]{1,0:T(8,128)(2,1)S(1)}, u32[]{:S(2)}, u32[]{:S(2)}) collective-permute-start(bf16[512,128]{1,0:T(8,128)(2,1)} %refs_0_.1), channel_id=1, source_target_pairs={{0,48},{8,56},{16,32},{24,40},{32,16},{40,24},{48,0},{56,8},{64,11... | collective-permute-start | bytes 393224 | tf_op jit(solution)/shard_map/weight_half/ppermute | solution.py:524
  9.4 6.9 %collective-permute-start.1 = (bf16[544,128]{1,0:T(8,128)(2,1)}, bf16[544,128]{1,0:T(8,128)(2,1)S(1)}, u32[]{:S(2)}, u32[]{:S(2)}) collective-permute-start(bf16[544,128]{1,0:T(8,128)(2,1)} %get-tuple-element.46), channel_id=1, source_target_pairs={{0,8},{8,0},{16,24},{24,16},{32,40},{40,32},{48,56},{56,48},{64,72... | collective-permute-start | bytes 417800 | tf_op jit(solution)/shard_map/reshard/ppermute | solution.py:524
  10.5 11.6 %collective-permute-start.2 = (bf16[544,128]{1,0:T(8,128)(2,1)}, bf16[544,128]{1,0:T(8,128)(2,1)S(1)}, u32[]{:S(2)}, u32[]{:S(2)}) collective-permute-start(bf16[544,128]{1,0:T(8,128)(2,1)} %get-tuple-element.47), channel_id=1, source_target_pairs={{0,16},{8,24},{16,0},{24,8},{32,48},{40,56},{48,32},{56,40},{64,80... | collective-permute-start | bytes 417800 | tf_op jit(solution)/shard_map/reshard/ppermute | solution.py:524
  12.0 13.1 %collective-permute-start.3 = (bf16[544,128]{1,0:T(8,128)(2,1)}, bf16[544,128]{1,0:T(8,128)(2,1)S(1)}, u32[]{:S(2)}, u32[]{:S(2)}) collective-permute-start(bf16[544,128]{1,0:T(8,128)(2,1)} %get-tuple-element.48), channel_id=1, source_target_pairs={{0,24},{8,16},{16,8},{24,0},{32,56},{40,48},{48,40},{56,32},{64,88... | collective-permute-start | bytes 417800 | tf_op jit(solution)/shard_map/reshard/ppermute | solution.py:524
  13.0 0.9 copy-start.1
  13.9 0.9 copy-start.2
  25.0 9.0 %collective-permute-start.5 = (bf16[512,128]{1,0:T(8,128)(2,1)S(1)}, bf16[512,128]{1,0:T(8,128)(2,1)S(1)}, u32[]{:S(2)}, u32[]{:S(2)}) collective-permute-start(bf16[512,128]{1,0:T(8,128)(2,1)S(1)} %collect.1.refs_5_.refs_0_), channel_id=1, source_target_pairs={{0,2},{1,3},{2,0},{3,1},{4,6},{5,7},{6,4},{7,5},{8,10},{9,11},{10,... | collective-permute-start | bytes 393224 | tf_op jit(solution)/shard_map/grad_y_x/ppermute | solution.py:524
  26.6 17.4 %collective-permute-start.10 = (bf16[1024,128]{1,0:T(8,128)(2,1)S(1)}, bf16[1024,128]{1,0:T(8,128)(2,1)S(1)}, u32[]{:S(2)}, u32[]{:S(2)}) collective-permute-start(bf16[1024,128]{1,0:T(8,128)(2,1)S(1)} %get-tuple-element.49.refs_4_.refs_3_.refs_5_), channel_id=1, source_target_pairs={{0,192},{8,200},{16,208},{24,216},{32,224},{40,232},{48,240},{56,2... | collective-permute-start | bytes 786440 | tf_op jit(solution)/shard_map/weight_y/ppermute | solution.py:524
  29.6 14.4 %collective-permute-start.8 = (bf16[1024,128]{1,0:T(8,128)(2,1)S(1)}, bf16[1024,128]{1,0:T(8,128)(2,1)S(1)}, u32[]{:S(2)}, u32[]{:S(2)}) collective-permute-start(bf16[1024,128]{1,0:T(8,128)(2,1)S(1)} %get-tuple-element.49.refs_4_.refs_3_.refs_5_), channel_id=1, source_target_pairs={{0,64},{8,72},{16,80},{24,88},{32,96},{40,104},{48,112},{56,120},{... | collective-permute-start | bytes 786440 | tf_op jit(solution)/shard_map/weight_y/ppermute | solution.py:524
  29.8 14.3 %collective-permute-start.9 = (bf16[1024,128]{1,0:T(8,128)(2,1)S(1)}, bf16[1024,128]{1,0:T(8,128)(2,1)S(1)}, u32[]{:S(2)}, u32[]{:S(2)}) collective-permute-start(bf16[1024,128]{1,0:T(8,128)(2,1)S(1)} %get-tuple-element.49.refs_4_.refs_3_.refs_5_), channel_id=1, source_target_pairs={{0,128},{8,136},{16,144},{24,152},{32,160},{40,168},{48,176},{56,1... | collective-permute-start | bytes 786440 | tf_op jit(solution)/shard_map/weight_y/ppermute | solution.py:524
  31.3 12.7 %collective-permute-start.6 = (bf16[512,128]{1,0:T(8,128)(2,1)S(1)}, bf16[512,128]{1,0:T(8,128)(2,1)S(1)}, u32[]{:S(2)}, u32[]{:S(2)}) collective-permute-start(bf16[512,128]{1,0:T(8,128)(2,1)S(1)} %collect.1.refs_5_.refs_0_), channel_id=1, source_target_pairs={{0,4},{1,5},{2,6},{3,7},{4,0},{5,1},{6,2},{7,3},{8,12},{9,13},{10,... | collective-permute-start | bytes 393224 | tf_op jit(solution)/shard_map/grad_y_x/ppermute | solution.py:524
  34.1 10.0 %collective-permute-start.7 = (bf16[512,128]{1,0:T(8,128)(2,1)S(1)}, bf16[512,128]{1,0:T(8,128)(2,1)S(1)}, u32[]{:S(2)}, u32[]{:S(2)}) collective-permute-start(bf16[512,128]{1,0:T(8,128)(2,1)S(1)} %collect.1.refs_5_.refs_0_), channel_id=1, source_target_pairs={{0,6},{1,7},{2,4},{3,5},{4,2},{5,3},{6,0},{7,1},{8,14},{9,15},{10,... | collective-permute-start | bytes 393224 | tf_op jit(solution)/shard_map/grad_y_x/ppermute | solution.py:524
  34.5 0.6 copy-start.3
  44.0 16.9 %copy-start.4 = (s32[8]{0:T(128)S(1)}, s32[8]{0:T(128)}, u32[]{:S(2)}) copy-start(s32[8]{0:T(128)} %stack.27.refs_0_) | copy-start | bytes 100
  44.1 22.0 %copy-start = (f32[4,128,128]{2,1,0:T(8,128)S(1)}, f32[4,128,128]{2,1,0:T(8,128)}, u32[]{:S(2)}) copy-start(f32[4,128,128]{2,1,0:T(8,128)} %refs_7_.3) | copy-start | bytes 786436
  44.1 2.0 %collective-permute-start.11 = (bf16[2048,128]{1,0:T(8,128)(2,1)S(1)}, bf16[2048,128]{1,0:T(8,128)(2,1)S(1)}, u32[]{:S(2)}, u32[]{:S(2)}) collective-permute-start(bf16[2048,128]{1,0:T(8,128)(2,1)S(1)} %join.1.refs_1_), channel_id=1, source_target_pairs={{0,1},{1,0},{2,3},{3,2},{4,5},{5,4},{6,7},{7,6},{8,9},{9,8},{10,11... | collective-permute-start | bytes 1572872 | tf_op jit(solution)/shard_map/grad_y_core/ppermute | solution.py:524
  44.2 7.4 %collective-permute-start.4 = (bf16[256,128]{1,0:T(8,128)(2,1)S(1)}, bf16[256,128]{1,0:T(8,128)(2,1)S(1)}, u32[]{:S(2)}, u32[]{:S(2)}) collective-permute-start(bf16[256,128]{1,0:T(8,128)(2,1)S(1)} %get-tuple-element.51.refs_4_), channel_id=1, source_target_pairs={{0,48},{8,56},{16,32},{24,40},{32,16},{40,24},{48,0},{56,8},{64,11... | collective-permute-start | bytes 196616 | tf_op jit(solution)/shard_map/scan_half/ppermute | solution.py:524
  52.4 8.2 %collective-permute-start.12 = (bf16[256,128]{1,0:T(8,128)(2,1)S(1)}, bf16[256,128]{1,0:T(8,128)(2,1)S(1)}, u32[]{:S(2)}, u32[]{:S(2)}) collective-permute-start(bf16[256,128]{1,0:T(8,128)(2,1)S(1)} %get-tuple-element.54.refs_6_), channel_id=1, source_target_pairs={{0,64},{8,72},{16,80},{24,88},{32,96},{40,104},{48,112},{56,120},{... | collective-permute-start | bytes 196616 | tf_op jit(solution)/shard_map/scan_y/ppermute | solution.py:524
  53.6 16.9 %collective-permute-start.18 = (bf16[512,128]{1,0:T(8,128)(2,1)S(1)}, bf16[512,128]{1,0:T(8,128)(2,1)S(1)}, u32[]{:S(2)}, u32[]{:S(2)}) collective-permute-start(bf16[512,128]{1,0:T(8,128)(2,1)S(1)} %get-tuple-element.52.refs_3_), channel_id=1, source_target_pairs={{0,8},{8,0},{16,24},{24,16},{32,40},{40,32},{48,56},{56,48},{64,72... | collective-permute-start | bytes 393224 | tf_op jit(solution)/shard_map/grad_attn/ppermute | solution.py:524
  53.6 18.0 %collective-permute-start.19 = (bf16[512,128]{1,0:T(8,128)(2,1)S(1)}, bf16[512,128]{1,0:T(8,128)(2,1)S(1)}, u32[]{:S(2)}, u32[]{:S(2)}) collective-permute-start(bf16[512,128]{1,0:T(8,128)(2,1)S(1)} %get-tuple-element.60), channel_id=1, source_target_pairs={{0,16},{8,24},{16,0},{24,8},{32,48},{40,56},{48,32},{56,40},{64,80... | collective-permute-start | bytes 393224 | tf_op jit(solution)/shard_map/grad_attn/ppermute | solution.py:524
  56.1 15.5 %collective-permute-start.20 = (bf16[512,128]{1,0:T(8,128)(2,1)S(1)}, bf16[512,128]{1,0:T(8,128)(2,1)S(1)}, u32[]{:S(2)}, u32[]{:S(2)}) collective-permute-start(bf16[512,128]{1,0:T(8,128)(2,1)S(1)} %get-tuple-element.61), channel_id=1, source_target_pairs={{0,24},{8,16},{16,8},{24,0},{32,56},{40,48},{48,40},{56,32},{64,88... | collective-permute-start | bytes 393224 | tf_op jit(solution)/shard_map/grad_attn/ppermute | solution.py:524
  57.1 6.1 %collective-permute-start.13 = (bf16[256,128]{1,0:T(8,128)(2,1)S(1)}, bf16[256,128]{1,0:T(8,128)(2,1)S(1)}, u32[]{:S(2)}, u32[]{:S(2)}) collective-permute-start(bf16[256,128]{1,0:T(8,128)(2,1)S(1)} %get-tuple-element.54.refs_6_), channel_id=1, source_target_pairs={{0,128},{8,136},{16,144},{24,152},{32,160},{40,168},{48,176},{56,1... | collective-permute-start | bytes 196616 | tf_op jit(solution)/shard_map/scan_y/ppermute | solution.py:524
  60.6 5.5 %collective-permute-start.14 = (bf16[256,128]{1,0:T(8,128)(2,1)S(1)}, bf16[256,128]{1,0:T(8,128)(2,1)S(1)}, u32[]{:S(2)}, u32[]{:S(2)}) collective-permute-start(bf16[256,128]{1,0:T(8,128)(2,1)S(1)} %get-tuple-element.54.refs_6_), channel_id=1, source_target_pairs={{0,192},{8,200},{16,208},{24,216},{32,224},{40,232},{48,240},{56,2... | collective-permute-start | bytes 196616 | tf_op jit(solution)/shard_map/scan_y/ppermute | solution.py:524
  68.0 18.5 %collective-permute-start.15 = (bf16[512,128]{1,0:T(8,128)(2,1)S(1)}, bf16[512,128]{1,0:T(8,128)(2,1)S(1)}, u32[]{:S(2)}, u32[]{:S(2)}) collective-permute-start(bf16[512,128]{1,0:T(8,128)(2,1)S(1)} %get-tuple-element.58.refs_7_.refs_1_), channel_id=1, source_target_pairs={{0,8},{8,0},{16,24},{24,16},{32,40},{40,32},{48,56},{56,48},{64,72... | collective-permute-start | bytes 393224 | tf_op jit(solution)/shard_map/attn/ppermute | solution.py:524
  69.0 17.6 %collective-permute-start.16 = (bf16[512,128]{1,0:T(8,128)(2,1)S(1)}, bf16[512,128]{1,0:T(8,128)(2,1)S(1)}, u32[]{:S(2)}, u32[]{:S(2)}) collective-permute-start(bf16[512,128]{1,0:T(8,128)(2,1)S(1)} %get-tuple-element.58.refs_7_.refs_1_), channel_id=1, source_target_pairs={{0,16},{8,24},{16,0},{24,8},{32,48},{40,56},{48,32},{56,40},{64,80... | collective-permute-start | bytes 393224 | tf_op jit(solution)/shard_map/attn/ppermute | solution.py:524
  70.6 16.0 %collective-permute-start.17 = (bf16[512,128]{1,0:T(8,128)(2,1)S(1)}, bf16[512,128]{1,0:T(8,128)(2,1)S(1)}, u32[]{:S(2)}, u32[]{:S(2)}) collective-permute-start(bf16[512,128]{1,0:T(8,128)(2,1)S(1)} %get-tuple-element.58.refs_7_.refs_1_), channel_id=1, source_target_pairs={{0,24},{8,16},{16,8},{24,0},{32,56},{40,48},{48,40},{56,32},{64,88... | collective-permute-start | bytes 393224 | tf_op jit(solution)/shard_map/attn/ppermute | solution.py:524
  73.0 7.3 %collective-permute-start.21 = (bf16[128,128]{1,0:T(8,128)(2,1)S(1)}, bf16[128,128]{1,0:T(8,128)(2,1)S(1)}, u32[]{:S(2)}, u32[]{:S(2)}) collective-permute-start(bf16[128,128]{1,0:T(8,128)(2,1)S(1)} %get-tuple-element.62), channel_id=1, source_target_pairs={{0,64},{8,72},{16,80},{24,88},{32,96},{40,104},{48,112},{56,120},{... | collective-permute-start | bytes 98312 | tf_op jit(solution)/shard_map/back_y/ppermute | solution.py:524
  74.3 8.4 %collective-permute-start.22 = (bf16[128,128]{1,0:T(8,128)(2,1)S(1)}, bf16[128,128]{1,0:T(8,128)(2,1)S(1)}, u32[]{:S(2)}, u32[]{:S(2)}) collective-permute-start(bf16[128,128]{1,0:T(8,128)(2,1)S(1)} %get-tuple-element.63), channel_id=1, source_target_pairs={{0,128},{8,136},{16,144},{24,152},{32,160},{40,168},{48,176},{56,1... | collective-permute-start | bytes 98312 | tf_op jit(solution)/shard_map/back_y/ppermute | solution.py:524
  80.4 5.1 %collective-permute-start.23 = (bf16[128,128]{1,0:T(8,128)(2,1)S(1)}, bf16[128,128]{1,0:T(8,128)(2,1)S(1)}, u32[]{:S(2)}, u32[]{:S(2)}) collective-permute-start(bf16[128,128]{1,0:T(8,128)(2,1)S(1)} %get-tuple-element.63), channel_id=1, source_target_pairs={{0,192},{8,200},{16,208},{24,216},{32,224},{40,232},{48,240},{56,2... | collective-permute-start | bytes 98312 | tf_op jit(solution)/shard_map/back_y/ppermute | solution.py:524
  88.5 6.2 %collective-permute-start.24 = (bf16[2048,128]{1,0:T(8,128)(2,1)S(1)}, bf16[2048,128]{1,0:T(8,128)(2,1)S(1)}, u32[]{:S(2)}, u32[]{:S(2)}) collective-permute-start(bf16[2048,128]{1,0:T(8,128)(2,1)S(1)} %get-tuple-element.69), channel_id=1, source_target_pairs={{0,1},{1,0},{2,3},{3,2},{4,5},{5,4},{6,7},{7,6},{8,9},{9,8},{10,11... | collective-permute-start | bytes 1572872 | tf_op jit(solution)/shard_map/out_core/ppermute | solution.py:524
  88.6 6.1 %collective-permute-start.25 = (bf16[128,128]{1,0:T(8,128)(2,1)S(1)}, bf16[128,128]{1,0:T(8,128)(2,1)S(1)}, u32[]{:S(2)}, u32[]{:S(2)}) collective-permute-start(bf16[128,128]{1,0:T(8,128)(2,1)S(1)} %get-tuple-element.67.refs_9_), channel_id=1, source_target_pairs={{0,48},{8,56},{16,32},{24,40},{32,16},{40,24},{48,0},{56,8},{64,11... | collective-permute-start | bytes 98312 | tf_op jit(solution)/shard_map/back_half/ppermute | solution.py:524
  94.8 11.0 %collective-permute-start.26 = (bf16[512,128]{1,0:T(8,128)(2,1)S(1)}, bf16[512,128]{1,0:T(8,128)(2,1)S(1)}, u32[]{:S(2)}, u32[]{:S(2)}) collective-permute-start(bf16[512,128]{1,0:T(8,128)(2,1)S(1)} %get-tuple-element.71.refs_6_), channel_id=1, source_target_pairs={{0,2},{1,3},{2,0},{3,1},{4,6},{5,7},{6,4},{7,5},{8,10},{9,11},{10,... | collective-permute-start | bytes 393224 | tf_op jit(solution)/shard_map/out_x/ppermute | solution.py:524
  95.4 10.5 %collective-permute-start.27 = (bf16[512,128]{1,0:T(8,128)(2,1)S(1)}, bf16[512,128]{1,0:T(8,128)(2,1)S(1)}, u32[]{:S(2)}, u32[]{:S(2)}) collective-permute-start(bf16[512,128]{1,0:T(8,128)(2,1)S(1)} %get-tuple-element.72), channel_id=1, source_target_pairs={{0,4},{1,5},{2,6},{3,7},{4,0},{5,1},{6,2},{7,3},{8,12},{9,13},{10,... | collective-permute-start | bytes 393224 | tf_op jit(solution)/shard_map/out_x/ppermute | solution.py:524
  99.3 7.3 %collective-permute-start.28 = (bf16[512,128]{1,0:T(8,128)(2,1)S(1)}, bf16[512,128]{1,0:T(8,128)(2,1)S(1)}, u32[]{:S(2)}, u32[]{:S(2)}) collective-permute-start(bf16[512,128]{1,0:T(8,128)(2,1)S(1)} %get-tuple-element.73), channel_id=1, source_target_pairs={{0,6},{1,7},{2,4},{3,5},{4,2},{5,3},{6,0},{7,1},{8,14},{9,15},{10,... | collective-permute-start | bytes 393224 | tf_op jit(solution)/shard_map/out_x/ppermute | solution.py:524
  107.3 5.9 %collective-permute-start.29 = (bf16[384,128]{1,0:T(8,128)(2,1)S(1)}, bf16[384,128]{1,0:T(8,128)(2,1)S(1)}, u32[]{:S(2)}, u32[]{:S(2)}) collective-permute-start(bf16[384,128]{1,0:T(8,128)(2,1)S(1)} %get-tuple-element.82), channel_id=1, source_target_pairs={{0,8},{8,0},{16,24},{24,16},{32,40},{40,32},{48,56},{56,48},{64,72... | collective-permute-start | bytes 294920 | tf_op jit(solution)/shard_map/home/ppermute | solution.py:524
  107.4 8.5 %collective-permute-start.30 = (bf16[384,128]{1,0:T(8,128)(2,1)S(1)}, bf16[384,128]{1,0:T(8,128)(2,1)S(1)}, u32[]{:S(2)}, u32[]{:S(2)}) collective-permute-start(bf16[384,128]{1,0:T(8,128)(2,1)S(1)} %get-tuple-element.83), channel_id=1, source_target_pairs={{0,16},{8,24},{16,0},{24,8},{32,48},{40,56},{48,32},{56,40},{64,80... | collective-permute-start | bytes 294920 | tf_op jit(solution)/shard_map/home/ppermute | solution.py:524
  109.9 8.7 %collective-permute-start.31 = (bf16[384,128]{1,0:T(8,128)(2,1)S(1)}, bf16[384,128]{1,0:T(8,128)(2,1)S(1)}, u32[]{:S(2)}, u32[]{:S(2)}) collective-permute-start(bf16[384,128]{1,0:T(8,128)(2,1)S(1)} %get-tuple-element.84), channel_id=1, source_target_pairs={{0,24},{8,16},{16,8},{24,0},{32,56},{40,48},{48,40},{56,32},{64,88... | collective-permute-start | bytes 294920 | tf_op jit(solution)/shard_map/home/ppermute | solution.py:524

commit v2 on v1

--- a/solution.py
+++ b/solution.py
@@ -176,6 +176,7 @@
     eyef = eye.astype(F32)
     lblk = causal.astype(BF)
     trans, writes = [], []
+    saved = []
     for i in range(4):
         k = pack[i, 0:128, :]
         v = pack[i, 128:256, :]
@@ -193,26 +194,37 @@
         kept[at("er", i), :] = decay
         kept[at("k", i), :] = kf
         lower = jnp.where(strict, (beta_col * rk_col) * (decay * mm(k, k, NT)), 0.0)
-        inv = eyef - jnp.where((row >> 1) == (col >> 1), lower, 0.0)
-        for bit in range(1, 6):
-            near = ((row >> (bit + 1)) == (col >> (bit + 1))) & ((row >> bit) != (col >> bit))
-            inv = inv - dot3(dot3(inv, jnp.where(near, lower, 0.0)), inv)
+        saved.append((k, v, scal, scalf, cum_col, cum_row, beta_row, kf, rk_col, rk_row, lower))
+    lowers = [x[-1] for x in saved]
+    invs = [eyef - jnp.where((row >> 1) == (col >> 1), lower, 0.0) for lower in lowers]
+    for bit in range(1, 6):
+        near = ((row >> (bit + 1)) == (col >> (bit + 1))) & ((row >> bit) != (col >> bit))
+        steps = [dot3(inv, jnp.where(near, lower, 0.0)) for inv, lower in zip(invs, lowers)]
+        steps = [dot3(step, inv) for step, inv in zip(steps, invs)]
+        invs = [inv - step for inv, step in zip(invs, steps)]
+    ws, us = [], []
+    for x, inv in zip(saved, invs):
+        k, v, cum_row, beta_row, rk_row = x[0], x[1], x[5], x[6], x[9]
+        ws.append(dot2(inv * (beta_row * jnp.exp(cum_row) * rk_row), k))
+        us.append(dot2(inv * beta_row, v))
+    abs_ = []
+    top = lax.broadcasted_iota(jnp.int32, (128, 256), 0) < 64
+    for i, (x, inv, w, u) in enumerate(zip(saved, invs, ws, us)):
+        cum_col, cum_row, kf, rk_col = x[4], x[5], x[7], x[8]
         kept[at("inv", i), :] = inv
-        w = dot2(inv * (beta_row * jnp.exp(cum_row) * rk_row), k)
-        u = dot2(inv * beta_row, v)
-        wu = jnp.concatenate([w, u], 1)
         kept[at("w", i), :] = w
         kept[at("u", i), :] = u
-        last0, last1 = cum_row[:, 63:64], cum_row[:, 127:128]
-        tail = jnp.exp(jnp.where(row[:, 0:1] < 64, last0, last1) - cum_col) * rk_col
+        tail = jnp.exp(jnp.where(row[:, 0:1] < 64, cum_row[:, 63:64], cum_row[:, 127:128]) - cum_col) * rk_col
         kept[at("kt", i), :] = tail * kf
-        rhs = wu * tail
-        top = lax.broadcasted_iota(jnp.int32, (128, 256), 0) < 64
+        rhs = jnp.concatenate([w, u], 1) * tail
         rhs = jnp.concatenate([jnp.where(top, rhs, 0.0), jnp.where(top, 0.0, rhs)], 1)
         kt = kf.T.astype(BF)
-        ab = stack(NN, [kt, kt], split(rhs))
-        for b, last in ((0, last0), (1, last1)):
+        abs_.append(stack(NN, [kt, kt], split(rhs)))
+    for x, ab in zip(saved, abs_):
+        scalf, cum_row = x[3], x[5]
+        for b in range(2):
             keep = scalf[19:20, 64 * b : 64 * b + 1]
+            last = cum_row[:, 64 * b + 63 : 64 * b + 64]
             trans.append(keep * (jnp.exp(last) * eyef - ab[:, 256 * b : 256 * b + 128]))
             writes.append(keep * ab[:, 256 * b + 128 : 256 * b + 256])
 
@@ -268,19 +280,31 @@
         scals[pl.ds(wh[0] ^ m, 1)] = a[256:288, :][None]
         qs[pl.ds(wh[0] ^ m, 1)] = a[288:416, :][None]
     lblk = block_masks()[2].astype(BF)
+    saved, pws, reads = [], [], []
     for i in range(4):
         q = qs[i]
         qf = q.astype(F32)
         cum_col, cols = gates(scals[i], lblk)
-        exp_col = jnp.exp(cum_col)
         rq_col = lax.rsqrt(jnp.sum(qf * qf, 1, keepdims=True) + 1e-6)
         scores = kept[at("er", i), :] * (rq_col * mm(q, kept[at("k", i), :].astype(BF), NT))
         later[at("p", i), :] = scores
-        pw = dot2(scores, jnp.concatenate([kept[at("w", i), :], kept[at("u", i), :]], 1))
+        saved.append((qf, jnp.exp(cum_col), cols, rq_col, scores))
+    for i in range(4):
+        pws.append(dot2(saved[i][-1], jnp.concatenate([kept[at("w", i), :], kept[at("u", i), :]], 1)))
+    for i in range(4):
+        qf, exp_col, _, rq_col, _ = saved[i]
         qn = rq_col * qf
-        qe = exp_col * qn - pw[:, 0:128]
+        qe = exp_col * qn - pws[i][:, 0:128]
         later[at("qe", i), :] = qe
         later[at("qn", i), :] = qn
+        for c in (2 * i, 2 * i + 1):
+            levels = [n for n in (1, 2, 3) if c >> (n - 1) & 1]
+            rhs = jnp.concatenate(
+                [kept[at("s", READS.index((c, n))), :] for n in levels] + [kept[at("m", c), :]], 1
+            )
+            reads.append(dot2(qe[64 * (c & 1) : 64 * (c & 1) + 64], rhs))
+    for i in range(4):
+        _, exp_col, cols, rq_col, _ = saved[i]
         weights = [cols[:, 5 + 2 * n : 6 + 2 * n] + cols[:, 6 + 2 * n : 7 + 2 * n] for n in range(TIERS)]
         beta_col = cols[:, 3:4] + cols[:, 4:5]
         held[i * 128 : (i + 1) * 128, :] = jnp.concatenate(
@@ -289,15 +313,11 @@
         for c in (2 * i, 2 * i + 1):
             rows = slice(64 * (c & 1), 64 * (c & 1) + 64)
             levels = [n for n in (1, 2, 3) if c >> (n - 1) & 1]
-            rhs = jnp.concatenate(
-                [kept[at("s", READS.index((c, n))), :] for n in levels] + [kept[at("m", c), :]], 1
-            )
-            read = dot2(qe[rows], rhs)
-            out = weights[0][rows] * pw[rows, 128:256]
+            out = weights[0][rows] * pws[i][rows, 128:256]
             for n, level in enumerate(levels):
-                out = out + weights[level][rows] * read[:, 128 * n : 128 * n + 128]
+                out = out + weights[level][rows] * reads[c][:, 128 * n : 128 * n + 128]
             held[1024 + 64 * c : 1024 + 64 * c + 64, :] = out
-            held[512 + 64 * c : 512 + 64 * c + 64, :] = read[:, 128 * len(levels) :]
+            held[512 + 64 * c : 512 + 64 * c + 64, :] = reads[c][:, 128 * len(levels) :]
 
 
 def pair_body(wh, own, other, bf_out, f_out, omap_out):
@@ -399,7 +419,7 @@
     wd = [held[0:512, 4 + n : 5 + n] * dof for n in range(3)]
     carried = dot2(jnp.concatenate(wd, 1), far[...], NT)
     reach = {}
-    dqe = []
+    dqe, dps, dqns, lefts = [], [], [], []
     for c in range(8):
         rows = slice(64 * (c & 1), 64 * (c & 1) + 64)
         doc = do[c >> 1, rows, :].astype(F32)
@@ -408,20 +428,24 @@
         right = jnp.concatenate(
             [kept[at("s", READS.index((c, n))), :] for n in levels] + [kept[at("m", c), :]], 1
         )
+        lefts.append(left)
         dqe.append(dot2(left, right, NT))
-        if levels:
-            r = tn(later[at("qe", c, 64), :], left[:, 0 : 128 * len(levels)], dot2)
-            for n, level in enumerate(levels):
-                reach[c, level] = r[:, 128 * n : 128 * n + 128]
+    for c in range(1, 8):
+        levels = [n for n in (1, 2, 3) if c >> (n - 1) & 1]
+        r = tn(later[at("qe", c, 64), :], lefts[c][:, 0 : 128 * len(levels)], dot2)
+        for n, level in enumerate(levels):
+            reach[c, level] = r[:, 128 * n : 128 * n + 128]
+    dqe = [jnp.concatenate([dqe[2 * i], dqe[2 * i + 1]], 0) for i in range(4)]
+    chunks = [slice(128 * i, 128 * i + 128) for i in range(4)]
+    outs = [held[rows, 0:1] * do[i].astype(F32) for i, rows in enumerate(chunks)]
     for i in range(4):
-        doc = do[i].astype(F32)
-        rows = slice(128 * i, 128 * i + 128)
-        dqei = jnp.concatenate([dqe[2 * i], dqe[2 * i + 1]], 0)
         wu = jnp.concatenate([kept[at("w", i), :], kept[at("u", i), :]], 1)
-        dp = dot2(jnp.concatenate([-dqei, held[rows, 0:1] * doc], 1), wu, NT) * kept[at("er", i), :]
-        dqn = held[rows, 9:10] * dqei + dot2(dp, kept[at("k", i), :])
+        dps.append(dot2(jnp.concatenate([-dqe[i], outs[i]], 1), wu, NT) * kept[at("er", i), :])
+    for i, rows in enumerate(chunks):
+        dqns.append(held[rows, 9:10] * dqe[i] + dot2(dps[i], kept[at("k", i), :]))
+    for i, rows in enumerate(chunks):
         q = later[at("qn", i), :]
-        dq_out[i] = (held[rows, 8:9] * (dqn - q * jnp.sum(q * dqn, 1, keepdims=True))).astype(BF)
+        dq_out[i] = (held[rows, 8:9] * (dqns[i] - q * jnp.sum(q * dqns[i], 1, keepdims=True))).astype(BF)
     row, col = iotas(128, 128)
     eyef = (row == col).astype(F32)
 
@@ -437,23 +461,25 @@
     }
     a4 = kept[at("a4", 1), :]
     suf = {3: eyef, 2: kept[at("a2", 3), :], 1: a4, 0: dot3(a4, kept[at("a2", 1), :])}
-    for i in range(4):
-        odd = pair[i]
-        even = reach[2 * i + 1, 1] if odd is None else reach[2 * i + 1, 1] + tnn("a", 2 * i + 1, odd)
-        odd = jnp.zeros((128, 128), F32) if odd is None else odd
-        s_odd = suf[i]
-        s_even = dot3(s_odd, kept[at("a", 2 * i + 1), :])
-        rows = slice(128 * i, 128 * i + 128)
-        doc = do[i].astype(F32)
-        pd = tn(later[at("p", i), :], held[rows, 0:1] * doc, dot3)
+    zero = jnp.zeros((128, 128), F32)
+    odds = [zero if pair[i] is None else pair[i] for i in range(4)]
+    pds = [tn(later[at("p", i), :], outs[i], dot3) for i in range(4)]
+    evens = [
+        reach[2 * i + 1, 1] if pair[i] is None else reach[2 * i + 1, 1] + tnn("a", 2 * i + 1, pair[i])
+        for i in range(4)
+    ]
+    s_evens = [dot3(suf[i], kept[at("a", 2 * i + 1), :]) for i in range(4)]
+    both = []
+    for i, rows in enumerate(chunks):
         kk = held[rows, 7:8] * kept[at("kt", i), :]
-        left = dot3(kk[0:64], jnp.concatenate([even, s_even.T], 1))
-        right = dot3(kk[64:128], jnp.concatenate([odd, s_odd.T], 1))
-        hn = jnp.concatenate([left, right], 0)
-        both = jnp.concatenate([pd + hn[:, 0:128], hn[:, 128:256]], 1)
-        both = held[rows, 10:11] * tn(kept[at("inv", i), :], both, dot3)
-        dv_out[rows, :] = both[:, 0:128]
-        gmap_out[rows, :] = both[:, 128:256]
+        left = dot3(kk[0:64], jnp.concatenate([evens[i], s_evens[i].T], 1))
+        right = dot3(kk[64:128], jnp.concatenate([odds[i], suf[i].T], 1))
+        both.append(jnp.concatenate([left, right], 0))
+    both = [jnp.concatenate([pd + hn[:, 0:128], hn[:, 128:256]], 1) for pd, hn in zip(pds, both)]
+    both = [tn(kept[at("inv", i), :], both[i], dot3) for i in range(4)]
+    for i, rows in enumerate(chunks):
+        dv_out[rows, :] = held[rows, 10:11] * both[i][:, 0:128]
+        gmap_out[rows, :] = held[rows, 10:11] * both[i][:, 128:256]
 
 
 def near_body(wh, r1, r2, r3, ups, own, fin, x4, send_out, keep_out):
@@ -588,13 +614,13 @@
     at = [attn] + [xor(attn, "seq", m, "attn") for m in (1, 2, 3)]
     even, odd = call(3, project_body, [((2048, 128), BF)] * 2, [where] + at + weight, [pltpu.VMEM((8, 512, 128), BF)], after=[send])
     swapped = xor(odd, "head", 1, "out_core")
-    sums = call(1, sum_pair_body, [(T, F32), (T, BF), (T, BF), (T, BF)], [even, swapped], after=[got])
+    sums = call(1, sum_pair_body, [(T, F32), (T, BF), (T, BF), (T, BF)], [even, swapped])
     rx = [xor(sums[n], "head", 2 * n, "out_x") for n in (1, 2, 3)]
     dq, dv_part, gmap = call(
-        4, grad_body,
+        200, grad_body,
         [((4,) + S, BF), (T, F32), (T, F32)],
         [where, do, held, far_states, kept, later],
-        after=[sums[1]],
+        after=[got],
     )
     dv = call(1, value_body, [((4,) + S, BF)], [where, got, local, other, dv_part, gmap])[0]
     parts = call(

time: 120 us -> 109 us (0.908)
  starting transfers between devices: 49.2 us -> 43 us
  Pallas kernels: 31.2 us -> 25.2 us
    ppermute x32, starting transfers between devices: 49.2 us -> 43 us  [xor(): lax.ppermute(value, axis, [(s, s ^ mask) for s in range(lax.axis_size(axi...]
    pallas_call x17, Pallas kernels: 31.2 us -> 25.2 us  [call(): pl.pallas_call(waiting, out_shape=[jax.ShapeDtypeStruct(s, d) for s, d in...]
  transfers between devices with their start and end apart: 32 -> 32, of which waited for: 12 -> 17; matrix products, arithmetic and copies ran while one was open for 0% -> 1% of each run, Pallas kernels for 22% -> 19%
where the time goes in v2:
time: 109 us
  starting transfers between devices  43 us (39%)
  waiting for transfers between devices  36.7 us (34%)
  Pallas kernels  25.2 us (23%)
  local copies, waits for them, and re-layouts  2.97 us (3%)
    ppermute x32, starting transfers between devices, xor(): lax.ppermute(value, axis, [(s, s ^ mask) for s in range(lax.axis_size(axi...  43 us
    ppermute x32, waiting for transfers between devices, xor(): lax.ppermute(value, axis, [(s, s ^ mask) for s in range(lax.axis_size(axi...  36.7 us
    pallas_call x17, Pallas kernels, call(): pl.pallas_call(waiting, out_shape=[jax.ShapeDtypeStruct(s, d) for s, d in...  25.2 us
    unnamed x10, local copies, waits for them, and re-layouts  2.39 us
  transfers between devices with their start and end apart: 32, of which 17 were waited for; matrix products, arithmetic and copies ran while one was open for 1% of the time, Pallas kernels for 19%

profile of v2, /device:TPU:32, one launch (start us, length us, event | category | flops | bytes accessed | tf_op | source)
XLA Modules:
  0.0 108.7 jit_solution(6163229432393175117)
XLA Ops:
  0.6 5.5 %collective-permute-start = (bf16[512,128]{1,0:T(8,128)(2,1)}, bf16[512,128]{1,0:T(8,128)(2,1)S(1)}, u32[]{:S(2)}, u32[]{:S(2)}) collective-permute-start(bf16[512,128]{1,0:T(8,128)(2,1)} %refs_0_.1), channel_id=1, source_target_pairs={{0,48},{8,56},{16,32},{24,40},{32,16},{40,24},{48,0},{56,8},{64,11... | collective-permute-start | bytes 393224 | tf_op jit(solution)/shard_map/weight_half/ppermute | solution.py:550
  6.7 2.7 %pack.1 = (bf16[544,128]{1,0:T(8,128)(2,1)}, bf16[544,128]{1,0:T(8,128)(2,1)}, bf16[544,128]{1,0:T(8,128)(2,1)}, bf16[544,128]{1,0:T(8,128)(2,1)}) custom-call(s32[8]{0:T(128)} %stack.27.refs_0_, s32[2]{0:T(128)} %refs_1_.1, bf16[128,512]{1,0:T(8,128)(2,1)} %refs_2_.1, bf16[128,512]{1,0:T(8,128)(2,1)} %refs_3_.1, bf16[128,512]{1,0:T(8,128)(2,1)} %refs_4_.1, ...), custom_call_target="tpu_custom_call" | custom-call | flops 300000000 | tf_op jit(solution)/shard_map/pack/pallas_call | solution.py:105
  9.4 1.1 %collective-permute-start.1 = (bf16[544,128]{1,0:T(8,128)(2,1)}, bf16[544,128]{1,0:T(8,128)(2,1)S(1)}, u32[]{:S(2)}, u32[]{:S(2)}) collective-permute-start(bf16[544,128]{1,0:T(8,128)(2,1)} %get-tuple-element.46), channel_id=1, source_target_pairs={{0,8},{8,0},{16,24},{24,16},{32,40},{40,32},{48,56},{56,48},{64,72... | collective-permute-start | bytes 417800 | tf_op jit(solution)/shard_map/reshard/ppermute | solution.py:550
  10.5 1.5 %collective-permute-start.2 = (bf16[544,128]{1,0:T(8,128)(2,1)}, bf16[544,128]{1,0:T(8,128)(2,1)S(1)}, u32[]{:S(2)}, u32[]{:S(2)}) collective-permute-start(bf16[544,128]{1,0:T(8,128)(2,1)} %get-tuple-element.47), channel_id=1, source_target_pairs={{0,16},{8,24},{16,0},{24,8},{32,48},{40,56},{48,32},{56,40},{64,80... | collective-permute-start | bytes 417800 | tf_op jit(solution)/shard_map/reshard/ppermute | solution.py:550
  12.0 1.0 collective-permute-start.3
  13.0 0.9 copy-done.1
  13.9 0.9 copy-done.2
  14.8 1.5 %collective-permute-done.1.refs_1_.refs_2_ = bf16[544,128]{1,0:T(8,128)(2,1)S(1)} collective-permute-done((bf16[544,128]{1,0:T(8,128)(2,1)}, bf16[544,128]{1,0:T(8,128)(2,1)S(1)}, u32[]{:S(2)}, u32[]{:S(2)}) %collective-permute-start.1) | collective-permute-done | bytes 139296 | tf_op jit(solution)/shard_map/reshard/ppermute | solution.py:550
  16.3 5.8 %collective-permute-done.2.refs_2_.refs_3_ = bf16[544,128]{1,0:T(8,128)(2,1)S(1)} collective-permute-done((bf16[544,128]{1,0:T(8,128)(2,1)}, bf16[544,128]{1,0:T(8,128)(2,1)S(1)}, u32[]{:S(2)}, u32[]{:S(2)}) %collective-permute-start.2) | collective-permute-done | bytes 139296 | tf_op jit(solution)/shard_map/reshard/ppermute | solution.py:550
  22.2 2.9 %collective-permute-done.3.refs_3_.refs_4_ = bf16[544,128]{1,0:T(8,128)(2,1)S(1)} collective-permute-done((bf16[544,128]{1,0:T(8,128)(2,1)}, bf16[544,128]{1,0:T(8,128)(2,1)S(1)}, u32[]{:S(2)}, u32[]{:S(2)}) %collective-permute-start.3) | collective-permute-done | bytes 139296 | tf_op jit(solution)/shard_map/reshard/ppermute | solution.py:550
  25.0 2.8 %collective-permute-start.7 = (bf16[512,128]{1,0:T(8,128)(2,1)S(1)}, bf16[512,128]{1,0:T(8,128)(2,1)S(1)}, u32[]{:S(2)}, u32[]{:S(2)}) collective-permute-start(bf16[512,128]{1,0:T(8,128)(2,1)S(1)} %collect.1.refs_5_.refs_0_), channel_id=1, source_target_pairs={{0,6},{1,7},{2,4},{3,5},{4,2},{5,3},{6,0},{7,1},{8,14},{9,15},{10,... | collective-permute-start | bytes 393224 | tf_op jit(solution)/shard_map/grad_y_x/ppermute | solution.py:550
  27.9 3.0 %collective-permute-start.10 = (bf16[1024,128]{1,0:T(8,128)(2,1)S(1)}, bf16[1024,128]{1,0:T(8,128)(2,1)S(1)}, u32[]{:S(2)}, u32[]{:S(2)}) collective-permute-start(bf16[1024,128]{1,0:T(8,128)(2,1)S(1)} %get-tuple-element.49.refs_4_.refs_3_.refs_5_), channel_id=1, source_target_pairs={{0,192},{8,200},{16,208},{24,216},{32,224},{40,232},{48,240},{56,2... | collective-permute-start | bytes 786440 | tf_op jit(solution)/shard_map/weight_y/ppermute | solution.py:550
  32.0 0.8 collective-permute-start.6
  33.9 4.4 %block.1 = (bf16[256,128]{1,0:T(8,128)(2,1)S(1)}, f32[256,128]{1,0:T(8,128)S(1)}, f32[7424,128]{1,0:T(8,128)S(1)}) custom-call(s32[8]{0:T(128)S(1)} %copy-done.3, bf16[544,128]{1,0:T(8,128)(2,1)S(1)} %get-tuple-element.45.refs_0_.refs_1_, bf16[544,128]{1,0:T(8,128)(2,1)S(1)} %collective-permute-done.1.refs_1_.refs_2_, ...), custom_call_target="tpu_custom_call" | custom-call | flops 6000000000 | tf_op jit(solution)/shard_map/block/pallas_call | solution.py:105
  38.5 1.8 %collective-permute-done.10.refs_7_.refs_6_.refs_8_ = bf16[1024,128]{1,0:T(8,128)(2,1)S(1)} collective-permute-done((bf16[1024,128]{1,0:T(8,128)(2,1)S(1)}, bf16[1024,128]{1,0:T(8,128)(2,1)S(1)}, u32[]{:S(2)}, u32[]{:S(2)}) %collective-permute-start.10) | collective-permute-done | bytes 262176 | tf_op jit(solution)/shard_map/weight_y/ppermute | solution.py:550
  41.8 1.7 %collective-permute-done.11.refs_2_ = bf16[2048,128]{1,0:T(8,128)(2,1)S(1)} collective-permute-done((bf16[2048,128]{1,0:T(8,128)(2,1)S(1)}, bf16[2048,128]{1,0:T(8,128)(2,1)S(1)}, u32[]{:S(2)}, u32[]{:S(2)}) %collective-permute-start.11) | collective-permute-done | bytes 524320 | tf_op jit(solution)/shard_map/grad_y_core/ppermute | solution.py:550
  43.5 2.0 %back_product.1 = (f32[512,128]{1,0:T(8,128)S(1)}, bf16[512,128]{1,0:T(8,128)(2,1)S(1)}, bf16[512,128]{1,0:T(8,128)(2,1)S(1)}, bf16[512,128]{1,0:T(8,128)(2,1)S(1)}) custom-call(s32[8]{0:T(128)S(1)} %copy-done.4, bf16[2048,128]{1,0:T(8,128)(2,1)S(1)} %join.1.refs_1_, bf16[2048,128]{1,0:T(8,128)(2,1)S(1)} %collective-permute-done.11.refs_2_, ...), custom_call_target="tpu_custom_call" | custom-call | flops 300000000 | tf_op jit(solution)/shard_map/back_product/pallas_call | solution.py:105
  45.5 3.4 %collective-permute-done.4.refs_2_.refs_3_ = bf16[256,128]{1,0:T(8,128)(2,1)S(1)} collective-permute-done((bf16[256,128]{1,0:T(8,128)(2,1)S(1)}, bf16[256,128]{1,0:T(8,128)(2,1)S(1)}, u32[]{:S(2)}, u32[]{:S(2)}) %collective-permute-start.4) | collective-permute-done | bytes 65568 | tf_op jit(solution)/shard_map/scan_half/ppermute | solution.py:550
  48.9 0.7 pair.1
  49.6 3.0 %collective-permute-start.14 = (bf16[256,128]{1,0:T(8,128)(2,1)S(1)}, bf16[256,128]{1,0:T(8,128)(2,1)S(1)}, u32[]{:S(2)}, u32[]{:S(2)}) collective-permute-start(bf16[256,128]{1,0:T(8,128)(2,1)S(1)} %get-tuple-element.54.refs_6_), channel_id=1, source_target_pairs={{0,192},{8,200},{16,208},{24,216},{32,224},{40,232},{48,240},{56,2... | collective-permute-start | bytes 196616 | tf_op jit(solution)/shard_map/scan_y/ppermute | solution.py:550
  52.7 1.0 collective-permute-start.20
  53.7 3.4 %collective-permute-start.18 = (bf16[512,128]{1,0:T(8,128)(2,1)S(1)}, bf16[512,128]{1,0:T(8,128)(2,1)S(1)}, u32[]{:S(2)}, u32[]{:S(2)}) collective-permute-start(bf16[512,128]{1,0:T(8,128)(2,1)S(1)} %get-tuple-element.52.refs_3_), channel_id=1, source_target_pairs={{0,8},{8,0},{16,24},{24,16},{32,40},{40,32},{48,56},{56,48},{64,72... | collective-permute-start | bytes 393224 | tf_op jit(solution)/shard_map/grad_attn/ppermute | solution.py:550
  58.2 2.3 %query.1 = (f32[1536,128]{1,0:T(8,128)S(1)}, f32[1536,128]{1,0:T(8,128)S(1)}) custom-call(s32[8]{0:T(128)S(1)} %copy-done.4, bf16[544,128]{1,0:T(8,128)(2,1)S(1)} %get-tuple-element.45.refs_0_.refs_1_, bf16[544,128]{1,0:T(8,128)(2,1)S(1)} %collective-permute-done.1.refs_1_.refs_2_, bf16[544,128]{1,0:T(8,128)(2,1)S(1)} %collective-permute-done.2.refs_2_.refs_3_, ...), custom_call_target="tpu_custom_call" | custom-call | flops 400000000 | tf_op jit(solution)/shard_map/query/pallas_call | solution.py:105
  60.5 2.3 %collective-permute-done.13.refs_3_ = bf16[256,128]{1,0:T(8,128)(2,1)S(1)} collective-permute-done((bf16[256,128]{1,0:T(8,128)(2,1)S(1)}, bf16[256,128]{1,0:T(8,128)(2,1)S(1)}, u32[]{:S(2)}, u32[]{:S(2)}) %collective-permute-start.13) | collective-permute-done | bytes 65568 | tf_op jit(solution)/shard_map/scan_y/ppermute | solution.py:550
  62.8 1.9 %far.1 = (bf16[512,128]{1,0:T(8,128)(2,1)S(1)}, f32[128,384]{1,0:T(8,128)S(1)}, f32[4,128,128]{2,1,0:T(8,128)S(1)}, f32[128,128]{1,0:T(8,128)S(1)}) custom-call(s32[8]{0:T(128)S(1)} %copy-done.4, f32[256,128]{1,0:T(8,128)S(1)} %get-tuple-element.53.refs_1_, bf16[256,128]{1,0:T(8,128)(2,1)S(1)} %collective-permute-done.12.refs_2_, ...), custom_call_target="tpu_custom_call" | custom-call | flops 200000000 | tf_op jit(solution)/shard_map/far/pallas_call | solution.py:105
  64.7 1.1 %collective-permute-start.17 = (bf16[512,128]{1,0:T(8,128)(2,1)S(1)}, bf16[512,128]{1,0:T(8,128)(2,1)S(1)}, u32[]{:S(2)}, u32[]{:S(2)}) collective-permute-start(bf16[512,128]{1,0:T(8,128)(2,1)S(1)} %get-tuple-element.58.refs_7_.refs_1_), channel_id=1, source_target_pairs={{0,24},{8,16},{16,8},{24,0},{32,56},{40,48},{48,40},{56,32},{64,88... | collective-permute-start | bytes 393224 | tf_op jit(solution)/shard_map/attn/ppermute | solution.py:550
  65.8 1.3 %collective-permute-start.16 = (bf16[512,128]{1,0:T(8,128)(2,1)S(1)}, bf16[512,128]{1,0:T(8,128)(2,1)S(1)}, u32[]{:S(2)}, u32[]{:S(2)}) collective-permute-start(bf16[512,128]{1,0:T(8,128)(2,1)S(1)} %get-tuple-element.58.refs_7_.refs_1_), channel_id=1, source_target_pairs={{0,16},{8,24},{16,0},{24,8},{32,48},{40,56},{48,32},{56,40},{64,80... | collective-permute-start | bytes 393224 | tf_op jit(solution)/shard_map/attn/ppermute | solution.py:550
  67.2 1.1 %collective-permute-start.15 = (bf16[512,128]{1,0:T(8,128)(2,1)S(1)}, bf16[512,128]{1,0:T(8,128)(2,1)S(1)}, u32[]{:S(2)}, u32[]{:S(2)}) collective-permute-start(bf16[512,128]{1,0:T(8,128)(2,1)S(1)} %get-tuple-element.58.refs_7_.refs_1_), channel_id=1, source_target_pairs={{0,8},{8,0},{16,24},{24,16},{32,40},{40,32},{48,56},{56,48},{64,72... | collective-permute-start | bytes 393224 | tf_op jit(solution)/shard_map/attn/ppermute | solution.py:550
  68.3 1.4 %reach.1 = (bf16[4,128,128]{2,1,0:T(8,128)(2,1)S(1)}, bf16[128,128]{1,0:T(8,128)(2,1)S(1)}, bf16[128,128]{1,0:T(8,128)(2,1)S(1)}, f32[128,128]{1,0:T(8,128)S(1)}) custom-call(s32[8]{0:T(128)S(1)} %copy-done.4, f32[512,128]{1,0:T(8,128)S(1)} %get-tuple-element.59.refs_1_, bf16[512,128]{1,0:T(8,128)(2,1)S(1)} %collective-permute-done.18.refs_2_, ...), custom_call_target="tpu_custom_call" | custom-call | flops 200000000 | tf_op jit(solution)/shard_map/reach/pallas_call | solution.py:105
  69.9 2.4 %collective-permute-start.23 = (bf16[128,128]{1,0:T(8,128)(2,1)S(1)}, bf16[128,128]{1,0:T(8,128)(2,1)S(1)}, u32[]{:S(2)}, u32[]{:S(2)}) collective-permute-start(bf16[128,128]{1,0:T(8,128)(2,1)S(1)} %get-tuple-element.63), channel_id=1, source_target_pairs={{0,192},{8,200},{16,208},{24,216},{32,224},{40,232},{48,240},{56,2... | collective-permute-start | bytes 98312 | tf_op jit(solution)/shard_map/back_y/ppermute | solution.py:550
  72.4 1.3 %collective-permute-done.21.refs_1_ = bf16[128,128]{1,0:T(8,128)(2,1)S(1)} collective-permute-done((bf16[128,128]{1,0:T(8,128)(2,1)S(1)}, bf16[128,128]{1,0:T(8,128)(2,1)S(1)}, u32[]{:S(2)}, u32[]{:S(2)}) %collective-permute-start.21) | collective-permute-done | bytes 32800 | tf_op jit(solution)/shard_map/back_y/ppermute | solution.py:550
  73.7 2.0 %collective-permute-start.22 = (bf16[128,128]{1,0:T(8,128)(2,1)S(1)}, bf16[128,128]{1,0:T(8,128)(2,1)S(1)}, u32[]{:S(2)}, u32[]{:S(2)}) collective-permute-start(bf16[128,128]{1,0:T(8,128)(2,1)S(1)} %get-tuple-element.63), channel_id=1, source_target_pairs={{0,128},{8,136},{16,144},{24,152},{32,160},{40,168},{48,176},{56,1... | collective-permute-start | bytes 98312 | tf_op jit(solution)/shard_map/back_y/ppermute | solution.py:550
  75.7 3.4 %collective-permute-done.22.refs_2_ = bf16[128,128]{1,0:T(8,128)(2,1)S(1)} collective-permute-done((bf16[128,128]{1,0:T(8,128)(2,1)S(1)}, bf16[128,128]{1,0:T(8,128)(2,1)S(1)}, u32[]{:S(2)}, u32[]{:S(2)}) %collective-permute-start.22) | collective-permute-done | bytes 32800 | tf_op jit(solution)/shard_map/back_y/ppermute | solution.py:550
  79.1 1.1 %near.1 = (bf16[128,128]{1,0:T(8,128)(2,1)S(1)}, f32[128,128]{1,0:T(8,128)S(1)}) custom-call(s32[8]{0:T(128)S(1)} %copy-done.4, bf16[128,128]{1,0:T(8,128)(2,1)S(1)} %collective-permute-done.21.refs_1_, bf16[128,128]{1,0:T(8,128)(2,1)S(1)} %collective-permute-done.22.refs_2_, bf16[128,128]{1,0:T(8,128)(2,1)S(1)} %collective-permute-done.23.refs_3_, ...), custom_call_target="tpu_custom_call" | custom-call | flops 100000000 | tf_op jit(solution)/shard_map/near/pallas_call | solution.py:105
  80.3 1.9 %project.1 = (bf16[2048,128]{1,0:T(8,128)(2,1)S(1)}, bf16[2048,128]{1,0:T(8,128)(2,1)S(1)}) custom-call(s32[8]{0:T(128)S(1)} %copy-done.4, bf16[512,128]{1,0:T(8,128)(2,1)S(1)} %get-tuple-element.58.refs_7_.refs_1_, bf16[512,128]{1,0:T(8,128)(2,1)S(1)} %collective-permute-done.15.refs_2_, bf16[512,128]{1,0:T(8,128)(2,1)S(1)} %collective-permute-done.16.refs_3_, ...), custom_call_target="tpu_custom_call" | custom-call | flops 300000000 | tf_op jit(solution)/shard_map/project/pallas_call | solution.py:105
  82.3 1.8 %collective-permute-done.24.refs_1_ = bf16[2048,128]{1,0:T(8,128)(2,1)S(1)} collective-permute-done((bf16[2048,128]{1,0:T(8,128)(2,1)S(1)}, bf16[2048,128]{1,0:T(8,128)(2,1)S(1)}, u32[]{:S(2)}, u32[]{:S(2)}) %collective-permute-start.24) | collective-permute-done | bytes 524320 | tf_op jit(solution)/shard_map/out_core/ppermute | solution.py:550
  84.5 1.7 %collective-permute-start.26 = (bf16[512,128]{1,0:T(8,128)(2,1)S(1)}, bf16[512,128]{1,0:T(8,128)(2,1)S(1)}, u32[]{:S(2)}, u32[]{:S(2)}) collective-permute-start(bf16[512,128]{1,0:T(8,128)(2,1)S(1)} %get-tuple-element.72), channel_id=1, source_target_pairs={{0,4},{1,5},{2,6},{3,7},{4,0},{5,1},{6,2},{7,3},{8,12},{9,13},{10,... | collective-permute-start | bytes 393224 | tf_op jit(solution)/shard_map/out_x/ppermute | solution.py:550
  86.3 2.8 %collective-permute-start.27 = (bf16[512,128]{1,0:T(8,128)(2,1)S(1)}, bf16[512,128]{1,0:T(8,128)(2,1)S(1)}, u32[]{:S(2)}, u32[]{:S(2)}) collective-permute-start(bf16[512,128]{1,0:T(8,128)(2,1)S(1)} %get-tuple-element.73), channel_id=1, source_target_pairs={{0,6},{1,7},{2,4},{3,5},{4,2},{5,3},{6,0},{7,1},{8,14},{9,15},{10,... | collective-permute-start | bytes 393224 | tf_op jit(solution)/shard_map/out_x/ppermute | solution.py:550
  89.0 3.7 %grad.1 = (bf16[4,128,128]{2,1,0:T(8,128)(2,1)S(1)}, f32[512,128]{1,0:T(8,128)S(1)}, f32[512,128]{1,0:T(8,128)S(1)}) custom-call(s32[8]{0:T(128)S(1)} %copy-done.4, bf16[4,128,128]{2,1,0:T(8,128)(2,1)S(1)} %get-tuple-element.74.refs_1_, f32[1536,128]{1,0:T(8,128)S(1)} %get-tuple-element.57.refs_6_.refs_5_.refs_2_, f32[128,384]{1,0:T(8,128)S(1)} %get-tuple-element.75.refs_3_, ...), custom_call_target="tpu_custom_call" | custom-call | flops 20000000000 | tf_op jit(solution)/shard_map/grad/pallas_call | solution.py:105
  92.7 1.0 value.1.refs_6_
  93.7 1.2 %collective-permute-done.27.refs_4_ = bf16[512,128]{1,0:T(8,128)(2,1)S(1)} collective-permute-done((bf16[512,128]{1,0:T(8,128)(2,1)S(1)}, bf16[512,128]{1,0:T(8,128)(2,1)S(1)}, u32[]{:S(2)}, u32[]{:S(2)}) %collective-permute-start.27) | collective-permute-done | bytes 131104 | tf_op jit(solution)/shard_map/out_x/ppermute | solution.py:550
  95.6 1.1 collective-permute-start.29
  96.6 1.5 %collective-permute-start.30 = (bf16[384,128]{1,0:T(8,128)(2,1)S(1)}, bf16[384,128]{1,0:T(8,128)(2,1)S(1)}, u32[]{:S(2)}, u32[]{:S(2)}) collective-permute-start(bf16[384,128]{1,0:T(8,128)(2,1)S(1)} %get-tuple-element.83), channel_id=1, source_target_pairs={{0,16},{8,24},{16,0},{24,8},{32,48},{40,56},{48,32},{56,40},{64,80... | collective-permute-start | bytes 294920 | tf_op jit(solution)/shard_map/home/ppermute | solution.py:550
  98.2 1.0 collective-permute-start.31
  99.2 2.2 %collective-permute-done.29.refs_2_ = bf16[384,128]{1,0:T(8,128)(2,1)S(1)} collective-permute-done((bf16[384,128]{1,0:T(8,128)(2,1)S(1)}, bf16[384,128]{1,0:T(8,128)(2,1)S(1)}, u32[]{:S(2)}, u32[]{:S(2)}) %collective-permute-start.29) | collective-permute-done | bytes 98336 | tf_op jit(solution)/shard_map/home/ppermute | solution.py:550
  101.3 3.5 %collective-permute-done.30.refs_3_ = bf16[384,128]{1,0:T(8,128)(2,1)S(1)} collective-permute-done((bf16[384,128]{1,0:T(8,128)(2,1)S(1)}, bf16[384,128]{1,0:T(8,128)(2,1)S(1)}, u32[]{:S(2)}, u32[]{:S(2)}) %collective-permute-start.30) | collective-permute-done | bytes 98336 | tf_op jit(solution)/shard_map/home/ppermute | solution.py:550
  104.8 2.6 %collective-permute-done.31.refs_4_ = bf16[384,128]{1,0:T(8,128)(2,1)S(1)} collective-permute-done((bf16[384,128]{1,0:T(8,128)(2,1)S(1)}, bf16[384,128]{1,0:T(8,128)(2,1)S(1)}, u32[]{:S(2)}, u32[]{:S(2)}) %collective-permute-start.31) | collective-permute-done | bytes 98336 | tf_op jit(solution)/shard_map/home/ppermute | solution.py:550
  107.4 1.4 %place.1 = (bf16[128,512]{1,0:T(8,128)(2,1)}, bf16[128,512]{1,0:T(8,128)(2,1)}, bf16[128,512]{1,0:T(8,128)(2,1)}) custom-call(s32[8]{0:T(128)S(1)} %copy-done.4, bf16[384,128]{1,0:T(8,128)(2,1)S(1)} %get-tuple-element.81.refs_1_, bf16[384,128]{1,0:T(8,128)(2,1)S(1)} %collective-permute-done.29.refs_2_, bf16[384,128]{1,0:T(8,128)(2,1)S(1)} %collective-permute-done.30.refs_3_, ...), custom_call_target="tpu_custom_call" | custom-call | flops 100000000 | tf_op jit(solution)/shard_map/place/pallas_call | solution.py:105
  (45 shorter events, 7.1 us)
Async XLA Ops:
  0.6 12.4 %collective-permute-start = (bf16[512,128]{1,0:T(8,128)(2,1)}, bf16[512,128]{1,0:T(8,128)(2,1)S(1)}, u32[]{:S(2)}, u32[]{:S(2)}) collective-permute-start(bf16[512,128]{1,0:T(8,128)(2,1)} %refs_0_.1), channel_id=1, source_target_pairs={{0,48},{8,56},{16,32},{24,40},{32,16},{40,24},{48,0},{56,8},{64,11... | collective-permute-start | bytes 393224 | tf_op jit(solution)/shard_map/weight_half/ppermute | solution.py:550
  9.4 6.9 %collective-permute-start.1 = (bf16[544,128]{1,0:T(8,128)(2,1)}, bf16[544,128]{1,0:T(8,128)(2,1)S(1)}, u32[]{:S(2)}, u32[]{:S(2)}) collective-permute-start(bf16[544,128]{1,0:T(8,128)(2,1)} %get-tuple-element.46), channel_id=1, source_target_pairs={{0,8},{8,0},{16,24},{24,16},{32,40},{40,32},{48,56},{56,48},{64,72... | collective-permute-start | bytes 417800 | tf_op jit(solution)/shard_map/reshard/ppermute | solution.py:550
  10.5 11.6 %collective-permute-start.2 = (bf16[544,128]{1,0:T(8,128)(2,1)}, bf16[544,128]{1,0:T(8,128)(2,1)S(1)}, u32[]{:S(2)}, u32[]{:S(2)}) collective-permute-start(bf16[544,128]{1,0:T(8,128)(2,1)} %get-tuple-element.47), channel_id=1, source_target_pairs={{0,16},{8,24},{16,0},{24,8},{32,48},{40,56},{48,32},{56,40},{64,80... | collective-permute-start | bytes 417800 | tf_op jit(solution)/shard_map/reshard/ppermute | solution.py:550
  12.0 13.1 %collective-permute-start.3 = (bf16[544,128]{1,0:T(8,128)(2,1)}, bf16[544,128]{1,0:T(8,128)(2,1)S(1)}, u32[]{:S(2)}, u32[]{:S(2)}) collective-permute-start(bf16[544,128]{1,0:T(8,128)(2,1)} %get-tuple-element.48), channel_id=1, source_target_pairs={{0,24},{8,16},{16,8},{24,0},{32,56},{40,48},{48,40},{56,32},{64,88... | collective-permute-start | bytes 417800 | tf_op jit(solution)/shard_map/reshard/ppermute | solution.py:550
  13.0 0.9 copy-start.1
  13.9 0.9 copy-start.2
  25.0 18.5 %copy-start.4 = (s32[8]{0:T(128)S(1)}, s32[8]{0:T(128)}, u32[]{:S(2)}) copy-start(s32[8]{0:T(128)} %stack.27.refs_0_) | copy-start | bytes 100
  25.0 7.7 %collective-permute-start.7 = (bf16[512,128]{1,0:T(8,128)(2,1)S(1)}, bf16[512,128]{1,0:T(8,128)(2,1)S(1)}, u32[]{:S(2)}, u32[]{:S(2)}) collective-permute-start(bf16[512,128]{1,0:T(8,128)(2,1)S(1)} %collect.1.refs_5_.refs_0_), channel_id=1, source_target_pairs={{0,6},{1,7},{2,4},{3,5},{4,2},{5,3},{6,0},{7,1},{8,14},{9,15},{10,... | collective-permute-start | bytes 393224 | tf_op jit(solution)/shard_map/grad_y_x/ppermute | solution.py:550
  27.9 12.4 %collective-permute-start.10 = (bf16[1024,128]{1,0:T(8,128)(2,1)S(1)}, bf16[1024,128]{1,0:T(8,128)(2,1)S(1)}, u32[]{:S(2)}, u32[]{:S(2)}) collective-permute-start(bf16[1024,128]{1,0:T(8,128)(2,1)S(1)} %get-tuple-element.49.refs_4_.refs_3_.refs_5_), channel_id=1, source_target_pairs={{0,192},{8,200},{16,208},{24,216},{32,224},{40,232},{48,240},{56,2... | collective-permute-start | bytes 786440 | tf_op jit(solution)/shard_map/weight_y/ppermute | solution.py:550
  30.9 10.1 %collective-permute-start.9 = (bf16[1024,128]{1,0:T(8,128)(2,1)S(1)}, bf16[1024,128]{1,0:T(8,128)(2,1)S(1)}, u32[]{:S(2)}, u32[]{:S(2)}) collective-permute-start(bf16[1024,128]{1,0:T(8,128)(2,1)S(1)} %get-tuple-element.49.refs_4_.refs_3_.refs_5_), channel_id=1, source_target_pairs={{0,128},{8,136},{16,144},{24,152},{32,160},{40,168},{48,176},{56,1... | collective-permute-start | bytes 786440 | tf_op jit(solution)/shard_map/weight_y/ppermute | solution.py:550
  31.5 9.9 %collective-permute-start.8 = (bf16[1024,128]{1,0:T(8,128)(2,1)S(1)}, bf16[1024,128]{1,0:T(8,128)(2,1)S(1)}, u32[]{:S(2)}, u32[]{:S(2)}) collective-permute-start(bf16[1024,128]{1,0:T(8,128)(2,1)S(1)} %get-tuple-element.49.refs_4_.refs_3_.refs_5_), channel_id=1, source_target_pairs={{0,64},{8,72},{16,80},{24,88},{32,96},{40,104},{48,112},{56,120},{... | collective-permute-start | bytes 786440 | tf_op jit(solution)/shard_map/weight_y/ppermute | solution.py:550
  32.0 6.5 %collective-permute-start.6 = (bf16[512,128]{1,0:T(8,128)(2,1)S(1)}, bf16[512,128]{1,0:T(8,128)(2,1)S(1)}, u32[]{:S(2)}, u32[]{:S(2)}) collective-permute-start(bf16[512,128]{1,0:T(8,128)(2,1)S(1)} %collect.1.refs_5_.refs_0_), channel_id=1, source_target_pairs={{0,4},{1,5},{2,6},{3,7},{4,0},{5,1},{6,2},{7,3},{8,12},{9,13},{10,... | collective-permute-start | bytes 393224 | tf_op jit(solution)/shard_map/grad_y_x/ppermute | solution.py:550
  32.8 5.7 %collective-permute-start.5 = (bf16[512,128]{1,0:T(8,128)(2,1)S(1)}, bf16[512,128]{1,0:T(8,128)(2,1)S(1)}, u32[]{:S(2)}, u32[]{:S(2)}) collective-permute-start(bf16[512,128]{1,0:T(8,128)(2,1)S(1)} %collect.1.refs_5_.refs_0_), channel_id=1, source_target_pairs={{0,2},{1,3},{2,0},{3,1},{4,6},{5,7},{6,4},{7,5},{8,10},{9,11},{10,... | collective-permute-start | bytes 393224 | tf_op jit(solution)/shard_map/grad_y_x/ppermute | solution.py:550
  33.3 0.6 copy-start.3
  41.5 21.3 %copy-start = (f32[4,128,128]{2,1,0:T(8,128)S(1)}, f32[4,128,128]{2,1,0:T(8,128)}, u32[]{:S(2)}) copy-start(f32[4,128,128]{2,1,0:T(8,128)} %refs_7_.3) | copy-start | bytes 786436
  41.5 2.0 %collective-permute-start.11 = (bf16[2048,128]{1,0:T(8,128)(2,1)S(1)}, bf16[2048,128]{1,0:T(8,128)(2,1)S(1)}, u32[]{:S(2)}, u32[]{:S(2)}) collective-permute-start(bf16[2048,128]{1,0:T(8,128)(2,1)S(1)} %join.1.refs_1_), channel_id=1, source_target_pairs={{0,1},{1,0},{2,3},{3,2},{4,5},{5,4},{6,7},{7,6},{8,9},{9,8},{10,11... | collective-permute-start | bytes 1572872 | tf_op jit(solution)/shard_map/grad_y_core/ppermute | solution.py:550
  41.6 7.3 %collective-permute-start.4 = (bf16[256,128]{1,0:T(8,128)(2,1)S(1)}, bf16[256,128]{1,0:T(8,128)(2,1)S(1)}, u32[]{:S(2)}, u32[]{:S(2)}) collective-permute-start(bf16[256,128]{1,0:T(8,128)(2,1)S(1)} %get-tuple-element.51.refs_4_), channel_id=1, source_target_pairs={{0,48},{8,56},{16,32},{24,40},{32,16},{40,24},{48,0},{56,8},{64,11... | collective-permute-start | bytes 196616 | tf_op jit(solution)/shard_map/scan_half/ppermute | solution.py:550
  49.6 8.1 %collective-permute-start.14 = (bf16[256,128]{1,0:T(8,128)(2,1)S(1)}, bf16[256,128]{1,0:T(8,128)(2,1)S(1)}, u32[]{:S(2)}, u32[]{:S(2)}) collective-permute-start(bf16[256,128]{1,0:T(8,128)(2,1)S(1)} %get-tuple-element.54.refs_6_), channel_id=1, source_target_pairs={{0,192},{8,200},{16,208},{24,216},{32,224},{40,232},{48,240},{56,2... | collective-permute-start | bytes 196616 | tf_op jit(solution)/shard_map/scan_y/ppermute | solution.py:550
  52.7 14.5 %collective-permute-start.19 = (bf16[512,128]{1,0:T(8,128)(2,1)S(1)}, bf16[512,128]{1,0:T(8,128)(2,1)S(1)}, u32[]{:S(2)}, u32[]{:S(2)}) collective-permute-start(bf16[512,128]{1,0:T(8,128)(2,1)S(1)} %get-tuple-element.60), channel_id=1, source_target_pairs={{0,16},{8,24},{16,0},{24,8},{32,48},{40,56},{48,32},{56,40},{64,80... | collective-permute-start | bytes 393224 | tf_op jit(solution)/shard_map/grad_attn/ppermute | solution.py:550
  52.7 15.7 %collective-permute-start.20 = (bf16[512,128]{1,0:T(8,128)(2,1)S(1)}, bf16[512,128]{1,0:T(8,128)(2,1)S(1)}, u32[]{:S(2)}, u32[]{:S(2)}) collective-permute-start(bf16[512,128]{1,0:T(8,128)(2,1)S(1)} %get-tuple-element.61), channel_id=1, source_target_pairs={{0,24},{8,16},{16,8},{24,0},{32,56},{40,48},{48,40},{56,32},{64,88... | collective-permute-start | bytes 393224 | tf_op jit(solution)/shard_map/grad_attn/ppermute | solution.py:550
  53.7 14.6 %collective-permute-start.18 = (bf16[512,128]{1,0:T(8,128)(2,1)S(1)}, bf16[512,128]{1,0:T(8,128)(2,1)S(1)}, u32[]{:S(2)}, u32[]{:S(2)}) collective-permute-start(bf16[512,128]{1,0:T(8,128)(2,1)S(1)} %get-tuple-element.52.refs_3_), channel_id=1, source_target_pairs={{0,8},{8,0},{16,24},{24,16},{32,40},{40,32},{48,56},{56,48},{64,72... | collective-permute-start | bytes 393224 | tf_op jit(solution)/shard_map/grad_attn/ppermute | solution.py:550
  57.0 5.8 %collective-permute-start.13 = (bf16[256,128]{1,0:T(8,128)(2,1)S(1)}, bf16[256,128]{1,0:T(8,128)(2,1)S(1)}, u32[]{:S(2)}, u32[]{:S(2)}) collective-permute-start(bf16[256,128]{1,0:T(8,128)(2,1)S(1)} %get-tuple-element.54.refs_6_), channel_id=1, source_target_pairs={{0,128},{8,136},{16,144},{24,152},{32,160},{40,168},{48,176},{56,1... | collective-permute-start | bytes 196616 | tf_op jit(solution)/shard_map/scan_y/ppermute | solution.py:550
  57.7 5.1 %collective-permute-start.12 = (bf16[256,128]{1,0:T(8,128)(2,1)S(1)}, bf16[256,128]{1,0:T(8,128)(2,1)S(1)}, u32[]{:S(2)}, u32[]{:S(2)}) collective-permute-start(bf16[256,128]{1,0:T(8,128)(2,1)S(1)} %get-tuple-element.54.refs_6_), channel_id=1, source_target_pairs={{0,64},{8,72},{16,80},{24,88},{32,96},{40,104},{48,112},{56,120},{... | collective-permute-start | bytes 196616 | tf_op jit(solution)/shard_map/scan_y/ppermute | solution.py:550
  64.7 15.5 %collective-permute-start.17 = (bf16[512,128]{1,0:T(8,128)(2,1)S(1)}, bf16[512,128]{1,0:T(8,128)(2,1)S(1)}, u32[]{:S(2)}, u32[]{:S(2)}) collective-permute-start(bf16[512,128]{1,0:T(8,128)(2,1)S(1)} %get-tuple-element.58.refs_7_.refs_1_), channel_id=1, source_target_pairs={{0,24},{8,16},{16,8},{24,0},{32,56},{40,48},{48,40},{56,32},{64,88... | collective-permute-start | bytes 393224 | tf_op jit(solution)/shard_map/attn/ppermute | solution.py:550
  65.8 14.4 %collective-permute-start.16 = (bf16[512,128]{1,0:T(8,128)(2,1)S(1)}, bf16[512,128]{1,0:T(8,128)(2,1)S(1)}, u32[]{:S(2)}, u32[]{:S(2)}) collective-permute-start(bf16[512,128]{1,0:T(8,128)(2,1)S(1)} %get-tuple-element.58.refs_7_.refs_1_), channel_id=1, source_target_pairs={{0,16},{8,24},{16,0},{24,8},{32,48},{40,56},{48,32},{56,40},{64,80... | collective-permute-start | bytes 393224 | tf_op jit(solution)/shard_map/attn/ppermute | solution.py:550
  67.2 13.1 %collective-permute-start.15 = (bf16[512,128]{1,0:T(8,128)(2,1)S(1)}, bf16[512,128]{1,0:T(8,128)(2,1)S(1)}, u32[]{:S(2)}, u32[]{:S(2)}) collective-permute-start(bf16[512,128]{1,0:T(8,128)(2,1)S(1)} %get-tuple-element.58.refs_7_.refs_1_), channel_id=1, source_target_pairs={{0,8},{8,0},{16,24},{24,16},{32,40},{40,32},{48,56},{56,48},{64,72... | collective-permute-start | bytes 393224 | tf_op jit(solution)/shard_map/attn/ppermute | solution.py:550
  69.7 4.0 %collective-permute-start.21 = (bf16[128,128]{1,0:T(8,128)(2,1)S(1)}, bf16[128,128]{1,0:T(8,128)(2,1)S(1)}, u32[]{:S(2)}, u32[]{:S(2)}) collective-permute-start(bf16[128,128]{1,0:T(8,128)(2,1)S(1)} %get-tuple-element.62), channel_id=1, source_target_pairs={{0,64},{8,72},{16,80},{24,88},{32,96},{40,104},{48,112},{56,120},{... | collective-permute-start | bytes 98312 | tf_op jit(solution)/shard_map/back_y/ppermute | solution.py:550
  69.9 5.8 %collective-permute-start.23 = (bf16[128,128]{1,0:T(8,128)(2,1)S(1)}, bf16[128,128]{1,0:T(8,128)(2,1)S(1)}, u32[]{:S(2)}, u32[]{:S(2)}) collective-permute-start(bf16[128,128]{1,0:T(8,128)(2,1)S(1)} %get-tuple-element.63), channel_id=1, source_target_pairs={{0,192},{8,200},{16,208},{24,216},{32,224},{40,232},{48,240},{56,2... | collective-permute-start | bytes 98312 | tf_op jit(solution)/shard_map/back_y/ppermute | solution.py:550
  73.7 5.4 %collective-permute-start.22 = (bf16[128,128]{1,0:T(8,128)(2,1)S(1)}, bf16[128,128]{1,0:T(8,128)(2,1)S(1)}, u32[]{:S(2)}, u32[]{:S(2)}) collective-permute-start(bf16[128,128]{1,0:T(8,128)(2,1)S(1)} %get-tuple-element.63), channel_id=1, source_target_pairs={{0,128},{8,136},{16,144},{24,152},{32,160},{40,168},{48,176},{56,1... | collective-permute-start | bytes 98312 | tf_op jit(solution)/shard_map/back_y/ppermute | solution.py:550
  82.1 2.0 %collective-permute-start.24 = (bf16[2048,128]{1,0:T(8,128)(2,1)S(1)}, bf16[2048,128]{1,0:T(8,128)(2,1)S(1)}, u32[]{:S(2)}, u32[]{:S(2)}) collective-permute-start(bf16[2048,128]{1,0:T(8,128)(2,1)S(1)} %get-tuple-element.69), channel_id=1, source_target_pairs={{0,1},{1,0},{2,3},{3,2},{4,5},{5,4},{6,7},{7,6},{8,9},{9,8},{10,11... | collective-permute-start | bytes 1572872 | tf_op jit(solution)/shard_map/out_core/ppermute | solution.py:550
  82.2 6.8 %collective-permute-start.28 = (bf16[128,128]{1,0:T(8,128)(2,1)S(1)}, bf16[128,128]{1,0:T(8,128)(2,1)S(1)}, u32[]{:S(2)}, u32[]{:S(2)}) collective-permute-start(bf16[128,128]{1,0:T(8,128)(2,1)S(1)} %get-tuple-element.67.refs_9_), channel_id=1, source_target_pairs={{0,48},{8,56},{16,32},{24,40},{32,16},{40,24},{48,0},{56,8},{64,11... | collective-permute-start | bytes 98312 | tf_op jit(solution)/shard_map/back_half/ppermute | solution.py:550
  84.2 9.5 %collective-permute-start.25 = (bf16[512,128]{1,0:T(8,128)(2,1)S(1)}, bf16[512,128]{1,0:T(8,128)(2,1)S(1)}, u32[]{:S(2)}, u32[]{:S(2)}) collective-permute-start(bf16[512,128]{1,0:T(8,128)(2,1)S(1)} %get-tuple-element.71), channel_id=1, source_target_pairs={{0,2},{1,3},{2,0},{3,1},{4,6},{5,7},{6,4},{7,5},{8,10},{9,11},{10,... | collective-permute-start | bytes 393224 | tf_op jit(solution)/shard_map/out_x/ppermute | solution.py:550
  84.5 9.2 %collective-permute-start.26 = (bf16[512,128]{1,0:T(8,128)(2,1)S(1)}, bf16[512,128]{1,0:T(8,128)(2,1)S(1)}, u32[]{:S(2)}, u32[]{:S(2)}) collective-permute-start(bf16[512,128]{1,0:T(8,128)(2,1)S(1)} %get-tuple-element.72), channel_id=1, source_target_pairs={{0,4},{1,5},{2,6},{3,7},{4,0},{5,1},{6,2},{7,3},{8,12},{9,13},{10,... | collective-permute-start | bytes 393224 | tf_op jit(solution)/shard_map/out_x/ppermute | solution.py:550
  86.3 8.7 %collective-permute-start.27 = (bf16[512,128]{1,0:T(8,128)(2,1)S(1)}, bf16[512,128]{1,0:T(8,128)(2,1)S(1)}, u32[]{:S(2)}, u32[]{:S(2)}) collective-permute-start(bf16[512,128]{1,0:T(8,128)(2,1)S(1)} %get-tuple-element.73), channel_id=1, source_target_pairs={{0,6},{1,7},{2,4},{3,5},{4,2},{5,3},{6,0},{7,1},{8,14},{9,15},{10,... | collective-permute-start | bytes 393224 | tf_op jit(solution)/shard_map/out_x/ppermute | solution.py:550
  95.6 5.8 %collective-permute-start.29 = (bf16[384,128]{1,0:T(8,128)(2,1)S(1)}, bf16[384,128]{1,0:T(8,128)(2,1)S(1)}, u32[]{:S(2)}, u32[]{:S(2)}) collective-permute-start(bf16[384,128]{1,0:T(8,128)(2,1)S(1)} %get-tuple-element.82), channel_id=1, source_target_pairs={{0,8},{8,0},{16,24},{24,16},{32,40},{40,32},{48,56},{56,48},{64,72... | collective-permute-start | bytes 294920 | tf_op jit(solution)/shard_map/home/ppermute | solution.py:550
  96.6 8.2 %collective-permute-start.30 = (bf16[384,128]{1,0:T(8,128)(2,1)S(1)}, bf16[384,128]{1,0:T(8,128)(2,1)S(1)}, u32[]{:S(2)}, u32[]{:S(2)}) collective-permute-start(bf16[384,128]{1,0:T(8,128)(2,1)S(1)} %get-tuple-element.83), channel_id=1, source_target_pairs={{0,16},{8,24},{16,0},{24,8},{32,48},{40,56},{48,32},{56,40},{64,80... | collective-permute-start | bytes 294920 | tf_op jit(solution)/shard_map/home/ppermute | solution.py:550
  98.2 9.2 %collective-permute-start.31 = (bf16[384,128]{1,0:T(8,128)(2,1)S(1)}, bf16[384,128]{1,0:T(8,128)(2,1)S(1)}, u32[]{:S(2)}, u32[]{:S(2)}) collective-permute-start(bf16[384,128]{1,0:T(8,128)(2,1)S(1)} %get-tuple-element.84), channel_id=1, source_target_pairs={{0,24},{8,16},{16,8},{24,0},{32,56},{40,48},{48,40},{56,32},{64,88... | collective-permute-start | bytes 294920 | tf_op jit(solution)/shard_map/home/ppermute | solution.py:550

commit v3 on v2

--- a/solution.py
+++ b/solution.py
@@ -571,7 +571,7 @@
     w0, own = call(1, join_weight_body, [((1024, 128), BF), ((544, 128), BF)], [out_weight, half, packs[0]])
     weight = [w0] + [xor(w0, "seq", 8 * n, "weight_y") for n in (1, 2, 3)]
     mine = [own] + mine
-    gm = call(1, collect_body, [((512, 128), BF)], mine, after=[w0])[0]
+    gm = call(200, collect_body, [((512, 128), BF)], mine, after=[w0])[0]
     T = (512, 128)
     S = (128, 128)
     ab, abf, kept = call(
@@ -579,7 +579,7 @@
         [((256, 128), BF), ((256, 128), F32), ((KEPT, 128), F32)],
         [where] + mine,
         [pltpu.VMEM((4, 288, 128), BF)],
-        after=[gm],
+        after=[gm, weight[1]],
     )
     other = xor(ab, "seq", 6, "scan_half")
     ga = [gm] + [xor(gm, "head", 2 * n, "grad_y_x") for n in (1, 2, 3)]

time: 109 us -> 106 us (0.972)
  waiting for transfers between devices: 36.7 us -> 30.4 us
  starting transfers between devices: 43 us -> 47 us
    ppermute x32, waiting for transfers between devices: 36.7 us -> 30.4 us  [xor(): lax.ppermute(value, axis, [(s, s ^ mask) for s in range(lax.axis_size(axi...]
    ppermute x32, starting transfers between devices: 43 us -> 47 us  [xor(): lax.ppermute(value, axis, [(s, s ^ mask) for s in range(lax.axis_size(axi...]
    unnamed x10 -> x8, local copies, waits for them, and re-layouts: 2.39 us -> 1.82 us
  transfers between devices with their start and end apart: 32 -> 32, of which waited for: 17 -> 13; matrix products, arithmetic and copies ran while one was open for 1% -> 1% of each run, Pallas kernels for 19% -> 19%
where the time goes in v3:
time: 106 us
  starting transfers between devices  47 us (44%)
  waiting for transfers between devices  30.4 us (29%)
  Pallas kernels  25.2 us (24%)
  local copies, waits for them, and re-layouts  2.49 us (2%)
    ppermute x32, starting transfers between devices, xor(): lax.ppermute(value, axis, [(s, s ^ mask) for s in range(lax.axis_size(axi...  47 us
    ppermute x32, waiting for transfers between devices, xor(): lax.ppermute(value, axis, [(s, s ^ mask) for s in range(lax.axis_size(axi...  30.4 us
    pallas_call x17, Pallas kernels, call(): pl.pallas_call(waiting, out_shape=[jax.ShapeDtypeStruct(s, d) for s, d in...  25.2 us
  transfers between devices with their start and end apart: 32, of which 13 were waited for; matrix products, arithmetic and copies ran while one was open for 1% of the time, Pallas kernels for 19%

profile of v3, /device:TPU:32, one launch (start us, length us, event | category | flops | bytes accessed | tf_op | source)
XLA Modules:
  0.0 106.0 jit_solution(8745190306976863622)
XLA Ops:
  0.6 5.5 %collective-permute-start = (bf16[512,128]{1,0:T(8,128)(2,1)}, bf16[512,128]{1,0:T(8,128)(2,1)S(1)}, u32[]{:S(2)}, u32[]{:S(2)}) collective-permute-start(bf16[512,128]{1,0:T(8,128)(2,1)} %refs_0_.1), channel_id=1, source_target_pairs={{0,48},{8,56},{16,32},{24,40},{32,16},{40,24},{48,0},{56,8},{64,11... | collective-permute-start | bytes 393224 | tf_op jit(solution)/shard_map/weight_half/ppermute | solution.py:550
  6.8 2.7 %pack.1 = (bf16[544,128]{1,0:T(8,128)(2,1)}, bf16[544,128]{1,0:T(8,128)(2,1)}, bf16[544,128]{1,0:T(8,128)(2,1)}, bf16[544,128]{1,0:T(8,128)(2,1)}) custom-call(s32[8]{0:T(128)} %stack.27.refs_0_, s32[2]{0:T(128)} %refs_1_.1, bf16[128,512]{1,0:T(8,128)(2,1)} %refs_2_.1, bf16[128,512]{1,0:T(8,128)(2,1)} %refs_3_.1, bf16[128,512]{1,0:T(8,128)(2,1)} %refs_4_.1, ...), custom_call_target="tpu_custom_call" | custom-call | flops 300000000 | tf_op jit(solution)/shard_map/pack/pallas_call | solution.py:105
  9.5 1.1 %collective-permute-start.1 = (bf16[544,128]{1,0:T(8,128)(2,1)}, bf16[544,128]{1,0:T(8,128)(2,1)S(1)}, u32[]{:S(2)}, u32[]{:S(2)}) collective-permute-start(bf16[544,128]{1,0:T(8,128)(2,1)} %get-tuple-element.46), channel_id=1, source_target_pairs={{0,8},{8,0},{16,24},{24,16},{32,40},{40,32},{48,56},{56,48},{64,72... | collective-permute-start | bytes 417800 | tf_op jit(solution)/shard_map/reshard/ppermute | solution.py:550
  10.6 1.5 %collective-permute-start.2 = (bf16[544,128]{1,0:T(8,128)(2,1)}, bf16[544,128]{1,0:T(8,128)(2,1)S(1)}, u32[]{:S(2)}, u32[]{:S(2)}) collective-permute-start(bf16[544,128]{1,0:T(8,128)(2,1)} %get-tuple-element.47), channel_id=1, source_target_pairs={{0,16},{8,24},{16,0},{24,8},{32,48},{40,56},{48,32},{56,40},{64,80... | collective-permute-start | bytes 417800 | tf_op jit(solution)/shard_map/reshard/ppermute | solution.py:550
  12.1 1.0 collective-permute-start.3
  13.1 0.9 copy-done.1
  14.0 0.9 copy-done.2
  14.9 3.1 %collective-permute-start.10 = (bf16[1024,128]{1,0:T(8,128)(2,1)S(1)}, bf16[1024,128]{1,0:T(8,128)(2,1)S(1)}, u32[]{:S(2)}, u32[]{:S(2)}) collective-permute-start(bf16[1024,128]{1,0:T(8,128)(2,1)S(1)} %get-tuple-element.49.refs_4_.refs_3_.refs_5_), channel_id=1, source_target_pairs={{0,192},{8,200},{16,208},{24,216},{32,224},{40,232},{48,240},{56,2... | collective-permute-start | bytes 786440 | tf_op jit(solution)/shard_map/weight_y/ppermute | solution.py:550
  19.1 3.1 %collective-permute-done.2.refs_2_.refs_3_ = bf16[544,128]{1,0:T(8,128)(2,1)S(1)} collective-permute-done((bf16[544,128]{1,0:T(8,128)(2,1)}, bf16[544,128]{1,0:T(8,128)(2,1)S(1)}, u32[]{:S(2)}, u32[]{:S(2)}) %collective-permute-start.2) | collective-permute-done | bytes 139296 | tf_op jit(solution)/shard_map/reshard/ppermute | solution.py:550
  22.3 2.9 %collective-permute-done.3.refs_3_.refs_4_ = bf16[544,128]{1,0:T(8,128)(2,1)S(1)} collective-permute-done((bf16[544,128]{1,0:T(8,128)(2,1)}, bf16[544,128]{1,0:T(8,128)(2,1)S(1)}, u32[]{:S(2)}, u32[]{:S(2)}) %collective-permute-start.3) | collective-permute-done | bytes 139296 | tf_op jit(solution)/shard_map/reshard/ppermute | solution.py:550
  25.2 2.8 %collective-permute-start.8 = (bf16[512,128]{1,0:T(8,128)(2,1)S(1)}, bf16[512,128]{1,0:T(8,128)(2,1)S(1)}, u32[]{:S(2)}, u32[]{:S(2)}) collective-permute-start(bf16[512,128]{1,0:T(8,128)(2,1)S(1)} %collect.1.refs_5_.refs_0_), channel_id=1, source_target_pairs={{0,6},{1,7},{2,4},{3,5},{4,2},{5,3},{6,0},{7,1},{8,14},{9,15},{10,... | collective-permute-start | bytes 393224 | tf_op jit(solution)/shard_map/grad_y_x/ppermute | solution.py:550
  28.0 0.8 collective-permute-start.7
  28.8 1.2 %collective-permute-done.4.refs_6_.refs_5_.refs_4_ = bf16[1024,128]{1,0:T(8,128)(2,1)S(1)} collective-permute-done((bf16[1024,128]{1,0:T(8,128)(2,1)S(1)}, bf16[1024,128]{1,0:T(8,128)(2,1)S(1)}, u32[]{:S(2)}, u32[]{:S(2)}) %collective-permute-start.4) | collective-permute-done | bytes 262176 | tf_op jit(solution)/shard_map/weight_y/ppermute | solution.py:550
  30.0 1.5 %collective-permute-start.6 = (bf16[512,128]{1,0:T(8,128)(2,1)S(1)}, bf16[512,128]{1,0:T(8,128)(2,1)S(1)}, u32[]{:S(2)}, u32[]{:S(2)}) collective-permute-start(bf16[512,128]{1,0:T(8,128)(2,1)S(1)} %collect.1.refs_5_.refs_0_), channel_id=1, source_target_pairs={{0,2},{1,3},{2,0},{3,1},{4,6},{5,7},{6,4},{7,5},{8,10},{9,11},{10,... | collective-permute-start | bytes 393224 | tf_op jit(solution)/shard_map/grad_y_x/ppermute | solution.py:550
  31.5 4.4 %block.1 = (bf16[256,128]{1,0:T(8,128)(2,1)S(1)}, f32[256,128]{1,0:T(8,128)S(1)}, f32[7424,128]{1,0:T(8,128)S(1)}) custom-call(s32[8]{0:T(128)S(1)} %copy-done.3, bf16[544,128]{1,0:T(8,128)(2,1)S(1)} %get-tuple-element.45.refs_0_.refs_1_, bf16[544,128]{1,0:T(8,128)(2,1)S(1)} %collective-permute-done.1.refs_1_.refs_2_, ...), custom_call_target="tpu_custom_call" | custom-call | flops 6000000000 | tf_op jit(solution)/shard_map/block/pallas_call | solution.py:105
  36.1 0.9 collective-permute-start.5
  37.0 1.0 collective-permute-done.11.refs_2_
  38.0 2.0 %back_product.1 = (f32[512,128]{1,0:T(8,128)S(1)}, bf16[512,128]{1,0:T(8,128)(2,1)S(1)}, bf16[512,128]{1,0:T(8,128)(2,1)S(1)}, bf16[512,128]{1,0:T(8,128)(2,1)S(1)}) custom-call(s32[8]{0:T(128)S(1)} %copy-done.3, bf16[2048,128]{1,0:T(8,128)(2,1)S(1)} %join.1.refs_1_, bf16[2048,128]{1,0:T(8,128)(2,1)S(1)} %collective-permute-done.11.refs_2_, ...), custom_call_target="tpu_custom_call" | custom-call | flops 300000000 | tf_op jit(solution)/shard_map/back_product/pallas_call | solution.py:105
  40.0 4.1 %collective-permute-done.5.refs_2_.refs_3_ = bf16[256,128]{1,0:T(8,128)(2,1)S(1)} collective-permute-done((bf16[256,128]{1,0:T(8,128)(2,1)S(1)}, bf16[256,128]{1,0:T(8,128)(2,1)S(1)}, u32[]{:S(2)}, u32[]{:S(2)}) %collective-permute-start.5) | collective-permute-done | bytes 65568 | tf_op jit(solution)/shard_map/scan_half/ppermute | solution.py:550
  44.9 2.9 %collective-permute-start.14 = (bf16[256,128]{1,0:T(8,128)(2,1)S(1)}, bf16[256,128]{1,0:T(8,128)(2,1)S(1)}, u32[]{:S(2)}, u32[]{:S(2)}) collective-permute-start(bf16[256,128]{1,0:T(8,128)(2,1)S(1)} %get-tuple-element.54.refs_6_), channel_id=1, source_target_pairs={{0,192},{8,200},{16,208},{24,216},{32,224},{40,232},{48,240},{56,2... | collective-permute-start | bytes 196616 | tf_op jit(solution)/shard_map/scan_y/ppermute | solution.py:550
  48.4 1.0 collective-permute-start.20
  49.4 2.7 %collective-permute-start.18 = (bf16[512,128]{1,0:T(8,128)(2,1)S(1)}, bf16[512,128]{1,0:T(8,128)(2,1)S(1)}, u32[]{:S(2)}, u32[]{:S(2)}) collective-permute-start(bf16[512,128]{1,0:T(8,128)(2,1)S(1)} %get-tuple-element.52.refs_3_), channel_id=1, source_target_pairs={{0,8},{8,0},{16,24},{24,16},{32,40},{40,32},{48,56},{56,48},{64,72... | collective-permute-start | bytes 393224 | tf_op jit(solution)/shard_map/grad_attn/ppermute | solution.py:550
  53.4 2.3 %query.1 = (f32[1536,128]{1,0:T(8,128)S(1)}, f32[1536,128]{1,0:T(8,128)S(1)}) custom-call(s32[8]{0:T(128)S(1)} %copy-done.3, bf16[544,128]{1,0:T(8,128)(2,1)S(1)} %get-tuple-element.45.refs_0_.refs_1_, bf16[544,128]{1,0:T(8,128)(2,1)S(1)} %collective-permute-done.1.refs_1_.refs_2_, bf16[544,128]{1,0:T(8,128)(2,1)S(1)} %collective-permute-done.2.refs_2_.refs_3_, ...), custom_call_target="tpu_custom_call" | custom-call | flops 400000000 | tf_op jit(solution)/shard_map/query/pallas_call | solution.py:105
  55.7 2.3 %collective-permute-done.13.refs_3_ = bf16[256,128]{1,0:T(8,128)(2,1)S(1)} collective-permute-done((bf16[256,128]{1,0:T(8,128)(2,1)S(1)}, bf16[256,128]{1,0:T(8,128)(2,1)S(1)}, u32[]{:S(2)}, u32[]{:S(2)}) %collective-permute-start.13) | collective-permute-done | bytes 65568 | tf_op jit(solution)/shard_map/scan_y/ppermute | solution.py:550
  58.0 1.9 %far.1 = (bf16[512,128]{1,0:T(8,128)(2,1)S(1)}, f32[128,384]{1,0:T(8,128)S(1)}, f32[4,128,128]{2,1,0:T(8,128)S(1)}, f32[128,128]{1,0:T(8,128)S(1)}) custom-call(s32[8]{0:T(128)S(1)} %copy-done.3, f32[256,128]{1,0:T(8,128)S(1)} %get-tuple-element.53.refs_1_, bf16[256,128]{1,0:T(8,128)(2,1)S(1)} %collective-permute-done.12.refs_2_, ...), custom_call_target="tpu_custom_call" | custom-call | flops 200000000 | tf_op jit(solution)/shard_map/far/pallas_call | solution.py:105
  59.9 0.8 collective-permute-start.17
  60.7 1.6 %collective-permute-start.16 = (bf16[512,128]{1,0:T(8,128)(2,1)S(1)}, bf16[512,128]{1,0:T(8,128)(2,1)S(1)}, u32[]{:S(2)}, u32[]{:S(2)}) collective-permute-start(bf16[512,128]{1,0:T(8,128)(2,1)S(1)} %get-tuple-element.58.refs_7_.refs_1_), channel_id=1, source_target_pairs={{0,16},{8,24},{16,0},{24,8},{32,48},{40,56},{48,32},{56,40},{64,80... | collective-permute-start | bytes 393224 | tf_op jit(solution)/shard_map/attn/ppermute | solution.py:550
  62.3 1.1 %collective-permute-start.15 = (bf16[512,128]{1,0:T(8,128)(2,1)S(1)}, bf16[512,128]{1,0:T(8,128)(2,1)S(1)}, u32[]{:S(2)}, u32[]{:S(2)}) collective-permute-start(bf16[512,128]{1,0:T(8,128)(2,1)S(1)} %get-tuple-element.58.refs_7_.refs_1_), channel_id=1, source_target_pairs={{0,8},{8,0},{16,24},{24,16},{32,40},{40,32},{48,56},{56,48},{64,72... | collective-permute-start | bytes 393224 | tf_op jit(solution)/shard_map/attn/ppermute | solution.py:550
  63.5 1.4 %reach.1 = (bf16[4,128,128]{2,1,0:T(8,128)(2,1)S(1)}, bf16[128,128]{1,0:T(8,128)(2,1)S(1)}, bf16[128,128]{1,0:T(8,128)(2,1)S(1)}, f32[128,128]{1,0:T(8,128)S(1)}) custom-call(s32[8]{0:T(128)S(1)} %copy-done.3, f32[512,128]{1,0:T(8,128)S(1)} %get-tuple-element.59.refs_1_, bf16[512,128]{1,0:T(8,128)(2,1)S(1)} %collective-permute-done.18.refs_2_, ...), custom_call_target="tpu_custom_call" | custom-call | flops 200000000 | tf_op jit(solution)/shard_map/reach/pallas_call | solution.py:105
  65.1 2.5 %collective-permute-start.23 = (bf16[128,128]{1,0:T(8,128)(2,1)S(1)}, bf16[128,128]{1,0:T(8,128)(2,1)S(1)}, u32[]{:S(2)}, u32[]{:S(2)}) collective-permute-start(bf16[128,128]{1,0:T(8,128)(2,1)S(1)} %get-tuple-element.63), channel_id=1, source_target_pairs={{0,192},{8,200},{16,208},{24,216},{32,224},{40,232},{48,240},{56,2... | collective-permute-start | bytes 98312 | tf_op jit(solution)/shard_map/back_y/ppermute | solution.py:550
  67.5 1.3 %collective-permute-done.21.refs_1_ = bf16[128,128]{1,0:T(8,128)(2,1)S(1)} collective-permute-done((bf16[128,128]{1,0:T(8,128)(2,1)S(1)}, bf16[128,128]{1,0:T(8,128)(2,1)S(1)}, u32[]{:S(2)}, u32[]{:S(2)}) %collective-permute-start.21) | collective-permute-done | bytes 32800 | tf_op jit(solution)/shard_map/back_y/ppermute | solution.py:550
  68.8 2.0 %collective-permute-start.22 = (bf16[128,128]{1,0:T(8,128)(2,1)S(1)}, bf16[128,128]{1,0:T(8,128)(2,1)S(1)}, u32[]{:S(2)}, u32[]{:S(2)}) collective-permute-start(bf16[128,128]{1,0:T(8,128)(2,1)S(1)} %get-tuple-element.63), channel_id=1, source_target_pairs={{0,128},{8,136},{16,144},{24,152},{32,160},{40,168},{48,176},{56,1... | collective-permute-start | bytes 98312 | tf_op jit(solution)/shard_map/back_y/ppermute | solution.py:550
  70.9 3.4 %collective-permute-done.22.refs_2_ = bf16[128,128]{1,0:T(8,128)(2,1)S(1)} collective-permute-done((bf16[128,128]{1,0:T(8,128)(2,1)S(1)}, bf16[128,128]{1,0:T(8,128)(2,1)S(1)}, u32[]{:S(2)}, u32[]{:S(2)}) %collective-permute-start.22) | collective-permute-done | bytes 32800 | tf_op jit(solution)/shard_map/back_y/ppermute | solution.py:550
  74.3 1.1 %near.1 = (bf16[128,128]{1,0:T(8,128)(2,1)S(1)}, f32[128,128]{1,0:T(8,128)S(1)}) custom-call(s32[8]{0:T(128)S(1)} %copy-done.3, bf16[128,128]{1,0:T(8,128)(2,1)S(1)} %collective-permute-done.21.refs_1_, bf16[128,128]{1,0:T(8,128)(2,1)S(1)} %collective-permute-done.22.refs_2_, bf16[128,128]{1,0:T(8,128)(2,1)S(1)} %collective-permute-done.23.refs_3_, ...), custom_call_target="tpu_custom_call" | custom-call | flops 100000000 | tf_op jit(solution)/shard_map/near/pallas_call | solution.py:105
  75.4 1.9 %project.1 = (bf16[2048,128]{1,0:T(8,128)(2,1)S(1)}, bf16[2048,128]{1,0:T(8,128)(2,1)S(1)}) custom-call(s32[8]{0:T(128)S(1)} %copy-done.3, bf16[512,128]{1,0:T(8,128)(2,1)S(1)} %get-tuple-element.58.refs_7_.refs_1_, bf16[512,128]{1,0:T(8,128)(2,1)S(1)} %collective-permute-done.15.refs_2_, bf16[512,128]{1,0:T(8,128)(2,1)S(1)} %collective-permute-done.16.refs_3_, ...), custom_call_target="tpu_custom_call" | custom-call | flops 300000000 | tf_op jit(solution)/shard_map/project/pallas_call | solution.py:105
  77.4 2.4 %collective-permute-start.28 = (bf16[128,128]{1,0:T(8,128)(2,1)S(1)}, bf16[128,128]{1,0:T(8,128)(2,1)S(1)}, u32[]{:S(2)}, u32[]{:S(2)}) collective-permute-start(bf16[128,128]{1,0:T(8,128)(2,1)S(1)} %get-tuple-element.67.refs_9_), channel_id=1, source_target_pairs={{0,48},{8,56},{16,32},{24,40},{32,16},{40,24},{48,0},{56,8},{64,11... | collective-permute-start | bytes 98312 | tf_op jit(solution)/shard_map/back_half/ppermute | solution.py:550
  80.5 3.0 %collective-permute-start.26 = (bf16[512,128]{1,0:T(8,128)(2,1)S(1)}, bf16[512,128]{1,0:T(8,128)(2,1)S(1)}, u32[]{:S(2)}, u32[]{:S(2)}) collective-permute-start(bf16[512,128]{1,0:T(8,128)(2,1)S(1)} %get-tuple-element.72), channel_id=1, source_target_pairs={{0,4},{1,5},{2,6},{3,7},{4,0},{5,1},{6,2},{7,3},{8,12},{9,13},{10,... | collective-permute-start | bytes 393224 | tf_op jit(solution)/shard_map/out_x/ppermute | solution.py:550
  83.5 1.1 %collective-permute-start.27 = (bf16[512,128]{1,0:T(8,128)(2,1)S(1)}, bf16[512,128]{1,0:T(8,128)(2,1)S(1)}, u32[]{:S(2)}, u32[]{:S(2)}) collective-permute-start(bf16[512,128]{1,0:T(8,128)(2,1)S(1)} %get-tuple-element.73), channel_id=1, source_target_pairs={{0,6},{1,7},{2,4},{3,5},{4,2},{5,3},{6,0},{7,1},{8,14},{9,15},{10,... | collective-permute-start | bytes 393224 | tf_op jit(solution)/shard_map/out_x/ppermute | solution.py:550
  84.6 3.7 %grad.1 = (bf16[4,128,128]{2,1,0:T(8,128)(2,1)S(1)}, f32[512,128]{1,0:T(8,128)S(1)}, f32[512,128]{1,0:T(8,128)S(1)}) custom-call(s32[8]{0:T(128)S(1)} %copy-done.3, bf16[4,128,128]{2,1,0:T(8,128)(2,1)S(1)} %get-tuple-element.74.refs_1_, f32[1536,128]{1,0:T(8,128)S(1)} %get-tuple-element.57.refs_6_.refs_5_.refs_2_, f32[128,384]{1,0:T(8,128)S(1)} %get-tuple-element.75.refs_3_, ...), custom_call_target="tpu_custom_call" | custom-call | flops 20000000000 | tf_op jit(solution)/shard_map/grad/pallas_call | solution.py:105
  88.3 1.0 value.1.refs_6_
  89.9 2.2 %collective-permute-done.27.refs_4_ = bf16[512,128]{1,0:T(8,128)(2,1)S(1)} collective-permute-done((bf16[512,128]{1,0:T(8,128)(2,1)S(1)}, bf16[512,128]{1,0:T(8,128)(2,1)S(1)}, u32[]{:S(2)}, u32[]{:S(2)}) %collective-permute-start.27) | collective-permute-done | bytes 131104 | tf_op jit(solution)/shard_map/out_x/ppermute | solution.py:550
  92.8 1.2 %collective-permute-start.29 = (bf16[384,128]{1,0:T(8,128)(2,1)S(1)}, bf16[384,128]{1,0:T(8,128)(2,1)S(1)}, u32[]{:S(2)}, u32[]{:S(2)}) collective-permute-start(bf16[384,128]{1,0:T(8,128)(2,1)S(1)} %get-tuple-element.82), channel_id=1, source_target_pairs={{0,8},{8,0},{16,24},{24,16},{32,40},{40,32},{48,56},{56,48},{64,72... | collective-permute-start | bytes 294920 | tf_op jit(solution)/shard_map/home/ppermute | solution.py:550
  94.0 1.4 %collective-permute-start.30 = (bf16[384,128]{1,0:T(8,128)(2,1)S(1)}, bf16[384,128]{1,0:T(8,128)(2,1)S(1)}, u32[]{:S(2)}, u32[]{:S(2)}) collective-permute-start(bf16[384,128]{1,0:T(8,128)(2,1)S(1)} %get-tuple-element.83), channel_id=1, source_target_pairs={{0,16},{8,24},{16,0},{24,8},{32,48},{40,56},{48,32},{56,40},{64,80... | collective-permute-start | bytes 294920 | tf_op jit(solution)/shard_map/home/ppermute | solution.py:550
  95.4 1.0 collective-permute-start.31
  96.4 2.2 %collective-permute-done.29.refs_2_ = bf16[384,128]{1,0:T(8,128)(2,1)S(1)} collective-permute-done((bf16[384,128]{1,0:T(8,128)(2,1)S(1)}, bf16[384,128]{1,0:T(8,128)(2,1)S(1)}, u32[]{:S(2)}, u32[]{:S(2)}) %collective-permute-start.29) | collective-permute-done | bytes 98336 | tf_op jit(solution)/shard_map/home/ppermute | solution.py:550
  98.6 3.5 %collective-permute-done.30.refs_3_ = bf16[384,128]{1,0:T(8,128)(2,1)S(1)} collective-permute-done((bf16[384,128]{1,0:T(8,128)(2,1)S(1)}, bf16[384,128]{1,0:T(8,128)(2,1)S(1)}, u32[]{:S(2)}, u32[]{:S(2)}) %collective-permute-start.30) | collective-permute-done | bytes 98336 | tf_op jit(solution)/shard_map/home/ppermute | solution.py:550
  102.1 2.5 %collective-permute-done.31.refs_4_ = bf16[384,128]{1,0:T(8,128)(2,1)S(1)} collective-permute-done((bf16[384,128]{1,0:T(8,128)(2,1)S(1)}, bf16[384,128]{1,0:T(8,128)(2,1)S(1)}, u32[]{:S(2)}, u32[]{:S(2)}) %collective-permute-start.31) | collective-permute-done | bytes 98336 | tf_op jit(solution)/shard_map/home/ppermute | solution.py:550
  104.6 1.4 %place.1 = (bf16[128,512]{1,0:T(8,128)(2,1)}, bf16[128,512]{1,0:T(8,128)(2,1)}, bf16[128,512]{1,0:T(8,128)(2,1)}) custom-call(s32[8]{0:T(128)S(1)} %copy-done.3, bf16[384,128]{1,0:T(8,128)(2,1)S(1)} %get-tuple-element.81.refs_1_, bf16[384,128]{1,0:T(8,128)(2,1)S(1)} %collective-permute-done.29.refs_2_, bf16[384,128]{1,0:T(8,128)(2,1)S(1)} %collective-permute-done.30.refs_3_, ...), custom_call_target="tpu_custom_call" | custom-call | flops 100000000 | tf_op jit(solution)/shard_map/place/pallas_call | solution.py:105
  (43 shorter events, 6.9 us)
Async XLA Ops:
  0.6 12.5 %collective-permute-start = (bf16[512,128]{1,0:T(8,128)(2,1)}, bf16[512,128]{1,0:T(8,128)(2,1)S(1)}, u32[]{:S(2)}, u32[]{:S(2)}) collective-permute-start(bf16[512,128]{1,0:T(8,128)(2,1)} %refs_0_.1), channel_id=1, source_target_pairs={{0,48},{8,56},{16,32},{24,40},{32,16},{40,24},{48,0},{56,8},{64,11... | collective-permute-start | bytes 393224 | tf_op jit(solution)/shard_map/weight_half/ppermute | solution.py:550
  9.5 9.2 %collective-permute-start.1 = (bf16[544,128]{1,0:T(8,128)(2,1)}, bf16[544,128]{1,0:T(8,128)(2,1)S(1)}, u32[]{:S(2)}, u32[]{:S(2)}) collective-permute-start(bf16[544,128]{1,0:T(8,128)(2,1)} %get-tuple-element.46), channel_id=1, source_target_pairs={{0,8},{8,0},{16,24},{24,16},{32,40},{40,32},{48,56},{56,48},{64,72... | collective-permute-start | bytes 417800 | tf_op jit(solution)/shard_map/reshard/ppermute | solution.py:550
  10.6 11.6 %collective-permute-start.2 = (bf16[544,128]{1,0:T(8,128)(2,1)}, bf16[544,128]{1,0:T(8,128)(2,1)S(1)}, u32[]{:S(2)}, u32[]{:S(2)}) collective-permute-start(bf16[544,128]{1,0:T(8,128)(2,1)} %get-tuple-element.47), channel_id=1, source_target_pairs={{0,16},{8,24},{16,0},{24,8},{32,48},{40,56},{48,32},{56,40},{64,80... | collective-permute-start | bytes 417800 | tf_op jit(solution)/shard_map/reshard/ppermute | solution.py:550
  12.1 13.1 %collective-permute-start.3 = (bf16[544,128]{1,0:T(8,128)(2,1)}, bf16[544,128]{1,0:T(8,128)(2,1)S(1)}, u32[]{:S(2)}, u32[]{:S(2)}) collective-permute-start(bf16[544,128]{1,0:T(8,128)(2,1)} %get-tuple-element.48), channel_id=1, source_target_pairs={{0,24},{8,16},{16,8},{24,0},{32,56},{40,48},{48,40},{56,32},{64,88... | collective-permute-start | bytes 417800 | tf_op jit(solution)/shard_map/reshard/ppermute | solution.py:550
  13.1 0.9 copy-start.1
  14.0 0.9 copy-start.2
  14.9 21.0 %collective-permute-start.10 = (bf16[1024,128]{1,0:T(8,128)(2,1)S(1)}, bf16[1024,128]{1,0:T(8,128)(2,1)S(1)}, u32[]{:S(2)}, u32[]{:S(2)}) collective-permute-start(bf16[1024,128]{1,0:T(8,128)(2,1)S(1)} %get-tuple-element.49.refs_4_.refs_3_.refs_5_), channel_id=1, source_target_pairs={{0,192},{8,200},{16,208},{24,216},{32,224},{40,232},{48,240},{56,2... | collective-permute-start | bytes 786440 | tf_op jit(solution)/shard_map/weight_y/ppermute | solution.py:550
  18.0 17.9 %collective-permute-start.9 = (bf16[1024,128]{1,0:T(8,128)(2,1)S(1)}, bf16[1024,128]{1,0:T(8,128)(2,1)S(1)}, u32[]{:S(2)}, u32[]{:S(2)}) collective-permute-start(bf16[1024,128]{1,0:T(8,128)(2,1)S(1)} %get-tuple-element.49.refs_4_.refs_3_.refs_5_), channel_id=1, source_target_pairs={{0,128},{8,136},{16,144},{24,152},{32,160},{40,168},{48,176},{56,1... | collective-permute-start | bytes 786440 | tf_op jit(solution)/shard_map/weight_y/ppermute | solution.py:550
  18.7 11.3 %collective-permute-start.4 = (bf16[1024,128]{1,0:T(8,128)(2,1)S(1)}, bf16[1024,128]{1,0:T(8,128)(2,1)S(1)}, u32[]{:S(2)}, u32[]{:S(2)}) collective-permute-start(bf16[1024,128]{1,0:T(8,128)(2,1)S(1)} %get-tuple-element.49.refs_4_.refs_3_.refs_5_), channel_id=1, source_target_pairs={{0,64},{8,72},{16,80},{24,88},{32,96},{40,104},{48,112},{56,120},{... | collective-permute-start | bytes 786440 | tf_op jit(solution)/shard_map/weight_y/ppermute | solution.py:550
  25.1 6.3 %copy-start.3 = (s32[8]{0:T(128)S(1)}, s32[8]{0:T(128)}, u32[]{:S(2)}) copy-start(s32[8]{0:T(128)} %stack.27.refs_0_) | copy-start | bytes 100
  25.2 10.7 %collective-permute-start.8 = (bf16[512,128]{1,0:T(8,128)(2,1)S(1)}, bf16[512,128]{1,0:T(8,128)(2,1)S(1)}, u32[]{:S(2)}, u32[]{:S(2)}) collective-permute-start(bf16[512,128]{1,0:T(8,128)(2,1)S(1)} %collect.1.refs_5_.refs_0_), channel_id=1, source_target_pairs={{0,6},{1,7},{2,4},{3,5},{4,2},{5,3},{6,0},{7,1},{8,14},{9,15},{10,... | collective-permute-start | bytes 393224 | tf_op jit(solution)/shard_map/grad_y_x/ppermute | solution.py:550
  28.0 7.9 %collective-permute-start.7 = (bf16[512,128]{1,0:T(8,128)(2,1)S(1)}, bf16[512,128]{1,0:T(8,128)(2,1)S(1)}, u32[]{:S(2)}, u32[]{:S(2)}) collective-permute-start(bf16[512,128]{1,0:T(8,128)(2,1)S(1)} %collect.1.refs_5_.refs_0_), channel_id=1, source_target_pairs={{0,4},{1,5},{2,6},{3,7},{4,0},{5,1},{6,2},{7,3},{8,12},{9,13},{10,... | collective-permute-start | bytes 393224 | tf_op jit(solution)/shard_map/grad_y_x/ppermute | solution.py:550
  30.0 5.9 %collective-permute-start.6 = (bf16[512,128]{1,0:T(8,128)(2,1)S(1)}, bf16[512,128]{1,0:T(8,128)(2,1)S(1)}, u32[]{:S(2)}, u32[]{:S(2)}) collective-permute-start(bf16[512,128]{1,0:T(8,128)(2,1)S(1)} %collect.1.refs_5_.refs_0_), channel_id=1, source_target_pairs={{0,2},{1,3},{2,0},{3,1},{4,6},{5,7},{6,4},{7,5},{8,10},{9,11},{10,... | collective-permute-start | bytes 393224 | tf_op jit(solution)/shard_map/grad_y_x/ppermute | solution.py:550
  36.0 22.0 %copy-start = (f32[4,128,128]{2,1,0:T(8,128)S(1)}, f32[4,128,128]{2,1,0:T(8,128)}, u32[]{:S(2)}) copy-start(f32[4,128,128]{2,1,0:T(8,128)} %refs_7_.3) | copy-start | bytes 786436
  36.0 2.0 %collective-permute-start.11 = (bf16[2048,128]{1,0:T(8,128)(2,1)S(1)}, bf16[2048,128]{1,0:T(8,128)(2,1)S(1)}, u32[]{:S(2)}, u32[]{:S(2)}) collective-permute-start(bf16[2048,128]{1,0:T(8,128)(2,1)S(1)} %join.1.refs_1_), channel_id=1, source_target_pairs={{0,1},{1,0},{2,3},{3,2},{4,5},{5,4},{6,7},{7,6},{8,9},{9,8},{10,11... | collective-permute-start | bytes 1572872 | tf_op jit(solution)/shard_map/grad_y_core/ppermute | solution.py:550
  36.1 8.0 %collective-permute-start.5 = (bf16[256,128]{1,0:T(8,128)(2,1)S(1)}, bf16[256,128]{1,0:T(8,128)(2,1)S(1)}, u32[]{:S(2)}, u32[]{:S(2)}) collective-permute-start(bf16[256,128]{1,0:T(8,128)(2,1)S(1)} %get-tuple-element.51.refs_4_), channel_id=1, source_target_pairs={{0,48},{8,56},{16,32},{24,40},{32,16},{40,24},{48,0},{56,8},{64,11... | collective-permute-start | bytes 196616 | tf_op jit(solution)/shard_map/scan_half/ppermute | solution.py:550
  44.9 8.0 %collective-permute-start.14 = (bf16[256,128]{1,0:T(8,128)(2,1)S(1)}, bf16[256,128]{1,0:T(8,128)(2,1)S(1)}, u32[]{:S(2)}, u32[]{:S(2)}) collective-permute-start(bf16[256,128]{1,0:T(8,128)(2,1)S(1)} %get-tuple-element.54.refs_6_), channel_id=1, source_target_pairs={{0,192},{8,200},{16,208},{24,216},{32,224},{40,232},{48,240},{56,2... | collective-permute-start | bytes 196616 | tf_op jit(solution)/shard_map/scan_y/ppermute | solution.py:550
  47.8 14.5 %collective-permute-start.19 = (bf16[512,128]{1,0:T(8,128)(2,1)S(1)}, bf16[512,128]{1,0:T(8,128)(2,1)S(1)}, u32[]{:S(2)}, u32[]{:S(2)}) collective-permute-start(bf16[512,128]{1,0:T(8,128)(2,1)S(1)} %get-tuple-element.60), channel_id=1, source_target_pairs={{0,16},{8,24},{16,0},{24,8},{32,48},{40,56},{48,32},{56,40},{64,80... | collective-permute-start | bytes 393224 | tf_op jit(solution)/shard_map/grad_attn/ppermute | solution.py:550
  48.4 15.0 %collective-permute-start.20 = (bf16[512,128]{1,0:T(8,128)(2,1)S(1)}, bf16[512,128]{1,0:T(8,128)(2,1)S(1)}, u32[]{:S(2)}, u32[]{:S(2)}) collective-permute-start(bf16[512,128]{1,0:T(8,128)(2,1)S(1)} %get-tuple-element.61), channel_id=1, source_target_pairs={{0,24},{8,16},{16,8},{24,0},{32,56},{40,48},{48,40},{56,32},{64,88... | collective-permute-start | bytes 393224 | tf_op jit(solution)/shard_map/grad_attn/ppermute | solution.py:550
  49.4 14.0 %collective-permute-start.18 = (bf16[512,128]{1,0:T(8,128)(2,1)S(1)}, bf16[512,128]{1,0:T(8,128)(2,1)S(1)}, u32[]{:S(2)}, u32[]{:S(2)}) collective-permute-start(bf16[512,128]{1,0:T(8,128)(2,1)S(1)} %get-tuple-element.52.refs_3_), channel_id=1, source_target_pairs={{0,8},{8,0},{16,24},{24,16},{32,40},{40,32},{48,56},{56,48},{64,72... | collective-permute-start | bytes 393224 | tf_op jit(solution)/shard_map/grad_attn/ppermute | solution.py:550
  52.2 5.8 %collective-permute-start.13 = (bf16[256,128]{1,0:T(8,128)(2,1)S(1)}, bf16[256,128]{1,0:T(8,128)(2,1)S(1)}, u32[]{:S(2)}, u32[]{:S(2)}) collective-permute-start(bf16[256,128]{1,0:T(8,128)(2,1)S(1)} %get-tuple-element.54.refs_6_), channel_id=1, source_target_pairs={{0,128},{8,136},{16,144},{24,152},{32,160},{40,168},{48,176},{56,1... | collective-permute-start | bytes 196616 | tf_op jit(solution)/shard_map/scan_y/ppermute | solution.py:550
  52.8 5.1 %collective-permute-start.12 = (bf16[256,128]{1,0:T(8,128)(2,1)S(1)}, bf16[256,128]{1,0:T(8,128)(2,1)S(1)}, u32[]{:S(2)}, u32[]{:S(2)}) collective-permute-start(bf16[256,128]{1,0:T(8,128)(2,1)S(1)} %get-tuple-element.54.refs_6_), channel_id=1, source_target_pairs={{0,64},{8,72},{16,80},{24,88},{32,96},{40,104},{48,112},{56,120},{... | collective-permute-start | bytes 196616 | tf_op jit(solution)/shard_map/scan_y/ppermute | solution.py:550
  59.9 15.5 %collective-permute-start.17 = (bf16[512,128]{1,0:T(8,128)(2,1)S(1)}, bf16[512,128]{1,0:T(8,128)(2,1)S(1)}, u32[]{:S(2)}, u32[]{:S(2)}) collective-permute-start(bf16[512,128]{1,0:T(8,128)(2,1)S(1)} %get-tuple-element.58.refs_7_.refs_1_), channel_id=1, source_target_pairs={{0,24},{8,16},{16,8},{24,0},{32,56},{40,48},{48,40},{56,32},{64,88... | collective-permute-start | bytes 393224 | tf_op jit(solution)/shard_map/attn/ppermute | solution.py:550
  60.7 14.7 %collective-permute-start.16 = (bf16[512,128]{1,0:T(8,128)(2,1)S(1)}, bf16[512,128]{1,0:T(8,128)(2,1)S(1)}, u32[]{:S(2)}, u32[]{:S(2)}) collective-permute-start(bf16[512,128]{1,0:T(8,128)(2,1)S(1)} %get-tuple-element.58.refs_7_.refs_1_), channel_id=1, source_target_pairs={{0,16},{8,24},{16,0},{24,8},{32,48},{40,56},{48,32},{56,40},{64,80... | collective-permute-start | bytes 393224 | tf_op jit(solution)/shard_map/attn/ppermute | solution.py:550
  62.3 13.1 %collective-permute-start.15 = (bf16[512,128]{1,0:T(8,128)(2,1)S(1)}, bf16[512,128]{1,0:T(8,128)(2,1)S(1)}, u32[]{:S(2)}, u32[]{:S(2)}) collective-permute-start(bf16[512,128]{1,0:T(8,128)(2,1)S(1)} %get-tuple-element.58.refs_7_.refs_1_), channel_id=1, source_target_pairs={{0,8},{8,0},{16,24},{24,16},{32,40},{40,32},{48,56},{56,48},{64,72... | collective-permute-start | bytes 393224 | tf_op jit(solution)/shard_map/attn/ppermute | solution.py:550
  64.8 4.0 %collective-permute-start.21 = (bf16[128,128]{1,0:T(8,128)(2,1)S(1)}, bf16[128,128]{1,0:T(8,128)(2,1)S(1)}, u32[]{:S(2)}, u32[]{:S(2)}) collective-permute-start(bf16[128,128]{1,0:T(8,128)(2,1)S(1)} %get-tuple-element.62), channel_id=1, source_target_pairs={{0,64},{8,72},{16,80},{24,88},{32,96},{40,104},{48,112},{56,120},{... | collective-permute-start | bytes 98312 | tf_op jit(solution)/shard_map/back_y/ppermute | solution.py:550
  65.1 5.8 %collective-permute-start.23 = (bf16[128,128]{1,0:T(8,128)(2,1)S(1)}, bf16[128,128]{1,0:T(8,128)(2,1)S(1)}, u32[]{:S(2)}, u32[]{:S(2)}) collective-permute-start(bf16[128,128]{1,0:T(8,128)(2,1)S(1)} %get-tuple-element.63), channel_id=1, source_target_pairs={{0,192},{8,200},{16,208},{24,216},{32,224},{40,232},{48,240},{56,2... | collective-permute-start | bytes 98312 | tf_op jit(solution)/shard_map/back_y/ppermute | solution.py:550
  68.8 5.4 %collective-permute-start.22 = (bf16[128,128]{1,0:T(8,128)(2,1)S(1)}, bf16[128,128]{1,0:T(8,128)(2,1)S(1)}, u32[]{:S(2)}, u32[]{:S(2)}) collective-permute-start(bf16[128,128]{1,0:T(8,128)(2,1)S(1)} %get-tuple-element.63), channel_id=1, source_target_pairs={{0,128},{8,136},{16,144},{24,152},{32,160},{40,168},{48,176},{56,1... | collective-permute-start | bytes 98312 | tf_op jit(solution)/shard_map/back_y/ppermute | solution.py:550
  77.3 2.5 %collective-permute-start.24 = (bf16[2048,128]{1,0:T(8,128)(2,1)S(1)}, bf16[2048,128]{1,0:T(8,128)(2,1)S(1)}, u32[]{:S(2)}, u32[]{:S(2)}) collective-permute-start(bf16[2048,128]{1,0:T(8,128)(2,1)S(1)} %get-tuple-element.69), channel_id=1, source_target_pairs={{0,1},{1,0},{2,3},{3,2},{4,5},{5,4},{6,7},{7,6},{8,9},{9,8},{10,11... | collective-permute-start | bytes 1572872 | tf_op jit(solution)/shard_map/out_core/ppermute | solution.py:550
  77.4 7.3 %collective-permute-start.28 = (bf16[128,128]{1,0:T(8,128)(2,1)S(1)}, bf16[128,128]{1,0:T(8,128)(2,1)S(1)}, u32[]{:S(2)}, u32[]{:S(2)}) collective-permute-start(bf16[128,128]{1,0:T(8,128)(2,1)S(1)} %get-tuple-element.67.refs_9_), channel_id=1, source_target_pairs={{0,48},{8,56},{16,32},{24,40},{32,16},{40,24},{48,0},{56,8},{64,11... | collective-permute-start | bytes 98312 | tf_op jit(solution)/shard_map/back_half/ppermute | solution.py:550
  79.8 9.5 %collective-permute-start.25 = (bf16[512,128]{1,0:T(8,128)(2,1)S(1)}, bf16[512,128]{1,0:T(8,128)(2,1)S(1)}, u32[]{:S(2)}, u32[]{:S(2)}) collective-permute-start(bf16[512,128]{1,0:T(8,128)(2,1)S(1)} %get-tuple-element.71), channel_id=1, source_target_pairs={{0,2},{1,3},{2,0},{3,1},{4,6},{5,7},{6,4},{7,5},{8,10},{9,11},{10,... | collective-permute-start | bytes 393224 | tf_op jit(solution)/shard_map/out_x/ppermute | solution.py:550
  80.5 9.5 %collective-permute-start.26 = (bf16[512,128]{1,0:T(8,128)(2,1)S(1)}, bf16[512,128]{1,0:T(8,128)(2,1)S(1)}, u32[]{:S(2)}, u32[]{:S(2)}) collective-permute-start(bf16[512,128]{1,0:T(8,128)(2,1)S(1)} %get-tuple-element.72), channel_id=1, source_target_pairs={{0,4},{1,5},{2,6},{3,7},{4,0},{5,1},{6,2},{7,3},{8,12},{9,13},{10,... | collective-permute-start | bytes 393224 | tf_op jit(solution)/shard_map/out_x/ppermute | solution.py:550
  83.5 8.7 %collective-permute-start.27 = (bf16[512,128]{1,0:T(8,128)(2,1)S(1)}, bf16[512,128]{1,0:T(8,128)(2,1)S(1)}, u32[]{:S(2)}, u32[]{:S(2)}) collective-permute-start(bf16[512,128]{1,0:T(8,128)(2,1)S(1)} %get-tuple-element.73), channel_id=1, source_target_pairs={{0,6},{1,7},{2,4},{3,5},{4,2},{5,3},{6,0},{7,1},{8,14},{9,15},{10,... | collective-permute-start | bytes 393224 | tf_op jit(solution)/shard_map/out_x/ppermute | solution.py:550
  92.8 5.8 %collective-permute-start.29 = (bf16[384,128]{1,0:T(8,128)(2,1)S(1)}, bf16[384,128]{1,0:T(8,128)(2,1)S(1)}, u32[]{:S(2)}, u32[]{:S(2)}) collective-permute-start(bf16[384,128]{1,0:T(8,128)(2,1)S(1)} %get-tuple-element.82), channel_id=1, source_target_pairs={{0,8},{8,0},{16,24},{24,16},{32,40},{40,32},{48,56},{56,48},{64,72... | collective-permute-start | bytes 294920 | tf_op jit(solution)/shard_map/home/ppermute | solution.py:550
  94.0 8.1 %collective-permute-start.30 = (bf16[384,128]{1,0:T(8,128)(2,1)S(1)}, bf16[384,128]{1,0:T(8,128)(2,1)S(1)}, u32[]{:S(2)}, u32[]{:S(2)}) collective-permute-start(bf16[384,128]{1,0:T(8,128)(2,1)S(1)} %get-tuple-element.83), channel_id=1, source_target_pairs={{0,16},{8,24},{16,0},{24,8},{32,48},{40,56},{48,32},{56,40},{64,80... | collective-permute-start | bytes 294920 | tf_op jit(solution)/shard_map/home/ppermute | solution.py:550
  95.4 9.2 %collective-permute-start.31 = (bf16[384,128]{1,0:T(8,128)(2,1)S(1)}, bf16[384,128]{1,0:T(8,128)(2,1)S(1)}, u32[]{:S(2)}, u32[]{:S(2)}) collective-permute-start(bf16[384,128]{1,0:T(8,128)(2,1)S(1)} %get-tuple-element.84), channel_id=1, source_target_pairs={{0,24},{8,16},{16,8},{24,0},{32,56},{40,48},{48,40},{56,32},{64,88... | collective-permute-start | bytes 294920 | tf_op jit(solution)/shard_map/home/ppermute | solution.py:550
